TPU v7x, 32 devices: a whole 2x2x4 slice. The times are simulated.
32 devices in a mesh: dp: 4 (over z), fsdp: 8 (over y, x, core).
Axes of the slice: x: 2, y: 2, z: 4, core: 2. Of those that a mesh axis runs over, the one named last changes fastest.
Arguments:
- tokens: bfloat16 [32768, 512], P(('dp', 'fsdp')), may hold values from -6 to 6
- chain_ids: int32 [32, 1024], P(('dp', 'fsdp')), may hold values from 0 to 127, as said below
- qkv_weight: bfloat16 [512, 1536], P(('dp', 'fsdp')), may hold values from -0.25 to 0.25
- mix_weight: bfloat16 [512, 512], P(('dp', 'fsdp')), may hold values from -0.75 to 0.75
- up_weight: bfloat16 [512, 2048], P(('dp', 'fsdp')), may hold values from -0.25 to 0.25
- down_weight: bfloat16 [2048, 512], P(('dp', 'fsdp')), may hold values from -0.125 to 0.125
- norm_gain: bfloat16 [2, 512], P(None, ('dp', 'fsdp')), may hold values from 0.5 to 1.5
- norm_bias: bfloat16 [2, 512], P(None, ('dp', 'fsdp')), may hold values from -1.796875 to 1.796875
- qv_bias: bfloat16 [2, 512], P(None, ('dp', 'fsdp')), may hold values from -1.796875 to 1.796875
- proj_bias: bfloat16 [2, 512], P(None, ('dp', 'fsdp')), may hold values from -1.796875 to 1.796875
- up_bias: bfloat16 [2048], P(('dp', 'fsdp')), may hold values from -1.796875 to 1.796875
- cotangent: bfloat16 [32768, 512], P(('dp', 'fsdp')), may hold values from -6 to 6
Outputs:
- output: bfloat16 [32768, 512], P(('dp', 'fsdp'))
- input_grad: float32 [32768, 512], P(('dp', 'fsdp'))
- qkv_grad: float32 [512, 1536], P(('dp', 'fsdp'))
- mix_grad: float32 [512, 512], P(('dp', 'fsdp'))
- up_grad: float32 [512, 2048], P(('dp', 'fsdp'))
- down_grad: float32 [2048, 512], P(('dp', 'fsdp'))
- norm_gain_grad: float32 [2, 512], P(None, ('dp', 'fsdp'))
- norm_bias_grad: float32 [2, 512], P(None, ('dp', 'fsdp'))
- qv_bias_grad: float32 [2, 512], P(None, ('dp', 'fsdp'))
- proj_bias_grad: float32 [2, 512], P(None, ('dp', 'fsdp'))
- up_bias_grad: float32 [2048], P(('dp', 'fsdp'))
Inputs may be any that keep to these rules, and one draw needn't show every extreme that they name: `chain_ids`: in each row (the residues of one device) the chain numbers start at 0 and never fall; residues with one number form one chain, and a new chain begins only at a position that is a multiple of 8. In every draw some device holds a single chain of all 1024 residues.
All inputs are finite; a program needn't handle non-finite values.
Results may differ from a plain program's by a relative error of at most 0.0093.
Values may be sent and summed in bfloat16 or wider, within the bound.
No kernel may reach another device: no remote copies, remote signals or barrier semaphores. Data moves between devices by JAX's collectives and lax.ppermute only.
A program may use at most 256 MiB of HBM per device.

v0:
```python
import functools
import math

import jax
import jax.numpy as jnp
from jax import lax
from jax.experimental import pallas as pl
from jax.experimental.pallas import tpu as pltpu
from jax.sharding import PartitionSpec as P

AXES = ("dp", "plane", "core")
HEADS = 8
EPS = 1e-05
SCALE = 0.125
EXP_SCALE = SCALE * math.log2(math.e)
HIDE = -(2.0**60)
MIB = 2**20

BF = jnp.bfloat16
F32 = jnp.float32
NN = (((1,), (0,)), ((), ()))
NT = (((1,), (1,)), ((), ()))
TN = (((0,), (0,)), ((), ()))


def dot(a, b, dims=NN):
    return lax.dot_general(a, b, dims, preferred_element_type=F32)


def vmem():
    return pl.BlockSpec(memory_space=pltpu.VMEM)


def smem():
    return pl.BlockSpec(memory_space=pltpu.SMEM)


def shape(dims, dtype):
    return jax.ShapeDtypeStruct(dims, dtype)


def block_of(index, block):
    return pl.ds(pl.multiple_of(index * block, block), block)


def cost(us):
    return pl.CostEstimate(flops=int(us * 1.1e9), bytes_accessed=0, transcendentals=0)


TALL_ORDER = (0, 2, 1, 3)


def slots():
    return [(c, j, i) for c in range(2) for j in range(4) for i in range(4)]


def block_row(me, c, j, i, rows):
    return pl.multiple_of((me ^ (c | (j << 1) | (i << 3))) * rows, rows)


def row_stats(rows_in):
    mean = jnp.mean(rows_in, axis=-1, keepdims=True)
    centred = rows_in - mean
    spread = jnp.mean(centred * centred, axis=-1, keepdims=True)
    return centred, lax.rsqrt(spread + EPS)


def split_three(row):
    first = row.astype(BF).astype(F32)
    rest = row - first
    second = rest.astype(BF).astype(F32)
    return first, second, rest - second


def pack_kernel(qkv, mix, up, down, gain, shift, qv, proj, up_bias, a0, c0, rows128):
    for pair in range(4):
        for part in range(3):
            base = 384 * pair + 128 * part
            a0[:, base : base + 128] = qkv[:, 512 * part + 128 * pair : 512 * part + 128 * pair + 128]
    rows128[...] = jnp.zeros_like(rows128)
    for index, ref in enumerate((gain, shift, qv, proj)):
        rows128[2 * index : 2 * index + 2, :] = ref[...].astype(F32)
    eye = (
        lax.broadcasted_iota(jnp.int32, (16, 16), 0) == lax.broadcasted_iota(jnp.int32, (16, 16), 1)
    ).astype(F32)
    columns = dot(eye.astype(BF), rows128[...].astype(BF), NT)
    bias = jnp.concatenate([jnp.zeros((1, 64), F32), up_bias[...].astype(F32)], axis=1)
    row = lax.broadcasted_iota(jnp.int32, (16, 128), 0)
    lane = lax.broadcasted_iota(jnp.int32, (16, 128), 1)
    a0[:, 1536:1664] = jnp.where((row == 0) & (lane >= 64), bias, columns).astype(BF)
    a0[:, 1664:2176] = mix[...]
    a0[:, 2176:4224] = up[...]
    for part in range(4):
        c0[:, 512 * part : 512 * part + 512] = down[16 * part : 16 * part + 16, :]


def pack(qkv, mix, up, down, gain, shift, qv, proj, up_bias):
    return pl.pallas_call(
        pack_kernel,
        in_specs=[vmem()] * 9,
        out_specs=[vmem()] * 2,
        out_shape=[shape((16, 4224), BF), shape((16, 2048), BF)],
        scratch_shapes=[pltpu.VMEM((128, 16), F32)],
        cost_estimate=cost(1.5),
        name="pack",
    )(qkv, mix, up, down, gain, shift, qv, proj, up_bias.reshape(1, 64))


def aux_rows(chain):
    row = lax.broadcasted_iota(jnp.int32, (128, chain.shape[1]), 0)
    low_bits = jnp.where(row < 7, (chain >> jnp.minimum(row, 6)) & 1, 0)
    high_bits = jnp.where(
        (row >= 7) & (row < 14), 1 - ((chain >> jnp.minimum(jnp.maximum(row - 7, 0), 6)) & 1), 0
    )
    bits = low_bits + high_bits
    query_side = bits.astype(F32) * HIDE
    key_side = jnp.where(row < 14, 1 - bits, jnp.where(row < 17, 1, 0)).astype(F32)
    return query_side.astype(BF), key_side.T.astype(BF)


def pair_forward(normed, weight, bias_q, bias_v, key_aux, qa, ot, outs, pair, block):
    qkv_out, o_out, ot_out, lse_out = outs
    rows = normed.shape[0]
    cols = block_of(pair, 128)
    q2 = (dot(normed, weight[:, 0:128]) + bias_q).astype(BF)
    k2 = dot(normed, weight[:, 128:256]).astype(BF)
    v2 = (dot(normed, weight[:, 256:384]) + bias_v).astype(BF)
    for index, value in enumerate((q2, k2, v2)):
        qkv_out[pair, index] = value
    qa[0:128, :] = q2.T
    vt = v2.T
    ones = (lax.broadcasted_iota(jnp.int32, (16, rows), 0) == 0).astype(F32).astype(BF)
    lane = lax.broadcasted_iota(jnp.int32, k2.shape, 1)
    zero = jnp.zeros_like(k2)
    keys = [
        jnp.concatenate([jnp.where((lane >= 64) == bool(h), k2, zero), key_aux], axis=1)
        for h in range(2)
    ]
    vts = [jnp.concatenate([vt[64 * h : 64 * h + 64], ones], axis=0) for h in range(2)]
    count = rows // block

    def score(index):
        q_cols = qa[:, block * index : block * index + block]
        return [dot(keys[h], q_cols) for h in range(2)]

    ahead = score(0)
    for index in range(count):
        scores = ahead
        if index + 1 < count:
            ahead = score(index + 1)
        span = slice(block * index, block * index + block)
        for h in range(2):
            peak = jnp.max(scores[h], axis=0, keepdims=True)
            probs = jnp.exp2((scores[h] - peak) * EXP_SCALE).astype(BF)
            mixed = dot(vts[h], probs)
            total = mixed[64:65]
            ot[64 * h : 64 * h + 64, span] = mixed[:64] * (1.0 / total)
            lse_out[pair, h : h + 1, span] = peak + jnp.log(total) * (1.0 / SCALE)
    ot_out[cols, :] = ot[...].astype(BF)
    o_out[:, cols] = ot[...].T.astype(BF)


def forward_kernel(me_ref, tokens, chain, mine, other, *refs):
    qkv_hbm, normed_t_hbm, weight_hbm, o_out, ot_out, lse_out = refs[:6]
    smalls, up_row, key_aux_out, query_aux_out = refs[6:10]
    qa, ot, columns, qkv_out, normed_out, normed_t, weight, sems = refs[10:]
    me = me_ref[1]
    for c, j, i in slots():
        source = (mine, other)[c]
        row = block_row(me, c, j, i, 16)
        weight[pl.ds(row, 16), :] = source[4 * j + i, :, 0:1536]
        columns[pl.ds(row, 16), :] = source[4 * j + i, :, 1536:1664].astype(F32)
    smalls[...] = columns[...].T[0:8, :]
    lane = lax.broadcasted_iota(jnp.int32, (1, 128), 1)
    for a in range(16):
        even = pltpu.roll(columns[32 * a : 32 * a + 8, :], 64, 1)[0:1, :]
        odd = columns[32 * a + 16 : 32 * a + 17, :]
        up_row[:, 128 * a : 128 * a + 128] = jnp.where(lane < 64, even, odd)
    query_side, key_side = aux_rows(chain[...])
    qa[128:256, :] = query_side
    query_aux_out[...] = query_side
    key_aux_out[...] = key_side

    def norm_block(index, carry):
        span = pl.ds(pl.multiple_of(index * 256, 256), 256)
        centred, scale = row_stats(tokens[span, :].astype(F32))
        normed_out[span, :] = (centred * scale * smalls[0:1, :] + smalls[2:3, :]).astype(BF)
        return carry

    lax.fori_loop(0, tokens.shape[0] // 256, norm_block, 0)
    normed = normed_out[...]
    normed_t[0:512, :] = normed.T
    ones_row = lax.broadcasted_iota(jnp.int32, (16, normed.shape[0]), 0) == 0
    normed_t[512:528, :] = ones_row.astype(F32).astype(BF)
    copies = [
        pltpu.make_async_copy(normed_t, normed_t_hbm, sems.at[4]),
        pltpu.make_async_copy(weight, weight_hbm, sems.at[5]),
    ]
    for copy in copies:
        copy.start()
    outs = (qkv_out, o_out, ot_out, lse_out)

    def one_pair(pair, carry):
        cols = block_of(pair, 128)
        pair_forward(
            normed_out[...], weight[:, block_of(pair, 384)], smalls[4:5, cols], smalls[5:6, cols],
            key_aux_out[...], qa, ot, outs, pair, 512,
        )
        pltpu.make_async_copy(qkv_out.at[pair], qkv_hbm.at[pair], sems.at[pair]).start()
        return carry

    lax.fori_loop(0, 4, one_pair, 0)
    for pair in range(4):
        pltpu.make_async_copy(qkv_out.at[pair], qkv_hbm.at[pair], sems.at[pair]).wait()
    for copy in copies:
        copy.wait()


def hbm():
    return pl.BlockSpec(memory_space=pltpu.HBM)


def forward(me, tokens, chain, mine, other):
    rows = tokens.shape[0]
    return pl.pallas_call(
        forward_kernel,
        in_specs=[smem()] + [vmem()] * 4,
        out_specs=[hbm()] * 3 + [vmem()] * 7,
        out_shape=[
            shape((4, 3, rows, 128), BF),
            shape((528, rows), BF),
            shape((512, 1536), BF),
            shape((rows, 512), BF),
            shape((512, rows), BF),
            shape((4, 2, rows), F32),
            shape((8, 512), F32),
            shape((1, 2048), F32),
            shape((rows, 128), BF),
            shape((128, rows), BF),
        ],
        scratch_shapes=[
            pltpu.VMEM((256, rows), BF),
            pltpu.VMEM((128, rows), F32),
            pltpu.VMEM((512, 128), F32),
            pltpu.VMEM((4, 3, rows, 128), BF),
            pltpu.VMEM((rows, 512), BF),
            pltpu.VMEM((528, rows), BF),
            pltpu.VMEM((512, 1536), BF),
            pltpu.SemaphoreType.DMA((6,)),
        ],
        compiler_params=pltpu.CompilerParams(vmem_limit_bytes=20 * MIB),
        cost_estimate=cost(15),
        name="attend",
    )(me, tokens, chain, mine, other)


def gelu_parts(u):
    half_cdf = 0.5 + 0.5 * lax.erf(u * math.sqrt(0.5))
    density = jnp.exp2(u * u * (-0.5 * math.log2(math.e))) * (1.0 / math.sqrt(2.0 * math.pi))
    return u * half_cdf, half_cdf + u * density


def scatter_tall(me, source, base_block, send, keep):
    core = me & 1
    for half in range(4):
        r = (me ^ (base_block + 2 * half)) >> 1
        place = ((r & 3) << 2) | (r >> 2)
        for part in range(4):
            row = 128 * half + 16 * part
            span = slice(512 * part, 512 * part + 512)
            keep[place, :, span] = source[pl.ds(pl.multiple_of(row + core * 64, 16), 16), :]
            sent = source[pl.ds(pl.multiple_of(row + (1 - core) * 64, 16), 16), :]
            send[place, :, span] = sent.astype(BF)


def scatter_blocks(me, source, rows, base_block, blocks, send, keep, span):
    core = me & 1
    for half in range(blocks // 2):
        first = base_block + 2 * half
        row = 2 * half * rows
        r = (me ^ first) >> 1
        place = ((r & 3) << 2) | (r >> 2)
        kept = source[pl.ds(pl.multiple_of(row + core * rows, rows), rows), :]
        sent = source[pl.ds(pl.multiple_of(row + (1 - core) * rows, rows), rows), :]
        keep[place, :, span] = kept
        send[place, :, span] = sent.astype(BF)


def feed_first_kernel(
    me_ref, tokens, o_in, mine, other, mine_tall, other_tall, smalls, up_row, cot,
    middle, normed_t, grad_pre_out, d_send, d_keep, mix, up, act_rows, down,
    normed, stage,
):
    me = me_ref[0]
    for c, j, i in slots():
        source = (mine, other)[c]
        row = block_row(me, c, j, i, 16)
        mix[pl.ds(row, 16), :] = source[4 * j + i, :, 0:512]
        up[pl.ds(row, 16), :] = source[4 * j + i, :, 512:2560]
        source = (mine_tall, other_tall)[c]
        for part in range(4):
            row = pl.multiple_of(block_row(me, c, j, i, 64) + 16 * part, 16)
            span = slice(512 * part, 512 * part + 512)
            down[pl.ds(row, 16), :] = source[4 * TALL_ORDER[i] + j, :, span]
    rows = tokens.shape[0]
    block = 256

    def ahead(index, carry):
        span = pl.ds(pl.multiple_of(index * block, block), block)
        mid = tokens[span, :].astype(F32) + dot(o_in[span, :], mix[...]) + smalls[6:7, :]
        middle[span, :] = mid
        centred, scale = row_stats(mid)
        normed[span, :] = (centred * scale * smalls[1:2, :] + smalls[3:4, :]).astype(BF)
        return carry

    lax.fori_loop(0, rows // block, ahead, 0)
    normed_t[0:512, :] = normed[...].T
    ones_row = lax.broadcasted_iota(jnp.int32, (16, rows), 0) == 0
    normed_t[512:528, :] = ones_row.astype(F32).astype(BF)
    width = 512

    def one_chunk(chunk, carry):
        span = block_of(chunk, width)
        down_part = down[span, :]
        act, slope = gelu_parts(dot(normed[...], up[:, span]) + up_row[:, span])
        act_low = act.astype(BF)
        grad_pre_out[:, span] = (dot(cot[...], down_part, NT) * slope).astype(BF)
        act_rows[:, span] = act_low
        stage[...] = dot(act_low, cot[...], TN)
        scatter_tall(me, stage, chunk * (width // 64), d_send, d_keep)
        return carry

    lax.fori_loop(0, 2048 // width, one_chunk, 0)


def feed_first(me, tokens, o_in, b_pair, c_pair, smalls, up_row, cot):
    rows = tokens.shape[0]
    return pl.pallas_call(
        feed_first_kernel,
        in_specs=[smem()] + [vmem()] * 9,
        out_specs=[vmem()] * 9,
        out_shape=[
            shape((rows, 512), F32),
            shape((528, rows), BF),
            shape((rows, 2048), BF),
            shape((16, 16, 2048), BF),
            shape((16, 16, 2048), F32),
            shape((512, 512), BF),
            shape((512, 2048), BF),
            shape((rows, 2048), BF),
            shape((2048, 512), BF),
        ],
        scratch_shapes=[
            pltpu.VMEM((rows, 512), BF),
            pltpu.VMEM((512, 512), F32),
        ],
        compiler_params=pltpu.CompilerParams(vmem_limit_bytes=14 * MIB),
        cost_estimate=cost(18),
        name="feed_first",
    )(me, tokens, o_in, *b_pair, *c_pair, smalls, up_row, cot)


def feed_second_kernel(me_ref, normed_t, grad_pre, u_send, u_keep, up_bias_grad, stage):
    me = me_ref[0]
    width = 512

    def one_chunk(chunk, carry):
        span = block_of(chunk, width)
        stage[...] = dot(normed_t[...], grad_pre[:, span])
        up_bias_grad[:, span] = stage[512:513, :]
        scatter_blocks(me, stage, 16, 0, 32, u_send, u_keep, span)
        return carry

    lax.fori_loop(0, 2048 // width, one_chunk, 0)


def feed_second(me, normed_t, grad_pre):
    return pl.pallas_call(
        feed_second_kernel,
        in_specs=[smem()] + [vmem()] * 2,
        out_specs=[vmem()] * 3,
        out_shape=[
            shape((16, 16, 2048), BF),
            shape((16, 16, 2048), F32),
            shape((1, 2048), F32),
        ],
        scratch_shapes=[pltpu.VMEM((528, 512), F32)],
        compiler_params=pltpu.CompilerParams(vmem_limit_bytes=10 * MIB),
        cost_estimate=cost(5),
        name="feed_second",
    )(me, normed_t, grad_pre)


def feed_third_kernel(
    middle, grad_pre, mix, up, smalls, cot, ot_in,
    grad_middle, grad_att, mix_grad, small_grads, low_rows,
):
    rows = middle.shape[0]
    block = 256

    def behind(index, carry):
        gain_sum, shift_sum, branch_sum, cot_sum = carry
        span = pl.ds(pl.multiple_of(index * block, block), block)
        centred, scale = row_stats(middle[span, :])
        xh = centred * scale
        h = dot(grad_pre[span, :], up[...], NT)
        hg = h * smalls[1:2, :]
        cot_rows = cot[span, :].astype(F32)
        grad = cot_rows + scale * (
            hg
            - jnp.mean(hg, axis=-1, keepdims=True)
            - xh * jnp.mean(hg * xh, axis=-1, keepdims=True)
        )
        grad_middle[span, :] = grad
        low = grad.astype(BF)
        low_rows[span, :] = low
        grad_att[span, :] = dot(low, mix[...], NT).astype(BF)
        return (
            gain_sum + jnp.sum(h * xh, axis=0, keepdims=True),
            shift_sum + jnp.sum(h, axis=0, keepdims=True),
            branch_sum + jnp.sum(low.astype(F32), axis=0, keepdims=True),
            cot_sum + jnp.sum(cot_rows, axis=0, keepdims=True),
        )

    zero = jnp.zeros((1, 512), F32)
    sums = lax.fori_loop(0, rows // block, behind, (zero, zero, zero, zero))
    for index in range(4):
        small_grads[index : index + 1, :] = sums[index]
    small_grads[4:8, :] = jnp.zeros((4, 512), F32)
    mix_grad[0:256, :] = dot(ot_in[0:256, :], low_rows[...])
    mix_grad[256:512, :] = dot(ot_in[256:512, :], low_rows[...])


def feed_third(middle, grad_pre, mix, up, smalls, cot, ot_in):
    rows = middle.shape[0]
    return pl.pallas_call(
        feed_third_kernel,
        in_specs=[vmem()] * 7,
        out_specs=[vmem()] * 4,
        out_shape=[
            shape((rows, 512), F32),
            shape((rows, 512), BF),
            shape((512, 512), F32),
            shape((8, 512), F32),
        ],
        scratch_shapes=[pltpu.VMEM((rows, 512), BF)],
        compiler_params=pltpu.CompilerParams(vmem_limit_bytes=12 * MIB),
        cost_estimate=cost(8),
        name="feed_third",
    )(middle, grad_pre, mix, up, smalls, cot, ot_in)


def pair_backward(q, k, v, do, ot_in, lse, key_aux, qa, da, dqt, acc_k, acc_v, gm, block):
    k2 = k[0, 0]
    v2 = v[0, 0]
    rows = k2.shape[0]
    kt = k2.T
    lane = lax.broadcasted_iota(jnp.int32, k2.shape, 1)
    zero = jnp.zeros_like(k2)
    keys = []
    vals = []
    for h in range(2):
        own = (lane >= 64) == bool(h)
        keys.append(jnp.concatenate([jnp.where(own, k2, zero), key_aux], axis=1))
        vals.append(jnp.concatenate([jnp.where(own, v2, zero), key_aux], axis=1))
    qt = q[0, 0].T
    dt = do[...].T
    product = dt.astype(F32) * ot_in[...].astype(F32)
    row = lax.broadcasted_iota(jnp.int32, (16, rows), 0)
    for h in range(2):
        qa[h, 0:128, :] = qt
        da[h, 0:128, :] = dt
        delta = jnp.sum(product[64 * h : 64 * h + 64], axis=0, keepdims=True)
        base = qa[h, 128:144, :].astype(F32)
        one, two, three = split_three(-lse[0, h : h + 1, :])
        base = jnp.where(row == 14, one, jnp.where(row == 15, two, base))
        qa[h, 128:144, :] = base.astype(BF)
        qa[h, 144:160, :] = jnp.where(row == 0, three, 0.0).astype(BF)
        one, two, three = split_three(-delta)
        base = jnp.where(row == 14, one, jnp.where(row == 15, two, 0.0))
        da[h, 128:144, :] = base.astype(BF)
        da[h, 144:160, :] = jnp.where(row == 0, three, 0.0).astype(BF)
    small_lane = lax.broadcasted_iota(jnp.int32, (block, 128), 1)
    for index in range(rows // block):
        span = slice(block * index, block * index + block)
        do_rows = do[span, :]
        q_rows = q[0, 0, span, :]
        blank = jnp.zeros_like(do_rows)
        sum_k = None
        sum_v = None
        for h in range(2):
            own = (small_lane >= 64) == bool(h)
            probs = jnp.exp2(dot(keys[h], qa[h, :, span]) * EXP_SCALE)
            grad = (probs * dot(vals[h], da[h, :, span])).astype(BF)
            probs = probs.astype(BF)
            dqt[64 * h : 64 * h + 64, span] = dot(kt[64 * h : 64 * h + 64, :], grad)
            part_k = dot(grad, jnp.where(own, q_rows, blank))
            part_v = dot(probs, jnp.where(own, do_rows, blank))
            sum_k = part_k if sum_k is None else sum_k + part_k
            sum_v = part_v if sum_v is None else sum_v + part_v
        if index == 0:
            acc_k[...] = sum_k
            acc_v[...] = sum_v
        else:
            acc_k[...] += sum_k
            acc_v[...] += sum_v
    gm[:, 0:128] = (dqt[...].T * SCALE).astype(BF)
    gm[:, 128:256] = (acc_k[...] * SCALE).astype(BF)
    gm[:, 256:384] = acc_v[...].astype(BF)


def backward_kernel(
    me_ref, q, k, v, do, ot_in, lse, weight, key_aux, query_aux, normed_t, smalls, small_grads,
    up_bias_grad, mix_term, gm, send, keep,
    qa, da, dqt, acc_k, acc_v, gm_pair, stage, sums, vectors, columns,
):
    me = me_ref[0]
    pair = pl.program_id(0)

    @pl.when(pair == 0)
    def _():
        for h in range(2):
            qa[h, 128:256, :] = query_aux[...]
            da[h, 128:256, :] = jnp.zeros((128, da.shape[2]), BF)
        vectors[...] = jnp.zeros_like(vectors)
        scatter_blocks(me, mix_term, 16, 0, 32, send, keep, slice(1536, 2048))

    pair_backward(q, k, v, do, ot_in, lse, key_aux[...], qa, da, dqt, acc_k, acc_v, gm_pair, 512)
    span = block_of(pair, 384)
    gm[:, span] = gm_pair[...]
    stage[...] = dot(normed_t[...], gm_pair[...])
    total = stage[512:513, :]
    sums[:, span] = jnp.broadcast_to(total, (8, 384))
    scatter_blocks(me, stage, 16, 0, 32, send, keep, span)
    wide = weight[...].astype(F32)
    vectors[:, 0:1] += jnp.sum(stage[0:512, :] * wide, axis=1, keepdims=True)
    vectors[:, 1:2] += jnp.sum(wide * total, axis=1, keepdims=True)

    @pl.when(pair == 3)
    def _():
        columns[...] = jnp.zeros_like(columns)
        columns[1:2, :] = small_grads[0:1, :]
        columns[3:4, :] = small_grads[1:2, :]
        for index in range(4):
            cols = slice(128 * index, 128 * index + 128)
            columns[4:5, cols] = sums[0:1, 384 * index : 384 * index + 128]
            columns[5:6, cols] = sums[0:1, 384 * index + 256 : 384 * index + 384]
        columns[6:7, :] = small_grads[2:3, :]
        columns[7:8, :] = small_grads[3:4, :]
        columns[8:9, :] = smalls[0:1, :]
        columns[9:10, :] = smalls[2:3, :]
        tile = columns[...].T
        plain = vectors[:, 1:2]
        gain_sum = (vectors[:, 0:1] - tile[:, 9:10] * plain) / tile[:, 8:9]
        lanes = lax.broadcasted_iota(jnp.int32, (512, 128), 1)
        stage[0:512, 0:128] = jnp.where(lanes == 0, gain_sum, jnp.where(lanes == 2, plain, tile))
        lane = lax.broadcasted_iota(jnp.int32, (1, 128), 1)
        for a in range(16):
            piece = up_bias_grad[:, 128 * a : 128 * a + 128]
            rolled = pltpu.roll(jnp.broadcast_to(piece, (8, 128)), 64, 1)[0:1, :]
            for half, values in enumerate((rolled, piece)):
                row = 32 * a + 16 * half
                old = stage[row : row + 1, 0:128]
                stage[row : row + 1, 0:128] = jnp.where(lane < 64, old, values)
        core = me & 1
        for half in range(16):
            r = (me ^ (2 * half)) >> 1
            place = ((r & 3) << 2) | (r >> 2)
            kept = pl.multiple_of(32 * half + core * 16, 16)
            sent = pl.multiple_of(32 * half + (1 - core) * 16, 16)
            keep[place, :, 2048:2176] = stage[pl.ds(kept, 16), 0:128]
            send[place, :, 2048:2176] = stage[pl.ds(sent, 16), 0:128].astype(BF)


def backward(me, qkv_rows, do, ot, lse, weight, *rest):
    rows = do.shape[0]
    parts = [pl.BlockSpec((1, 1, rows, 128), lambda i, part=part: (i, part, 0, 0)) for part in range(3)]
    return pl.pallas_call(
        backward_kernel,
        grid=(4,),
        in_specs=[smem()]
        + parts
        + [
            pl.BlockSpec((rows, 128), lambda i: (0, i)),
            pl.BlockSpec((128, rows), lambda i: (i, 0)),
            pl.BlockSpec((1, 2, rows), lambda i: (i, 0, 0)),
            pl.BlockSpec((512, 384), lambda i: (0, i)),
        ]
        + [vmem()] * 7,
        out_specs=[vmem()] * 3,
        out_shape=[
            shape((rows, 1536), BF),
            shape((16, 16, 2176), BF),
            shape((16, 16, 2176), F32),
        ],
        scratch_shapes=[
            pltpu.VMEM((2, 256, rows), BF),
            pltpu.VMEM((2, 256, rows), BF),
            pltpu.VMEM((128, rows), F32),
            pltpu.VMEM((rows, 128), F32),
            pltpu.VMEM((rows, 128), F32),
            pltpu.VMEM((rows, 384), BF),
            pltpu.VMEM((528, 384), F32),
            pltpu.VMEM((8, 1536), F32),
            pltpu.VMEM((512, 128), F32),
            pltpu.VMEM((128, 512), F32),
        ],
        compiler_params=pltpu.CompilerParams(vmem_limit_bytes=20 * MIB),
        cost_estimate=cost(25),
        name="attend_back",
    )(me, qkv_rows, qkv_rows, qkv_rows, do, ot, lse, weight, *rest)


def input_kernel(
    tokens, gm, weight, smalls, grad_middle, act, down, middle, input_grad, output
):
    block = 256

    def behind(index, carry):
        span = pl.ds(pl.multiple_of(index * block, block), block)
        centred, scale = row_stats(tokens[span, :].astype(F32))
        xh = centred * scale
        total = middle[span, :] + dot(act[span, :], down[...]) + smalls[7:8, :]
        output[span, :] = total.astype(BF)
        hg = dot(gm[span, :], weight[...], NT) * smalls[0:1, :]
        input_grad[span, :] = grad_middle[span, :] + scale * (
            hg
            - jnp.mean(hg, axis=-1, keepdims=True)
            - xh * jnp.mean(hg * xh, axis=-1, keepdims=True)
        )
        return carry

    lax.fori_loop(0, tokens.shape[0] // block, behind, 0)


def input_terms(operands):
    rows = operands[0].shape[0]
    return pl.pallas_call(
        input_kernel,
        in_specs=[vmem()] * 8,
        out_specs=[vmem()] * 2,
        out_shape=[shape((rows, 512), F32), shape((rows, 512), BF)],
        compiler_params=pltpu.CompilerParams(vmem_limit_bytes=12 * MIB),
        cost_estimate=cost(8),
        name="input_terms",
    )(*operands)


def combine_kernel(counts, pieces, *refs):
    total_in = sum(counts) + len(counts)
    outs = refs[total_in:]
    position = 0
    base = 0
    for count in counts:
        own, incoming = refs[position], refs[position + 1 : position + 1 + count]
        position += 1 + count
        width = own.shape[2]
        rows = own.shape[0] // pieces
        for index in range(pieces):
            span = slice(rows * index, rows * index + rows)
            total = own[span]
            for ref in incoming:
                total = total + ref[span].astype(F32)
            outs[index][:, :, base : base + width] = total.astype(outs[index].dtype)
        base += width


def combine(name, pieces, *sums):
    slot_count = sums[0][0].shape[0] // pieces
    width = sum(own.shape[2] for own, _ in sums)
    operands = [part for own, received in sums for part in (own, *received)]
    dims = (slot_count, 16, width)
    first, *rest = pl.pallas_call(
        functools.partial(combine_kernel, [len(received) for _, received in sums], pieces),
        in_specs=[vmem()] * len(operands),
        out_specs=[vmem()] * pieces,
        out_shape=[shape(dims, F32)] + [shape(dims, BF)] * (pieces - 1),
        compiler_params=pltpu.CompilerParams(vmem_limit_bytes=8 * MIB),
        cost_estimate=cost(1.5),
        name=name,
    )(*operands)
    return first, rest


def finish_kernel(
    own, r0, r1, r2, du_own, du_recv,
    qkv_grad, mix_grad, up_grad, down_grad, gain, shift, qv, proj, bias,
):
    total = own[0]
    for ref in (r0, r1, r2):
        total = total + ref[0].astype(F32)
    mix_grad[...] = total[:, 1536:2048]
    for pair in range(4):
        for part in range(3):
            base = 384 * pair + 128 * part
            column = 512 * part + 128 * pair
            qkv_grad[:, column : column + 128] = total[:, base : base + 128]
    tile = total[:, 2048:2176]
    wide = jnp.concatenate([tile, jnp.zeros((112, 128), F32)], axis=0).T
    for index, ref in enumerate((gain, shift, qv, proj)):
        ref[...] = wide[2 * index : 2 * index + 2, 0:16]
    bias[...] = tile[0:1, 64:128]
    total = du_own[0] + du_recv[0].astype(F32)
    for part in range(4):
        down_grad[16 * part : 16 * part + 16, :] = total[:, 512 * part : 512 * part + 512]
    up_grad[...] = total[:, 2048:4096]


def finish(own, received, du_own, du_recv):
    return pl.pallas_call(
        finish_kernel,
        in_specs=[vmem()] * 6,
        out_specs=[vmem()] * 9,
        out_shape=[
            shape((16, 1536), F32),
            shape((16, 512), F32),
            shape((16, 2048), F32),
            shape((64, 512), F32),
        ]
        + [shape((2, 16), F32)] * 4
        + [shape((1, 64), F32)],
        cost_estimate=cost(1.5),
        name="finish",
    )(own, *received, du_own, *du_recv)


def swap(value, mask, count):
    return lax.ppermute(value, AXES, [(d, d ^ mask) for d in range(count)])


Z_MASKS = (8, 16, 24)
PLANE_MASKS = (2, 4, 6)


def swaps(value, masks, count):
    return [swap(value, mask, count) for mask in masks]


def point(values, *tokens):
    return lax.optimization_barrier((values, tokens))[0]


def after(value, *tokens):
    return lax.optimization_barrier((value, tokens))[0]


def exchange(parts, masks, count):
    return [swap(part, mask, count) for part, mask in zip(parts, masks, strict=True)]


def group(own, others):
    joined = jnp.stack([own] + others)
    return joined.reshape((-1,) + joined.shape[-2:])


def pack_whole(qkv, mix, up, down, gain, shift, qv, proj, up_bias):
    pieces = []
    for pair in range(4):
        for part in range(3):
            base = 512 * part + 128 * pair
            pieces.append(qkv[:, base : base + 128])
    rows = jnp.concatenate([gain, shift, qv, proj], axis=0)
    tile = jnp.pad(rows.T, ((0, 0), (0, 120))).reshape(32, 16, 128)
    tile = tile.at[:, 0, 64:128].set(up_bias.reshape(32, 64))
    a0 = jnp.concatenate([jnp.concatenate(pieces, 1).reshape(32, 16, 1536), tile], axis=2)
    b0 = jnp.concatenate([mix, up], axis=1).reshape(32, 16, 2560)
    b1 = down.reshape(32, 4, 16, 512).swapaxes(1, 2).reshape(32, 16, 2048)
    return a0, b0, b1


def relative_halves(blocks):
    parts = blocks.reshape((4, 4, 2) + blocks.shape[1:])
    parts = parts.transpose((2, 1, 0) + tuple(range(3, parts.ndim)))
    return parts[0].reshape((16,) + blocks.shape[1:]), parts[1].reshape((16,) + blocks.shape[1:])


def whole_blocks(send, keep):
    parts = jnp.stack([keep, send.astype(F32)]).reshape((2, 4, 4) + keep.shape[1:])
    parts = parts.transpose((2, 1, 0) + tuple(range(3, parts.ndim)))
    return parts.reshape((32,) + keep.shape[1:])


def body(cubic, count, tokens, chain_ids, qkv, mix, up, down, gain, shift, qv, proj, up_bias, cot):
    params = (qkv, mix, up, down, gain, shift, qv, proj, up_bias)
    if cubic:
        index = lax.axis_index(AXES).astype(jnp.int32)
        me = jnp.stack([index, index & ~6])
        own, c_own = pack(*params)
        recv = swaps(own, Z_MASKS, count)
        c_recv = swaps(c_own, PLANE_MASKS, count)
        recv = point(recv)
        a_col = jnp.stack([part[:, :1664] for part in (own, *recv)])
        c_plane = group(c_own, after(c_recv, a_col))
        c_recv = swap(c_plane, 16, count)
        a_mine = lax.all_gather(after(a_col, c_plane), "plane").reshape(16, 16, -1)
        a_mine, c_recv = point((a_mine, c_recv))
        a_other = swap(a_mine, 1, count)
        own, *recv = after((own, *recv), a_mine)
        b_col = jnp.stack([part[:, 1664:] for part in (own, *recv)])
        b_recv = swaps(b_col, PLANE_MASKS, count)
        c_half = group(c_plane, [c_recv])
        c_recv = swap(c_half, 8, count)
        a_mine, a_other = after((a_mine, a_other), b_col, c_half)
    else:
        me = jnp.zeros((2,), jnp.int32)
        dims = (0, 0, 0, 0, 1, 1, 1, 1, 0)
        whole = [
            lax.all_gather(value, AXES, axis=dim, tiled=True)
            for value, dim in zip(params, dims, strict=True)
        ]
        a_parts, b_parts, c_parts = pack_whole(*whole)
        a_mine, a_other = relative_halves(a_parts)
        b_pair = relative_halves(b_parts)
        c_pair = [
            half.reshape(4, 2, 2, 16, 2048).transpose(2, 1, 0, 3, 4).reshape(16, 16, 2048)
            for half in relative_halves(c_parts)
        ]
    (
        qkv_rows, normed_t, weight, o, ot, lse, smalls, up_row, key_aux, query_aux,
    ) = forward(me, tokens, chain_ids, a_mine, a_other)
    if cubic:
        b_recv, c_recv, lse = point((b_recv, c_recv, lse))
        b_mine = group(b_col, b_recv)
        c_mine = group(c_half, [c_recv])
        b_pair = (b_mine, swap(b_mine, 1, count))
        c_pair = (c_mine, swap(c_mine, 1, count))
    (
        middle, normed_two_t, grad_pre, d_send, d_keep, mix_whole, up_whole, act_rows, down_whole,
    ) = feed_first(me, tokens, o, b_pair, c_pair, smalls, up_row, cot)
    if cubic:
        d_recv = swap(d_send, 1, count)
    u_send, u_keep, up_bias_grad = feed_second(me, normed_two_t, grad_pre)
    if cubic:
        u_recv = swap(u_send, 1, count)
    grad_middle, grad_att, mix_term, small_grads = feed_third(
        middle, grad_pre, mix_whole, up_whole, smalls, cot, ot
    )
    if cubic:
        d_recv, u_recv, small_grads = point((d_recv, u_recv, small_grads))
        du_own, du_parts = combine("feed_sum", 4, (d_keep, [d_recv]), (u_keep, [u_recv]))
        du_recv = exchange(du_parts, PLANE_MASKS, count)
        lse = after(lse, du_own)
    gm, g_send, g_keep = backward(
        me, qkv_rows, grad_att, ot, lse, weight, key_aux, query_aux, normed_t, smalls, small_grads,
        up_bias_grad, mix_term,
    )
    if cubic:
        du_recv, g_send, gm = point((du_recv, g_send, gm))
        g_recv = swap(g_send, 1, count)
        du_own, du_parts = combine("feed_sum_two", 2, (du_own, du_recv))
        du_recv = exchange(du_parts, (16,), count)
        g_own, g_parts = combine("last_sum", 4, (g_keep, [after(g_recv, du_own)]))
        g_recv = exchange(g_parts, PLANE_MASKS, count)
        smalls = after(smalls, g_own)
    input_grad, output = input_terms(
        [tokens, gm, weight, smalls, grad_middle, act_rows, down_whole, middle]
    )
    if cubic:
        g_recv, du_recv, input_grad = point((g_recv, du_recv, input_grad))
        own, parts = combine("last_sum_two", 4, (g_own, g_recv))
        g_recv = exchange(parts, Z_MASKS, count)
        du_own, du_parts = combine("feed_sum_three", 2, (du_own, du_recv))
        du_recv = exchange(du_parts, (8,), count)
        qkv_grad, mix_grad, up_grad, down_grad, *vectors, bias_grad = finish(
            own, g_recv, du_own, du_recv
        )
        return (
            output, input_grad, qkv_grad, mix_grad, up_grad, down_grad, *vectors,
            bias_grad.reshape(64),
        )
    pairs = ((d_send, d_keep), (u_send, u_keep), (g_send, g_keep))
    blocks = [whole_blocks(s, r) for s, r in pairs]
    tiles = blocks[2][:, :, 2048:2176]
    joined = blocks[2].reshape(512, 2176)
    wholes = (
        blocks[0].reshape(32, 16, 4, 512).swapaxes(1, 2).reshape(2048, 512),
        blocks[1].reshape(512, 2048),
        joined[:, 1536:2048],
        joined[:, :1536].reshape(512, 4, 3, 128).swapaxes(1, 2).reshape(512, 1536),
        tiles[:, 0, 64:128].reshape(2048),
    )
    down_grad, up_grad, mix_grad, qkv_grad, bias_grad = [
        lax.psum_scatter(value, AXES, scatter_dimension=0, tiled=True) for value in wholes
    ]
    vectors = lax.psum_scatter(
        tiles[:, :, 0:8].reshape(512, 8).T, AXES, scatter_dimension=1, tiled=True
    )
    return (
        output, input_grad, qkv_grad, mix_grad, up_grad, down_grad,
        vectors[0:2], vectors[2:4], vectors[4:6], vectors[6:8], bias_grad,
    )


def solution(mesh):
    groups = mesh.shape["dp"]
    count = groups * mesh.shape["fsdp"]
    inner = jax.sharding.Mesh(mesh.devices.reshape(groups, -1, 2), AXES)
    cubic = inner.devices.shape == (4, 4, 2)

    def entry(*operands):
        return body(cubic, count, *operands)

    rows = P(AXES, None)
    columns = P(None, AXES)
    flat = P(AXES)
    return jax.shard_map(
        entry,
        mesh=inner,
        in_specs=(rows,) * 6 + (columns,) * 4 + (flat, rows),
        out_specs=(rows,) * 6 + (columns,) * 4 + (flat,),
        check_vma=False,
    )
```

profile of v0, /device:TPU:0, one launch (start us, length us, event | category | flops | bytes accessed | tf_op | source)
XLA Modules:
  0.0 147.7 jit_solution(11568096871178794856)
XLA Ops:
  0.6 1.8 %pack.1 = (bf16[16,4224]{1,0:T(8,128)(2,1)}, bf16[16,2048]{1,0:T(8,128)(2,1)}) custom-call(bf16[16,1536]{1,0:T(8,128)(2,1)} %qkv.1, bf16[16,512]{1,0:T(8,128)(2,1)} %mix.1, bf16[16,2048]{1,0:T(8,128)(2,1)} %up.1, bf16[64,512]{1,0:T(8,128)(2,1)} %down.1, bf16[2,16]{1,0:T(2,128)(2,1)} %gain.1, bf16[2,16]{1,0:T(2,128)(2,1)} %shift.1, bf16[2,16]{1,0:T(2,128)(2,1)} %qv.1, ...), custom_call_target="tpu_custom_call" | custom-call | flops 1650000000 | tf_op jit(solution)/shard_map/pack/pallas_call | solution.py:98
  2.4 3.0 %collective-permute-start = (bf16[16,4224]{1,0:T(8,128)(2,1)}, bf16[16,4224]{1,0:T(8,128)(2,1)S(1)}, u32[]{:S(2)}, u32[]{:S(2)}) collective-permute-start(bf16[16,4224]{1,0:T(8,128)(2,1)} %get-tuple-element.115), channel_id=1, source_target_pairs={{0,8},{1,9},{2,10},{3,11},{4,12},{5,13},{6,14},{7,15},{8,0},{9,1},... | collective-permute-start | bytes 405512 | tf_op jit(solution)/shard_map/ppermute | solution.py:728
  5.4 2.6 %collective-permute-start.1 = (bf16[16,4224]{1,0:T(8,128)(2,1)}, bf16[16,4224]{1,0:T(8,128)(2,1)S(1)}, u32[]{:S(2)}, u32[]{:S(2)}) collective-permute-start(bf16[16,4224]{1,0:T(8,128)(2,1)} %get-tuple-element.115), channel_id=1, source_target_pairs={{0,16},{1,17},{2,18},{3,19},{4,20},{5,21},{6,22},{7,23},{8,24},{9,... | collective-permute-start | bytes 405512 | tf_op jit(solution)/shard_map/ppermute | solution.py:728
  13.6 5.3 %collective-permute-done.1 = bf16[16,4224]{1,0:T(8,128)(2,1)S(1)} collective-permute-done((bf16[16,4224]{1,0:T(8,128)(2,1)}, bf16[16,4224]{1,0:T(8,128)(2,1)S(1)}, u32[]{:S(2)}, u32[]{:S(2)}) %collective-permute-start.1) | collective-permute-done | bytes 135200 | tf_op jit(solution)/shard_map/ppermute | solution.py:728
  19.9 3.1 %collective-permute-start.6 = (bf16[4,16,2048]{2,1,0:T(8,128)(2,1)S(1)}, bf16[4,16,2048]{2,1,0:T(8,128)(2,1)S(1)}, u32[]{:S(2)}, u32[]{:S(2)}) collective-permute-start(bf16[4,16,2048]{2,1,0:T(8,128)(2,1)S(1)} %get-tuple-element.202), channel_id=1, source_target_pairs={{0,16},{1,17},{2,18},{3,19},{4,20},{5,21},{6,22},{7,23},{8,24},{9,... | collective-permute-start | bytes 786440 | tf_op jit(solution)/shard_map/ppermute | solution.py:728
  23.0 11.6 %all-gather.mine = bf16[16,16,1664]{2,1,0:T(8,128)(2,1)S(1)} all-gather(bf16[4,16,1664]{2,1,0:T(8,128)(2,1)S(1)} %pad_maximum_fusion.5), channel_id=2, replica_groups=mesh['dp'=4,'plane'=4,'core'=2] {'plane'}, dimensions={0}, use_global_device_ids=true | all-gather | bytes 1064960 | tf_op jit(solution)/shard_map/all_gather | solution.py:795
  34.8 1.7 %collective-permute-start.10 = (bf16[4,16,2560]{2,1,0:T(8,128)(2,1)S(1)}, bf16[4,16,2560]{2,1,0:T(8,128)(2,1)S(1)}, u32[]{:S(2)}, u32[]{:S(2)}) collective-permute-start(bf16[4,16,2560]{2,1,0:T(8,128)(2,1)S(1)} %get-tuple-element.200), channel_id=1, source_target_pairs={{0,6},{1,7},{2,4},{3,5},{4,2},{5,3},{6,0},{7,1},{8,14},{9,15},{10,... | collective-permute-start | bytes 983048 | tf_op jit(solution)/shard_map/ppermute | solution.py:728
  36.6 2.2 %collective-permute-start.8 = (bf16[4,16,2560]{2,1,0:T(8,128)(2,1)S(1)}, bf16[4,16,2560]{2,1,0:T(8,128)(2,1)S(1)}, u32[]{:S(2)}, u32[]{:S(2)}) collective-permute-start(bf16[4,16,2560]{2,1,0:T(8,128)(2,1)S(1)} %get-tuple-element.200), channel_id=1, source_target_pairs={{0,2},{1,3},{2,0},{3,1},{4,6},{5,7},{6,4},{7,5},{8,10},{9,11},{10,... | collective-permute-start | bytes 983048 | tf_op jit(solution)/shard_map/ppermute | solution.py:728
  39.0 17.1 %attend.1 = (bf16[4,3,1024,128]{3,2,1,0:T(8,128)(2,1)S(1)}, bf16[528,1024]{1,0:T(8,128)(2,1)S(1)}, bf16[512,1536]{1,0:T(8,128)(2,1)S(1)}, bf16[1024,512]{1,0:T(8...) custom-call(s32[2]{0:T(128)S(1)} %pad_add_fusion.me_ref, ...), custom_call_target="tpu_custom_call" | custom-call | flops 16499999744 | tf_op jit(solution)/shard_map/attend/pallas_call | solution.py:225
  57.0 3.9 %collective-permute-done.13.other_tall = bf16[16,16,2048]{2,1,0:T(8,128)(2,1)S(1)} collective-permute-done((bf16[16,16,2048]{2,1,0:T(8,128)(2,1)S(1)}, bf16[16,16,2048]{2,1,0:T(8,128)(2,1)S(1)}, u32[]{:S(2)}, u32[]{:S(2)}) %collective-permute-start.13) | collective-permute-done | bytes 1048608 | tf_op jit(solution)/shard_map/ppermute | solution.py:728
  60.9 12.8 %feed_first.1 = (f32[1024,512]{1,0:T(8,128)S(1)}, bf16[528,1024]{1,0:T(8,128)(2,1)S(1)}, bf16[1024,2048]{1,0:T(8,128)(2,1)S(1)}, bf16[16,16,2048]{2,1,0:T(8,128)...) custom-call(s32[2]{0:T(128)S(1)} %pad_add_fusion.me_ref, ...), custom_call_target="tpu_custom_call" | custom-call | flops 19800000512 | tf_op jit(solution)/shard_map/feed_first/pallas_call | solution.py:338
  73.7 4.0 %feed_second.1 = (bf16[16,16,2048]{2,1,0:T(8,128)(2,1)S(1)}, f32[16,16,2048]{2,1,0:T(8,128)S(1)}, f32[1,2048]{1,0:T(1,128)S(1)}) custom-call(s32[2]{0:T(128)S(1)} %pad_add_fusion.me_ref, bf16[528,1024]{1,0:T(8,128)(2,1)S(1)} %get-tuple-element.132.normed_t, bf16[1024,2048]{1,0:T(8,128)(2,1)S(1)} %get-tuple-element.133.grad_pre), custom_call_target="tpu_custom_call" | custom-call | flops 5500000256 | tf_op jit(solution)/shard_map/feed_second/pallas_call | solution.py:378
  78.2 5.3 %feed_third.1 = (f32[1024,512]{1,0:T(8,128)S(1)}, bf16[1024,512]{1,0:T(8,128)(2,1)S(1)}, f32[512,512]{1,0:T(8,128)S(1)}, f32[8,512]{1,0:T(8,128)S(1)}) custom-call(f32[1024,512]{1,0:T(8,128)S(1)} %get-tuple-element.135.middle, bf16[1024,2048]{1,0:T(8,128)(2,1)S(1)} %get-tuple-element.133.grad_pre, bf16[512,512]{1,0:T(8,128)(2,1)S(1)} %get-tuple-element.136.mix, ...), custom_call_target="tpu_custom_call" | custom-call | flops 8800000000 | tf_op jit(solution)/shard_map/feed_third/pallas_call | solution.py:436
  84.0 2.0 %collective-permute-start.16 = (bf16[4,16,4096]{2,1,0:T(8,128)(2,1)S(1)}, bf16[4,16,4096]{2,1,0:T(8,128)(2,1)S(1)}, u32[]{:S(2)}, u32[]{:S(2)}) collective-permute-start(bf16[4,16,4096]{2,1,0:T(8,128)(2,1)S(1)} %get-tuple-element.143), channel_id=1, source_target_pairs={{0,2},{1,3},{2,0},{3,1},{4,6},{5,7},{6,4},{7,5},{8,10},{9,11},{10,... | collective-permute-start | bytes 1572872 | tf_op jit(solution)/shard_map/ppermute | solution.py:728
  87.5 26.9 %attend_back.1 = (bf16[1024,1536]{1,0:T(8,128)(2,1)S(1)}, bf16[16,16,2176]{2,1,0:T(8,128)(2,1)S(1)}, f32[16,16,2176]{2,1,0:T(8,128)S(1)}) custom-call(s32[2]{0:T(128)S(1)} %pad_add_fusion.me_ref, bf16[4,3,1024,128]{3,2,1,0:T(8,128)(2,1)S(1)} %get-tuple-element.146.q.k.v, bf16[4,3,1024,128]{3,2,1,0:T(8,128)(2,1)S(1)} %get-tuple-element.146.q.k.v, ...), custom_call_target="tpu_custom_call" | custom-call | flops 27499999232 | tf_op jit(solution)/shard_map/attend_back/pallas_call | solution.py:578
  114.8 2.0 %collective-permute-start.23 = (bf16[2,16,4096]{2,1,0:T(8,128)(2,1)S(1)}, bf16[2,16,4096]{2,1,0:T(8,128)(2,1)S(1)}, u32[]{:S(2)}, u32[]{:S(2)}) collective-permute-start(bf16[2,16,4096]{2,1,0:T(8,128)(2,1)S(1)} %get-tuple-element.177), channel_id=1, source_target_pairs={{0,16},{1,17},{2,18},{3,19},{4,20},{5,21},{6,22},{7,23},{8,24},{9,... | collective-permute-start | bytes 786440 | tf_op jit(solution)/shard_map/ppermute | solution.py:728
  117.5 2.0 %collective-permute-start.20 = (bf16[4,16,2176]{2,1,0:T(8,128)(2,1)S(1)}, bf16[4,16,2176]{2,1,0:T(8,128)(2,1)S(1)}, u32[]{:S(2)}, u32[]{:S(2)}) collective-permute-start(bf16[4,16,2176]{2,1,0:T(8,128)(2,1)S(1)} %get-tuple-element.174), channel_id=1, source_target_pairs={{0,2},{1,3},{2,0},{3,1},{4,6},{5,7},{6,4},{7,5},{8,10},{9,11},{10,... | collective-permute-start | bytes 835592 | tf_op jit(solution)/shard_map/ppermute | solution.py:728
  121.1 6.4 %input_terms.1 = (f32[1024,512]{1,0:T(8,128)}, bf16[1024,512]{1,0:T(8,128)(2,1)}) custom-call(bf16[1024,512]{1,0:T(8,128)(2,1)S(1)} %copy-done.1, bf16[1024,1536]{1,0:T(8,128)(2,1)S(1)} %get-tuple-element.160.gm, bf16[512,1536]{1,0:T(8,128)(2,1)S(1)} %get-tuple-element.151.weight, f32[8,512]{1,0:T(8,128)S(1)} %get-tuple-element.169.smalls, ...), custom_call_target="tpu_custom_call" | custom-call | flops 8800000000 | tf_op jit(solution)/shard_map/input_terms/pallas_call | solution.py:638
  127.5 2.6 %collective-permute-done.23.refs_1_ = bf16[2,16,4096]{2,1,0:T(8,128)(2,1)S(1)} collective-permute-done((bf16[2,16,4096]{2,1,0:T(8,128)(2,1)S(1)}, bf16[2,16,4096]{2,1,0:T(8,128)(2,1)S(1)}, u32[]{:S(2)}, u32[]{:S(2)}) %collective-permute-start.23) | collective-permute-done | bytes 262176 | tf_op jit(solution)/shard_map/ppermute | solution.py:728
  130.1 3.9 %collective-permute-done.21.refs_2_ = bf16[4,16,2176]{2,1,0:T(8,128)(2,1)S(1)} collective-permute-done((bf16[4,16,2176]{2,1,0:T(8,128)(2,1)S(1)}, bf16[4,16,2176]{2,1,0:T(8,128)(2,1)S(1)}, u32[]{:S(2)}, u32[]{:S(2)}) %collective-permute-start.21) | collective-permute-done | bytes 278560 | tf_op jit(solution)/shard_map/ppermute | solution.py:728
  134.0 2.1 %collective-permute-start.27 = (bf16[1,16,4096]{2,1,0:T(8,128)(2,1)S(1)}, bf16[1,16,4096]{2,1,0:T(8,128)(2,1)S(1)}, u32[]{:S(2)}, u32[]{:S(2)}) collective-permute-start(bf16[1,16,4096]{2,1,0:T(8,128)(2,1)S(1)} %get-tuple-element.189), channel_id=1, source_target_pairs={{0,8},{1,9},{2,10},{3,11},{4,12},{5,13},{6,14},{7,15},{8,0},{9,1},... | collective-permute-start | bytes 393224 | tf_op jit(solution)/shard_map/ppermute | solution.py:728
  138.8 2.5 %collective-permute-start.26 = (bf16[1,16,2176]{2,1,0:T(8,128)(2,1)S(1)}, bf16[1,16,2176]{2,1,0:T(8,128)(2,1)S(1)}, u32[]{:S(2)}, u32[]{:S(2)}) collective-permute-start(bf16[1,16,2176]{2,1,0:T(8,128)(2,1)S(1)} %get-tuple-element.186), channel_id=1, source_target_pairs={{0,24},{1,25},{2,26},{3,27},{4,28},{5,29},{6,30},{7,31},{8,16},{9,... | collective-permute-start | bytes 208904 | tf_op jit(solution)/shard_map/ppermute | solution.py:728
  141.3 2.8 %collective-permute-done.25.r1 = bf16[1,16,2176]{2,1,0:T(8,128)(2,1)S(1)} collective-permute-done((bf16[1,16,2176]{2,1,0:T(8,128)(2,1)S(1)}, bf16[1,16,2176]{2,1,0:T(8,128)(2,1)S(1)}, u32[]{:S(2)}, u32[]{:S(2)}) %collective-permute-start.25) | collective-permute-done | bytes 69664 | tf_op jit(solution)/shard_map/ppermute | solution.py:728
  145.7 1.9 %finish.1 = (f32[16,1536]{1,0:T(8,128)}, f32[16,512]{1,0:T(8,128)}, f32[16,2048]{1,0:T(8,128)}, f32[64,512]{1,0:T(8,128)}, f32[2,16]{1,0:T(2,128)}, /*index=5*/f...) custom-call(f32[1,16,2176]{2,1,0:T(8,128)} %copy-done.4, bf16[1,16,2176]{2,1,0:T(8,128)(2,1)} %copy-done.7, ...), custom_call_target="tpu_custom_call" | custom-call | flops 1650000000 | tf_op jit(solution)/shard_map/finish/pallas_call | solution.py:710
  (80 shorter events, 17.3 us)
Async XLA Ops:
  2.4 9.7 %collective-permute-start = (bf16[16,4224]{1,0:T(8,128)(2,1)}, bf16[16,4224]{1,0:T(8,128)(2,1)S(1)}, u32[]{:S(2)}, u32[]{:S(2)}) collective-permute-start(bf16[16,4224]{1,0:T(8,128)(2,1)} %get-tuple-element.115), channel_id=1, source_target_pairs={{0,8},{1,9},{2,10},{3,11},{4,12},{5,13},{6,14},{7,15},{8,0},{9,1},... | collective-permute-start | bytes 405512 | tf_op jit(solution)/shard_map/ppermute | solution.py:728
  5.4 13.4 %collective-permute-start.1 = (bf16[16,4224]{1,0:T(8,128)(2,1)}, bf16[16,4224]{1,0:T(8,128)(2,1)S(1)}, u32[]{:S(2)}, u32[]{:S(2)}) collective-permute-start(bf16[16,4224]{1,0:T(8,128)(2,1)} %get-tuple-element.115), channel_id=1, source_target_pairs={{0,16},{1,17},{2,18},{3,19},{4,20},{5,21},{6,22},{7,23},{8,24},{9,... | collective-permute-start | bytes 405512 | tf_op jit(solution)/shard_map/ppermute | solution.py:728
  8.0 10.8 %collective-permute-start.2 = (bf16[16,4224]{1,0:T(8,128)(2,1)}, bf16[16,4224]{1,0:T(8,128)(2,1)S(1)}, u32[]{:S(2)}, u32[]{:S(2)}) collective-permute-start(bf16[16,4224]{1,0:T(8,128)(2,1)} %get-tuple-element.115), channel_id=1, source_target_pairs={{0,24},{1,25},{2,26},{3,27},{4,28},{5,29},{6,30},{7,31},{8,16},{9,... | collective-permute-start | bytes 405512 | tf_op jit(solution)/shard_map/ppermute | solution.py:728
  8.0 10.9 %collective-permute-start.3 = (bf16[16,2048]{1,0:T(8,128)(2,1)}, bf16[16,2048]{1,0:T(8,128)(2,1)S(1)}, u32[]{:S(2)}, u32[]{:S(2)}) collective-permute-start(bf16[16,2048]{1,0:T(8,128)(2,1)} %get-tuple-element.109), channel_id=1, source_target_pairs={{0,2},{1,3},{2,0},{3,1},{4,6},{5,7},{6,4},{7,5},{8,10},{9,11},{10,... | collective-permute-start | bytes 196616 | tf_op jit(solution)/shard_map/ppermute | solution.py:728
  9.7 9.2 %collective-permute-start.4 = (bf16[16,2048]{1,0:T(8,128)(2,1)}, bf16[16,2048]{1,0:T(8,128)(2,1)S(1)}, u32[]{:S(2)}, u32[]{:S(2)}) collective-permute-start(bf16[16,2048]{1,0:T(8,128)(2,1)} %get-tuple-element.109), channel_id=1, source_target_pairs={{0,4},{1,5},{2,6},{3,7},{4,0},{5,1},{6,2},{7,3},{8,12},{9,13},{10,... | collective-permute-start | bytes 196616 | tf_op jit(solution)/shard_map/ppermute | solution.py:728
  12.1 6.9 %collective-permute-start.5 = (bf16[16,2048]{1,0:T(8,128)(2,1)}, bf16[16,2048]{1,0:T(8,128)(2,1)S(1)}, u32[]{:S(2)}, u32[]{:S(2)}) collective-permute-start(bf16[16,2048]{1,0:T(8,128)(2,1)} %get-tuple-element.109), channel_id=1, source_target_pairs={{0,6},{1,7},{2,4},{3,5},{4,2},{5,3},{6,0},{7,1},{8,14},{9,15},{10,... | collective-permute-start | bytes 196616 | tf_op jit(solution)/shard_map/ppermute | solution.py:728
  19.9 14.8 %collective-permute-start.6 = (bf16[4,16,2048]{2,1,0:T(8,128)(2,1)S(1)}, bf16[4,16,2048]{2,1,0:T(8,128)(2,1)S(1)}, u32[]{:S(2)}, u32[]{:S(2)}) collective-permute-start(bf16[4,16,2048]{2,1,0:T(8,128)(2,1)S(1)} %get-tuple-element.202), channel_id=1, source_target_pairs={{0,16},{1,17},{2,18},{3,19},{4,20},{5,21},{6,22},{7,23},{8,24},{9,... | collective-permute-start | bytes 786440 | tf_op jit(solution)/shard_map/ppermute | solution.py:728
  34.8 21.2 %collective-permute-start.10 = (bf16[4,16,2560]{2,1,0:T(8,128)(2,1)S(1)}, bf16[4,16,2560]{2,1,0:T(8,128)(2,1)S(1)}, u32[]{:S(2)}, u32[]{:S(2)}) collective-permute-start(bf16[4,16,2560]{2,1,0:T(8,128)(2,1)S(1)} %get-tuple-element.200), channel_id=1, source_target_pairs={{0,6},{1,7},{2,4},{3,5},{4,2},{5,3},{6,0},{7,1},{8,14},{9,15},{10,... | collective-permute-start | bytes 983048 | tf_op jit(solution)/shard_map/ppermute | solution.py:728
  36.6 19.5 %collective-permute-start.8 = (bf16[4,16,2560]{2,1,0:T(8,128)(2,1)S(1)}, bf16[4,16,2560]{2,1,0:T(8,128)(2,1)S(1)}, u32[]{:S(2)}, u32[]{:S(2)}) collective-permute-start(bf16[4,16,2560]{2,1,0:T(8,128)(2,1)S(1)} %get-tuple-element.200), channel_id=1, source_target_pairs={{0,2},{1,3},{2,0},{3,1},{4,6},{5,7},{6,4},{7,5},{8,10},{9,11},{10,... | collective-permute-start | bytes 983048 | tf_op jit(solution)/shard_map/ppermute | solution.py:728
  38.8 17.3 %collective-permute-start.9 = (bf16[4,16,2560]{2,1,0:T(8,128)(2,1)S(1)}, bf16[4,16,2560]{2,1,0:T(8,128)(2,1)S(1)}, u32[]{:S(2)}, u32[]{:S(2)}) collective-permute-start(bf16[4,16,2560]{2,1,0:T(8,128)(2,1)S(1)} %get-tuple-element.200), channel_id=1, source_target_pairs={{0,4},{1,5},{2,6},{3,7},{4,0},{5,1},{6,2},{7,3},{8,12},{9,13},{10,... | collective-permute-start | bytes 983048 | tf_op jit(solution)/shard_map/ppermute | solution.py:728
  38.8 17.3 %collective-permute-start.11 = (bf16[8,16,2048]{2,1,0:T(8,128)(2,1)S(1)}, bf16[8,16,2048]{2,1,0:T(8,128)(2,1)S(1)}, u32[]{:S(2)}, u32[]{:S(2)}) collective-permute-start(bf16[8,16,2048]{2,1,0:T(8,128)(2,1)S(1)} %bitcast.41), channel_id=1, source_target_pairs={{0,8},{1,9},{2,10},{3,11},{4,12},{5,13},{6,14},{7,15},{8,0},{9,1},... | collective-permute-start | bytes 1572872 | tf_op jit(solution)/shard_map/ppermute | solution.py:728
  56.3 4.6 %collective-permute-start.12 = (bf16[16,16,2560]{2,1,0:T(8,128)(2,1)S(1)}, bf16[16,16,2560]{2,1,0:T(8,128)(2,1)S(1)}, u32[]{:S(2)}, u32[]{:S(2)}) collective-permute-start(bf16[16,16,2560]{2,1,0:T(8,128)(2,1)S(1)} %bitcast.37), channel_id=1, source_target_pairs={{0,1},{1,0},{2,3},{3,2},{4,5},{5,4},{6,7},{7,6},{8,9},{9,8},{10,11... | collective-permute-start | bytes 3932168 | tf_op jit(solution)/shard_map/ppermute | solution.py:728
  77.7 5.9 %collective-permute-start.15 = (bf16[16,16,2048]{2,1,0:T(8,128)(2,1)S(1)}, bf16[16,16,2048]{2,1,0:T(8,128)(2,1)S(1)}, u32[]{:S(2)}, u32[]{:S(2)}) collective-permute-start(bf16[16,16,2048]{2,1,0:T(8,128)(2,1)S(1)} %get-tuple-element.134), channel_id=1, source_target_pairs={{0,1},{1,0},{2,3},{3,2},{4,5},{5,4},{6,7},{7,6},{8,9},{9,8},{10,11... | collective-permute-start | bytes 3145736 | tf_op jit(solution)/shard_map/ppermute | solution.py:728
  77.9 5.7 %collective-permute-start.14 = (bf16[16,16,2048]{2,1,0:T(8,128)(2,1)S(1)}, bf16[16,16,2048]{2,1,0:T(8,128)(2,1)S(1)}, u32[]{:S(2)}, u32[]{:S(2)}) collective-permute-start(bf16[16,16,2048]{2,1,0:T(8,128)(2,1)S(1)} %get-tuple-element.131), channel_id=1, source_target_pairs={{0,1},{1,0},{2,3},{3,2},{4,5},{5,4},{6,7},{7,6},{8,9},{9,8},{10,11... | collective-permute-start | bytes 3145736 | tf_op jit(solution)/shard_map/ppermute | solution.py:728
  84.0 30.5 %collective-permute-start.16 = (bf16[4,16,4096]{2,1,0:T(8,128)(2,1)S(1)}, bf16[4,16,4096]{2,1,0:T(8,128)(2,1)S(1)}, u32[]{:S(2)}, u32[]{:S(2)}) collective-permute-start(bf16[4,16,4096]{2,1,0:T(8,128)(2,1)S(1)} %get-tuple-element.143), channel_id=1, source_target_pairs={{0,2},{1,3},{2,0},{3,1},{4,6},{5,7},{6,4},{7,5},{8,10},{9,11},{10,... | collective-permute-start | bytes 1572872 | tf_op jit(solution)/shard_map/ppermute | solution.py:728
  86.0 28.5 %collective-permute-start.17 = (bf16[4,16,4096]{2,1,0:T(8,128)(2,1)S(1)}, bf16[4,16,4096]{2,1,0:T(8,128)(2,1)S(1)}, u32[]{:S(2)}, u32[]{:S(2)}) collective-permute-start(bf16[4,16,4096]{2,1,0:T(8,128)(2,1)S(1)} %get-tuple-element.144), channel_id=1, source_target_pairs={{0,4},{1,5},{2,6},{3,7},{4,0},{5,1},{6,2},{7,3},{8,12},{9,13},{10,... | collective-permute-start | bytes 1572872 | tf_op jit(solution)/shard_map/ppermute | solution.py:728
  86.1 28.4 %collective-permute-start.18 = (bf16[4,16,4096]{2,1,0:T(8,128)(2,1)S(1)}, bf16[4,16,4096]{2,1,0:T(8,128)(2,1)S(1)}, u32[]{:S(2)}, u32[]{:S(2)}) collective-permute-start(bf16[4,16,4096]{2,1,0:T(8,128)(2,1)S(1)} %get-tuple-element.145), channel_id=1, source_target_pairs={{0,6},{1,7},{2,4},{3,5},{4,2},{5,3},{6,0},{7,1},{8,14},{9,15},{10,... | collective-permute-start | bytes 1572872 | tf_op jit(solution)/shard_map/ppermute | solution.py:728
  114.8 15.3 %collective-permute-start.23 = (bf16[2,16,4096]{2,1,0:T(8,128)(2,1)S(1)}, bf16[2,16,4096]{2,1,0:T(8,128)(2,1)S(1)}, u32[]{:S(2)}, u32[]{:S(2)}) collective-permute-start(bf16[2,16,4096]{2,1,0:T(8,128)(2,1)S(1)} %get-tuple-element.177), channel_id=1, source_target_pairs={{0,16},{1,17},{2,18},{3,19},{4,20},{5,21},{6,22},{7,23},{8,24},{9,... | collective-permute-start | bytes 786440 | tf_op jit(solution)/shard_map/ppermute | solution.py:728
  117.5 12.5 %collective-permute-start.20 = (bf16[4,16,2176]{2,1,0:T(8,128)(2,1)S(1)}, bf16[4,16,2176]{2,1,0:T(8,128)(2,1)S(1)}, u32[]{:S(2)}, u32[]{:S(2)}) collective-permute-start(bf16[4,16,2176]{2,1,0:T(8,128)(2,1)S(1)} %get-tuple-element.174), channel_id=1, source_target_pairs={{0,2},{1,3},{2,0},{3,1},{4,6},{5,7},{6,4},{7,5},{8,10},{9,11},{10,... | collective-permute-start | bytes 835592 | tf_op jit(solution)/shard_map/ppermute | solution.py:728
  119.5 14.4 %collective-permute-start.21 = (bf16[4,16,2176]{2,1,0:T(8,128)(2,1)S(1)}, bf16[4,16,2176]{2,1,0:T(8,128)(2,1)S(1)}, u32[]{:S(2)}, u32[]{:S(2)}) collective-permute-start(bf16[4,16,2176]{2,1,0:T(8,128)(2,1)S(1)} %get-tuple-element.175), channel_id=1, source_target_pairs={{0,4},{1,5},{2,6},{3,7},{4,0},{5,1},{6,2},{7,3},{8,12},{9,13},{10,... | collective-permute-start | bytes 835592 | tf_op jit(solution)/shard_map/ppermute | solution.py:728
  119.6 14.3 %collective-permute-start.22 = (bf16[4,16,2176]{2,1,0:T(8,128)(2,1)S(1)}, bf16[4,16,2176]{2,1,0:T(8,128)(2,1)S(1)}, u32[]{:S(2)}, u32[]{:S(2)}) collective-permute-start(bf16[4,16,2176]{2,1,0:T(8,128)(2,1)S(1)} %get-tuple-element.176), channel_id=1, source_target_pairs={{0,6},{1,7},{2,4},{3,5},{4,2},{5,3},{6,0},{7,1},{8,14},{9,15},{10,... | collective-permute-start | bytes 835592 | tf_op jit(solution)/shard_map/ppermute | solution.py:728
  134.0 11.0 %collective-permute-start.27 = (bf16[1,16,4096]{2,1,0:T(8,128)(2,1)S(1)}, bf16[1,16,4096]{2,1,0:T(8,128)(2,1)S(1)}, u32[]{:S(2)}, u32[]{:S(2)}) collective-permute-start(bf16[1,16,4096]{2,1,0:T(8,128)(2,1)S(1)} %get-tuple-element.189), channel_id=1, source_target_pairs={{0,8},{1,9},{2,10},{3,11},{4,12},{5,13},{6,14},{7,15},{8,0},{9,1},... | collective-permute-start | bytes 393224 | tf_op jit(solution)/shard_map/ppermute | solution.py:728
  137.4 6.8 %collective-permute-start.25 = (bf16[1,16,2176]{2,1,0:T(8,128)(2,1)S(1)}, bf16[1,16,2176]{2,1,0:T(8,128)(2,1)S(1)}, u32[]{:S(2)}, u32[]{:S(2)}) collective-permute-start(bf16[1,16,2176]{2,1,0:T(8,128)(2,1)S(1)} %get-tuple-element.185), channel_id=1, source_target_pairs={{0,16},{1,17},{2,18},{3,19},{4,20},{5,21},{6,22},{7,23},{8,24},{9,... | collective-permute-start | bytes 208904 | tf_op jit(solution)/shard_map/ppermute | solution.py:728
  138.8 6.2 %collective-permute-start.26 = (bf16[1,16,2176]{2,1,0:T(8,128)(2,1)S(1)}, bf16[1,16,2176]{2,1,0:T(8,128)(2,1)S(1)}, u32[]{:S(2)}, u32[]{:S(2)}) collective-permute-start(bf16[1,16,2176]{2,1,0:T(8,128)(2,1)S(1)} %get-tuple-element.186), channel_id=1, source_target_pairs={{0,24},{1,25},{2,26},{3,27},{4,28},{5,29},{6,30},{7,31},{8,16},{9,... | collective-permute-start | bytes 208904 | tf_op jit(solution)/shard_map/ppermute | solution.py:728
  (14 other events, 60.9 us)
where the time goes:
time: 148 us
  Pallas kernels  77.1 us (52%)
  starting transfers between devices  34.4 us (23%)
  waiting for transfers between devices  19.9 us (13%)
  blocking collectives  11.6 us (8%)
  local copies, waits for them, and re-layouts  2.19 us (1%)
    ppermute x28, starting transfers between devices, swap(): return lax.ppermute(value, AXES, [(d, d ^ mask) for d in range(count)])  34.4 us
    pallas_call x1, Pallas kernels, backward(): pl.pallas_call(backward_kernel, grid=(4,), in_specs=[smem()] + parts + [p...  26.9 us
    ppermute x28, waiting for transfers between devices, swap(): return lax.ppermute(value, AXES, [(d, d ^ mask) for d in range(count)])  19.9 us
    pallas_call x1, Pallas kernels, forward(): pl.pallas_call(forward_kernel, in_specs=[smem()] + [vmem()] * 4, out_spec...  17.1 us
    pallas_call x1, Pallas kernels, feed_first(): pl.pallas_call(feed_first_kernel, in_specs=[smem()] + [vmem()] * 9, out_s...  12.8 us
    all_gather x1, blocking collectives, body(): a_mine = lax.all_gather(after(a_col, c_plane), 'plane').reshape(16, 16, -1)  11.6 us
    pallas_call x1, Pallas kernels, input_terms(): pl.pallas_call(input_kernel, in_specs=[vmem()] * 8, out_specs=[vmem()] *...  6.4 us
    pallas_call x1, Pallas kernels, feed_third(): pl.pallas_call(feed_third_kernel, in_specs=[vmem()] * 7, out_specs=[vmem(...  5.34 us
  transfers between devices with their start and end apart: 28, of which 7 were waited for; matrix products, arithmetic and copies ran while one was open for 1% of the time, Pallas kernels for 38%

commit v1 on v0

--- a/solution.py
+++ b/solution.py
@@ -682,12 +682,42 @@
     return first, rest
 
 
+def last_kernel(g_own, g0, g1, g2, du_own, du_recv, own, du_first, p0, p1, p2):
+    width = g_own.shape[2]
+    for index in range(4):
+        total = g_own[index]
+        for ref in (g0, g1, g2):
+            total = total + ref[index].astype(F32)
+        if index == 0:
+            own[0] = total
+        else:
+            (p0, p1, p2)[index - 1][0, :, 0:width] = total.astype(BF)
+    du_first[0] = du_own[0] + du_recv[0].astype(F32)
+    p0[0, :, width:] = (du_own[1] + du_recv[1].astype(F32)).astype(BF)
+
+
+def last_sums(g_own, g_recv, du_own, du_recv):
+    width, wide = g_own.shape[2], du_own.shape[2]
+    own, du_first, *parts = pl.pallas_call(
+        last_kernel,
+        in_specs=[vmem()] * 6,
+        out_specs=[vmem()] * 5,
+        out_shape=[shape((1, 16, width), F32), shape((1, 16, wide), F32)]
+        + [shape((1, 16, width + wide), BF)]
+        + [shape((1, 16, width), BF)] * 2,
+        compiler_params=pltpu.CompilerParams(vmem_limit_bytes=8 * MIB),
+        cost_estimate=cost(1.5),
+        name="last_sums",
+    )(g_own, *g_recv, du_own, du_recv)
+    return own, du_first, parts
+
+
 def finish_kernel(
-    own, r0, r1, r2, du_own, du_recv,
+    own, r0, r1, r2, du_own,
     qkv_grad, mix_grad, up_grad, down_grad, gain, shift, qv, proj, bias,
 ):
-    total = own[0]
-    for ref in (r0, r1, r2):
+    total = own[0] + r0[0, :, 0:2176].astype(F32)
+    for ref in (r1, r2):
         total = total + ref[0].astype(F32)
     mix_grad[...] = total[:, 1536:2048]
     for pair in range(4):
@@ -700,16 +730,16 @@
     for index, ref in enumerate((gain, shift, qv, proj)):
         ref[...] = wide[2 * index : 2 * index + 2, 0:16]
     bias[...] = tile[0:1, 64:128]
-    total = du_own[0] + du_recv[0].astype(F32)
+    total = du_own[0] + r0[0, :, 2176:].astype(F32)
     for part in range(4):
         down_grad[16 * part : 16 * part + 16, :] = total[:, 512 * part : 512 * part + 512]
     up_grad[...] = total[:, 2048:4096]
 
 
-def finish(own, received, du_own, du_recv):
+def finish(own, received, du_own):
     return pl.pallas_call(
         finish_kernel,
-        in_specs=[vmem()] * 6,
+        in_specs=[vmem()] * 5,
         out_specs=[vmem()] * 9,
         out_shape=[
             shape((16, 1536), F32),
@@ -719,9 +749,10 @@
         ]
         + [shape((2, 16), F32)] * 4
         + [shape((1, 64), F32)],
+        compiler_params=pltpu.CompilerParams(vmem_limit_bytes=6 * MIB),
         cost_estimate=cost(1.5),
         name="finish",
-    )(own, *received, du_own, *du_recv)
+    )(own, *received, du_own)
 
 
 def swap(value, mask, count):
@@ -857,13 +888,9 @@
     )
     if cubic:
         g_recv, du_recv, input_grad = point((g_recv, du_recv, input_grad))
-        own, parts = combine("last_sum_two", 4, (g_own, g_recv))
+        own, du_own, parts = last_sums(g_own, g_recv, du_own, *du_recv)
         g_recv = exchange(parts, Z_MASKS, count)
-        du_own, du_parts = combine("feed_sum_three", 2, (du_own, du_recv))
-        du_recv = exchange(du_parts, (8,), count)
-        qkv_grad, mix_grad, up_grad, down_grad, *vectors, bias_grad = finish(
-            own, g_recv, du_own, du_recv
-        )
+        qkv_grad, mix_grad, up_grad, down_grad, *vectors, bias_grad = finish(own, g_recv, du_own)
         return (
             output, input_grad, qkv_grad, mix_grad, up_grad, down_grad, *vectors,
             bias_grad.reshape(64),

time: 148 us -> 146 us (0.986)
  waiting for transfers between devices: 19.9 us -> 22.1 us
  starting transfers between devices: 34.4 us -> 32.5 us
    ppermute x28 -> x27, waiting for transfers between devices: 19.9 us -> 22.1 us  [swap(): return lax.ppermute(value, AXES, [(d, d ^ mask) for d in range(count)])]
    ppermute x28 -> x27, starting transfers between devices: 34.4 us -> 32.5 us  [swap(): return lax.ppermute(value, AXES, [(d, d ^ mask) for d in range(count)])]
  transfers between devices with their start and end apart: 28 -> 27, of which waited for: 7 -> 7; matrix products, arithmetic and copies ran while one was open for 1% -> 1% of each run, Pallas kernels for 38% -> 39%
where the time goes in v1:
time: 146 us; the launch traced here: 145 us
  Pallas kernels  76 us (52%)
  starting transfers between devices  32.5 us (22%)
  waiting for transfers between devices  22.1 us (15%)
  blocking collectives  11.6 us (8%)
    ppermute x27, starting transfers between devices, swap(): return lax.ppermute(value, AXES, [(d, d ^ mask) for d in range(count)])  32.5 us
    pallas_call x1, Pallas kernels, backward(): pl.pallas_call(backward_kernel, grid=(4,), in_specs=[smem()] + parts + [p...  26.9 us
    ppermute x27, waiting for transfers between devices, swap(): return lax.ppermute(value, AXES, [(d, d ^ mask) for d in range(count)])  22.1 us
    pallas_call x1, Pallas kernels, forward(): pl.pallas_call(forward_kernel, in_specs=[smem()] + [vmem()] * 4, out_spec...  17.1 us
    pallas_call x1, Pallas kernels, feed_first(): pl.pallas_call(feed_first_kernel, in_specs=[smem()] + [vmem()] * 9, out_s...  12.8 us
    all_gather x1, blocking collectives, body(): a_mine = lax.all_gather(after(a_col, c_plane), 'plane').reshape(16, 16, -1)  11.6 us
    pallas_call x1, Pallas kernels, input_terms(): pl.pallas_call(input_kernel, in_specs=[vmem()] * 8, out_specs=[vmem()] *...  6.4 us
    pallas_call x1, Pallas kernels, feed_third(): pl.pallas_call(feed_third_kernel, in_specs=[vmem()] * 7, out_specs=[vmem(...  5.34 us
  transfers between devices with their start and end apart: 27, of which 7 were waited for; matrix products, arithmetic and copies ran while one was open for 1% of the time, Pallas kernels for 39%

profile of v1, /device:TPU:0, one launch (start us, length us, event | category | flops | bytes accessed | tf_op | source)
XLA Modules:
  0.0 145.3 jit_solution(15321276768305727160)
XLA Ops:
  0.6 1.8 %pack.1 = (bf16[16,4224]{1,0:T(8,128)(2,1)}, bf16[16,2048]{1,0:T(8,128)(2,1)}) custom-call(bf16[16,1536]{1,0:T(8,128)(2,1)} %qkv.1, bf16[16,512]{1,0:T(8,128)(2,1)} %mix.1, bf16[16,2048]{1,0:T(8,128)(2,1)} %up.1, bf16[64,512]{1,0:T(8,128)(2,1)} %down.1, bf16[2,16]{1,0:T(2,128)(2,1)} %gain.1, bf16[2,16]{1,0:T(2,128)(2,1)} %shift.1, bf16[2,16]{1,0:T(2,128)(2,1)} %qv.1, ...), custom_call_target="tpu_custom_call" | custom-call | flops 1650000000 | tf_op jit(solution)/shard_map/pack/pallas_call | solution.py:98
  2.4 3.0 %collective-permute-start = (bf16[16,4224]{1,0:T(8,128)(2,1)}, bf16[16,4224]{1,0:T(8,128)(2,1)S(1)}, u32[]{:S(2)}, u32[]{:S(2)}) collective-permute-start(bf16[16,4224]{1,0:T(8,128)(2,1)} %get-tuple-element.114), channel_id=1, source_target_pairs={{0,8},{1,9},{2,10},{3,11},{4,12},{5,13},{6,14},{7,15},{8,0},{9,1},... | collective-permute-start | bytes 405512 | tf_op jit(solution)/shard_map/ppermute | solution.py:759
  5.4 2.6 %collective-permute-start.1 = (bf16[16,4224]{1,0:T(8,128)(2,1)}, bf16[16,4224]{1,0:T(8,128)(2,1)S(1)}, u32[]{:S(2)}, u32[]{:S(2)}) collective-permute-start(bf16[16,4224]{1,0:T(8,128)(2,1)} %get-tuple-element.114), channel_id=1, source_target_pairs={{0,16},{1,17},{2,18},{3,19},{4,20},{5,21},{6,22},{7,23},{8,24},{9,... | collective-permute-start | bytes 405512 | tf_op jit(solution)/shard_map/ppermute | solution.py:759
  13.6 5.3 %collective-permute-done.1 = bf16[16,4224]{1,0:T(8,128)(2,1)S(1)} collective-permute-done((bf16[16,4224]{1,0:T(8,128)(2,1)}, bf16[16,4224]{1,0:T(8,128)(2,1)S(1)}, u32[]{:S(2)}, u32[]{:S(2)}) %collective-permute-start.1) | collective-permute-done | bytes 135200 | tf_op jit(solution)/shard_map/ppermute | solution.py:759
  19.9 3.1 %collective-permute-start.6 = (bf16[4,16,2048]{2,1,0:T(8,128)(2,1)S(1)}, bf16[4,16,2048]{2,1,0:T(8,128)(2,1)S(1)}, u32[]{:S(2)}, u32[]{:S(2)}) collective-permute-start(bf16[4,16,2048]{2,1,0:T(8,128)(2,1)S(1)} %get-tuple-element.200), channel_id=1, source_target_pairs={{0,16},{1,17},{2,18},{3,19},{4,20},{5,21},{6,22},{7,23},{8,24},{9,... | collective-permute-start | bytes 786440 | tf_op jit(solution)/shard_map/ppermute | solution.py:759
  23.0 11.6 %all-gather.mine = bf16[16,16,1664]{2,1,0:T(8,128)(2,1)S(1)} all-gather(bf16[4,16,1664]{2,1,0:T(8,128)(2,1)S(1)} %pad_maximum_fusion.5), channel_id=2, replica_groups=mesh['dp'=4,'plane'=4,'core'=2] {'plane'}, dimensions={0}, use_global_device_ids=true | all-gather | bytes 1064960 | tf_op jit(solution)/shard_map/all_gather | solution.py:826
  34.8 1.7 %collective-permute-start.10 = (bf16[4,16,2560]{2,1,0:T(8,128)(2,1)S(1)}, bf16[4,16,2560]{2,1,0:T(8,128)(2,1)S(1)}, u32[]{:S(2)}, u32[]{:S(2)}) collective-permute-start(bf16[4,16,2560]{2,1,0:T(8,128)(2,1)S(1)} %get-tuple-element.198), channel_id=1, source_target_pairs={{0,6},{1,7},{2,4},{3,5},{4,2},{5,3},{6,0},{7,1},{8,14},{9,15},{10,... | collective-permute-start | bytes 983048 | tf_op jit(solution)/shard_map/ppermute | solution.py:759
  36.6 2.2 %collective-permute-start.8 = (bf16[4,16,2560]{2,1,0:T(8,128)(2,1)S(1)}, bf16[4,16,2560]{2,1,0:T(8,128)(2,1)S(1)}, u32[]{:S(2)}, u32[]{:S(2)}) collective-permute-start(bf16[4,16,2560]{2,1,0:T(8,128)(2,1)S(1)} %get-tuple-element.198), channel_id=1, source_target_pairs={{0,2},{1,3},{2,0},{3,1},{4,6},{5,7},{6,4},{7,5},{8,10},{9,11},{10,... | collective-permute-start | bytes 983048 | tf_op jit(solution)/shard_map/ppermute | solution.py:759
  39.0 17.1 %attend.1 = (bf16[4,3,1024,128]{3,2,1,0:T(8,128)(2,1)S(1)}, bf16[528,1024]{1,0:T(8,128)(2,1)S(1)}, bf16[512,1536]{1,0:T(8,128)(2,1)S(1)}, bf16[1024,512]{1,0:T(8...) custom-call(s32[2]{0:T(128)S(1)} %pad_add_fusion.me_ref, ...), custom_call_target="tpu_custom_call" | custom-call | flops 16499999744 | tf_op jit(solution)/shard_map/attend/pallas_call | solution.py:225
  57.0 3.9 %collective-permute-done.13.other_tall = bf16[16,16,2048]{2,1,0:T(8,128)(2,1)S(1)} collective-permute-done((bf16[16,16,2048]{2,1,0:T(8,128)(2,1)S(1)}, bf16[16,16,2048]{2,1,0:T(8,128)(2,1)S(1)}, u32[]{:S(2)}, u32[]{:S(2)}) %collective-permute-start.13) | collective-permute-done | bytes 1048608 | tf_op jit(solution)/shard_map/ppermute | solution.py:759
  60.9 12.8 %feed_first.1 = (f32[1024,512]{1,0:T(8,128)S(1)}, bf16[528,1024]{1,0:T(8,128)(2,1)S(1)}, bf16[1024,2048]{1,0:T(8,128)(2,1)S(1)}, bf16[16,16,2048]{2,1,0:T(8,128)...) custom-call(s32[2]{0:T(128)S(1)} %pad_add_fusion.me_ref, ...), custom_call_target="tpu_custom_call" | custom-call | flops 19800000512 | tf_op jit(solution)/shard_map/feed_first/pallas_call | solution.py:338
  73.7 4.0 %feed_second.1 = (bf16[16,16,2048]{2,1,0:T(8,128)(2,1)S(1)}, f32[16,16,2048]{2,1,0:T(8,128)S(1)}, f32[1,2048]{1,0:T(1,128)S(1)}) custom-call(s32[2]{0:T(128)S(1)} %pad_add_fusion.me_ref, bf16[528,1024]{1,0:T(8,128)(2,1)S(1)} %get-tuple-element.131.normed_t, bf16[1024,2048]{1,0:T(8,128)(2,1)S(1)} %get-tuple-element.132.grad_pre), custom_call_target="tpu_custom_call" | custom-call | flops 5500000256 | tf_op jit(solution)/shard_map/feed_second/pallas_call | solution.py:378
  78.2 5.3 %feed_third.1 = (f32[1024,512]{1,0:T(8,128)S(1)}, bf16[1024,512]{1,0:T(8,128)(2,1)S(1)}, f32[512,512]{1,0:T(8,128)S(1)}, f32[8,512]{1,0:T(8,128)S(1)}) custom-call(f32[1024,512]{1,0:T(8,128)S(1)} %get-tuple-element.134.middle, bf16[1024,2048]{1,0:T(8,128)(2,1)S(1)} %get-tuple-element.132.grad_pre, bf16[512,512]{1,0:T(8,128)(2,1)S(1)} %get-tuple-element.135.mix, ...), custom_call_target="tpu_custom_call" | custom-call | flops 8800000000 | tf_op jit(solution)/shard_map/feed_third/pallas_call | solution.py:436
  84.0 2.0 %collective-permute-start.16 = (bf16[4,16,4096]{2,1,0:T(8,128)(2,1)S(1)}, bf16[4,16,4096]{2,1,0:T(8,128)(2,1)S(1)}, u32[]{:S(2)}, u32[]{:S(2)}) collective-permute-start(bf16[4,16,4096]{2,1,0:T(8,128)(2,1)S(1)} %get-tuple-element.142), channel_id=1, source_target_pairs={{0,2},{1,3},{2,0},{3,1},{4,6},{5,7},{6,4},{7,5},{8,10},{9,11},{10,... | collective-permute-start | bytes 1572872 | tf_op jit(solution)/shard_map/ppermute | solution.py:759
  87.5 26.9 %attend_back.1 = (bf16[1024,1536]{1,0:T(8,128)(2,1)S(1)}, bf16[16,16,2176]{2,1,0:T(8,128)(2,1)S(1)}, f32[16,16,2176]{2,1,0:T(8,128)S(1)}) custom-call(s32[2]{0:T(128)S(1)} %pad_add_fusion.me_ref, bf16[4,3,1024,128]{3,2,1,0:T(8,128)(2,1)S(1)} %get-tuple-element.145.q.k.v, bf16[4,3,1024,128]{3,2,1,0:T(8,128)(2,1)S(1)} %get-tuple-element.145.q.k.v, ...), custom_call_target="tpu_custom_call" | custom-call | flops 27499999232 | tf_op jit(solution)/shard_map/attend_back/pallas_call | solution.py:578
  114.8 2.0 %collective-permute-start.23 = (bf16[2,16,4096]{2,1,0:T(8,128)(2,1)S(1)}, bf16[2,16,4096]{2,1,0:T(8,128)(2,1)S(1)}, u32[]{:S(2)}, u32[]{:S(2)}) collective-permute-start(bf16[2,16,4096]{2,1,0:T(8,128)(2,1)S(1)} %get-tuple-element.176), channel_id=1, source_target_pairs={{0,16},{1,17},{2,18},{3,19},{4,20},{5,21},{6,22},{7,23},{8,24},{9,... | collective-permute-start | bytes 786440 | tf_op jit(solution)/shard_map/ppermute | solution.py:759
  117.5 2.0 %collective-permute-start.20 = (bf16[4,16,2176]{2,1,0:T(8,128)(2,1)S(1)}, bf16[4,16,2176]{2,1,0:T(8,128)(2,1)S(1)}, u32[]{:S(2)}, u32[]{:S(2)}) collective-permute-start(bf16[4,16,2176]{2,1,0:T(8,128)(2,1)S(1)} %get-tuple-element.173), channel_id=1, source_target_pairs={{0,2},{1,3},{2,0},{3,1},{4,6},{5,7},{6,4},{7,5},{8,10},{9,11},{10,... | collective-permute-start | bytes 835592 | tf_op jit(solution)/shard_map/ppermute | solution.py:759
  121.1 6.4 %input_terms.1 = (f32[1024,512]{1,0:T(8,128)}, bf16[1024,512]{1,0:T(8,128)(2,1)}) custom-call(bf16[1024,512]{1,0:T(8,128)(2,1)S(1)} %copy-done.1, bf16[1024,1536]{1,0:T(8,128)(2,1)S(1)} %get-tuple-element.159.gm, bf16[512,1536]{1,0:T(8,128)(2,1)S(1)} %get-tuple-element.150.weight, f32[8,512]{1,0:T(8,128)S(1)} %get-tuple-element.168.smalls, ...), custom_call_target="tpu_custom_call" | custom-call | flops 8800000000 | tf_op jit(solution)/shard_map/input_terms/pallas_call | solution.py:638
  127.5 2.6 %collective-permute-done.23.du_recv = bf16[2,16,4096]{2,1,0:T(8,128)(2,1)S(1)} collective-permute-done((bf16[2,16,4096]{2,1,0:T(8,128)(2,1)S(1)}, bf16[2,16,4096]{2,1,0:T(8,128)(2,1)S(1)}, u32[]{:S(2)}, u32[]{:S(2)}) %collective-permute-start.23) | collective-permute-done | bytes 262176 | tf_op jit(solution)/shard_map/ppermute | solution.py:759
  130.1 3.9 %collective-permute-done.21.g1 = bf16[4,16,2176]{2,1,0:T(8,128)(2,1)S(1)} collective-permute-done((bf16[4,16,2176]{2,1,0:T(8,128)(2,1)S(1)}, bf16[4,16,2176]{2,1,0:T(8,128)(2,1)S(1)}, u32[]{:S(2)}, u32[]{:S(2)}) %collective-permute-start.21) | collective-permute-done | bytes 278560 | tf_op jit(solution)/shard_map/ppermute | solution.py:759
  134.1 2.1 %collective-permute-start.24 = (bf16[1,16,6272]{2,1,0:T(8,128)(2,1)S(1)}, bf16[1,16,6272]{2,1,0:T(8,128)(2,1)S(1)}, u32[]{:S(2)}, u32[]{:S(2)}) collective-permute-start(bf16[1,16,6272]{2,1,0:T(8,128)(2,1)S(1)} %get-tuple-element.184), channel_id=1, source_target_pairs={{0,8},{1,9},{2,10},{3,11},{4,12},{5,13},{6,14},{7,15},{8,0},{9,1},... | collective-permute-start | bytes 602120 | tf_op jit(solution)/shard_map/ppermute | solution.py:759
  136.7 1.9 %collective-permute-start.26 = (bf16[1,16,2176]{2,1,0:T(8,128)(2,1)S(1)}, bf16[1,16,2176]{2,1,0:T(8,128)(2,1)S(1)}, u32[]{:S(2)}, u32[]{:S(2)}) collective-permute-start(bf16[1,16,2176]{2,1,0:T(8,128)(2,1)S(1)} %get-tuple-element.186), channel_id=1, source_target_pairs={{0,24},{1,25},{2,26},{3,27},{4,28},{5,29},{6,30},{7,31},{8,16},{9,... | collective-permute-start | bytes 208904 | tf_op jit(solution)/shard_map/ppermute | solution.py:759
  138.6 3.5 %collective-permute-done.25.r1 = bf16[1,16,2176]{2,1,0:T(8,128)(2,1)S(1)} collective-permute-done((bf16[1,16,2176]{2,1,0:T(8,128)(2,1)S(1)}, bf16[1,16,2176]{2,1,0:T(8,128)(2,1)S(1)}, u32[]{:S(2)}, u32[]{:S(2)}) %collective-permute-start.25) | collective-permute-done | bytes 69664 | tf_op jit(solution)/shard_map/ppermute | solution.py:759
  142.2 2.4 %collective-permute-done.26.r2 = bf16[1,16,2176]{2,1,0:T(8,128)(2,1)S(1)} collective-permute-done((bf16[1,16,2176]{2,1,0:T(8,128)(2,1)S(1)}, bf16[1,16,2176]{2,1,0:T(8,128)(2,1)S(1)}, u32[]{:S(2)}, u32[]{:S(2)}) %collective-permute-start.26) | collective-permute-done | bytes 69664 | tf_op jit(solution)/shard_map/ppermute | solution.py:759
  (65 shorter events, 14.5 us)
Async XLA Ops:
  2.4 9.7 %collective-permute-start = (bf16[16,4224]{1,0:T(8,128)(2,1)}, bf16[16,4224]{1,0:T(8,128)(2,1)S(1)}, u32[]{:S(2)}, u32[]{:S(2)}) collective-permute-start(bf16[16,4224]{1,0:T(8,128)(2,1)} %get-tuple-element.114), channel_id=1, source_target_pairs={{0,8},{1,9},{2,10},{3,11},{4,12},{5,13},{6,14},{7,15},{8,0},{9,1},... | collective-permute-start | bytes 405512 | tf_op jit(solution)/shard_map/ppermute | solution.py:759
  5.4 13.4 %collective-permute-start.1 = (bf16[16,4224]{1,0:T(8,128)(2,1)}, bf16[16,4224]{1,0:T(8,128)(2,1)S(1)}, u32[]{:S(2)}, u32[]{:S(2)}) collective-permute-start(bf16[16,4224]{1,0:T(8,128)(2,1)} %get-tuple-element.114), channel_id=1, source_target_pairs={{0,16},{1,17},{2,18},{3,19},{4,20},{5,21},{6,22},{7,23},{8,24},{9,... | collective-permute-start | bytes 405512 | tf_op jit(solution)/shard_map/ppermute | solution.py:759
  8.0 10.8 %collective-permute-start.2 = (bf16[16,4224]{1,0:T(8,128)(2,1)}, bf16[16,4224]{1,0:T(8,128)(2,1)S(1)}, u32[]{:S(2)}, u32[]{:S(2)}) collective-permute-start(bf16[16,4224]{1,0:T(8,128)(2,1)} %get-tuple-element.114), channel_id=1, source_target_pairs={{0,24},{1,25},{2,26},{3,27},{4,28},{5,29},{6,30},{7,31},{8,16},{9,... | collective-permute-start | bytes 405512 | tf_op jit(solution)/shard_map/ppermute | solution.py:759
  8.0 10.9 %collective-permute-start.3 = (bf16[16,2048]{1,0:T(8,128)(2,1)}, bf16[16,2048]{1,0:T(8,128)(2,1)S(1)}, u32[]{:S(2)}, u32[]{:S(2)}) collective-permute-start(bf16[16,2048]{1,0:T(8,128)(2,1)} %get-tuple-element.108), channel_id=1, source_target_pairs={{0,2},{1,3},{2,0},{3,1},{4,6},{5,7},{6,4},{7,5},{8,10},{9,11},{10,... | collective-permute-start | bytes 196616 | tf_op jit(solution)/shard_map/ppermute | solution.py:759
  9.7 9.2 %collective-permute-start.4 = (bf16[16,2048]{1,0:T(8,128)(2,1)}, bf16[16,2048]{1,0:T(8,128)(2,1)S(1)}, u32[]{:S(2)}, u32[]{:S(2)}) collective-permute-start(bf16[16,2048]{1,0:T(8,128)(2,1)} %get-tuple-element.108), channel_id=1, source_target_pairs={{0,4},{1,5},{2,6},{3,7},{4,0},{5,1},{6,2},{7,3},{8,12},{9,13},{10,... | collective-permute-start | bytes 196616 | tf_op jit(solution)/shard_map/ppermute | solution.py:759
  12.1 6.9 %collective-permute-start.5 = (bf16[16,2048]{1,0:T(8,128)(2,1)}, bf16[16,2048]{1,0:T(8,128)(2,1)S(1)}, u32[]{:S(2)}, u32[]{:S(2)}) collective-permute-start(bf16[16,2048]{1,0:T(8,128)(2,1)} %get-tuple-element.108), channel_id=1, source_target_pairs={{0,6},{1,7},{2,4},{3,5},{4,2},{5,3},{6,0},{7,1},{8,14},{9,15},{10,... | collective-permute-start | bytes 196616 | tf_op jit(solution)/shard_map/ppermute | solution.py:759
  19.9 14.8 %collective-permute-start.6 = (bf16[4,16,2048]{2,1,0:T(8,128)(2,1)S(1)}, bf16[4,16,2048]{2,1,0:T(8,128)(2,1)S(1)}, u32[]{:S(2)}, u32[]{:S(2)}) collective-permute-start(bf16[4,16,2048]{2,1,0:T(8,128)(2,1)S(1)} %get-tuple-element.200), channel_id=1, source_target_pairs={{0,16},{1,17},{2,18},{3,19},{4,20},{5,21},{6,22},{7,23},{8,24},{9,... | collective-permute-start | bytes 786440 | tf_op jit(solution)/shard_map/ppermute | solution.py:759
  34.8 21.2 %collective-permute-start.10 = (bf16[4,16,2560]{2,1,0:T(8,128)(2,1)S(1)}, bf16[4,16,2560]{2,1,0:T(8,128)(2,1)S(1)}, u32[]{:S(2)}, u32[]{:S(2)}) collective-permute-start(bf16[4,16,2560]{2,1,0:T(8,128)(2,1)S(1)} %get-tuple-element.198), channel_id=1, source_target_pairs={{0,6},{1,7},{2,4},{3,5},{4,2},{5,3},{6,0},{7,1},{8,14},{9,15},{10,... | collective-permute-start | bytes 983048 | tf_op jit(solution)/shard_map/ppermute | solution.py:759
  36.6 19.5 %collective-permute-start.8 = (bf16[4,16,2560]{2,1,0:T(8,128)(2,1)S(1)}, bf16[4,16,2560]{2,1,0:T(8,128)(2,1)S(1)}, u32[]{:S(2)}, u32[]{:S(2)}) collective-permute-start(bf16[4,16,2560]{2,1,0:T(8,128)(2,1)S(1)} %get-tuple-element.198), channel_id=1, source_target_pairs={{0,2},{1,3},{2,0},{3,1},{4,6},{5,7},{6,4},{7,5},{8,10},{9,11},{10,... | collective-permute-start | bytes 983048 | tf_op jit(solution)/shard_map/ppermute | solution.py:759
  38.8 17.3 %collective-permute-start.9 = (bf16[4,16,2560]{2,1,0:T(8,128)(2,1)S(1)}, bf16[4,16,2560]{2,1,0:T(8,128)(2,1)S(1)}, u32[]{:S(2)}, u32[]{:S(2)}) collective-permute-start(bf16[4,16,2560]{2,1,0:T(8,128)(2,1)S(1)} %get-tuple-element.198), channel_id=1, source_target_pairs={{0,4},{1,5},{2,6},{3,7},{4,0},{5,1},{6,2},{7,3},{8,12},{9,13},{10,... | collective-permute-start | bytes 983048 | tf_op jit(solution)/shard_map/ppermute | solution.py:759
  38.8 17.3 %collective-permute-start.11 = (bf16[8,16,2048]{2,1,0:T(8,128)(2,1)S(1)}, bf16[8,16,2048]{2,1,0:T(8,128)(2,1)S(1)}, u32[]{:S(2)}, u32[]{:S(2)}) collective-permute-start(bf16[8,16,2048]{2,1,0:T(8,128)(2,1)S(1)} %bitcast.41), channel_id=1, source_target_pairs={{0,8},{1,9},{2,10},{3,11},{4,12},{5,13},{6,14},{7,15},{8,0},{9,1},... | collective-permute-start | bytes 1572872 | tf_op jit(solution)/shard_map/ppermute | solution.py:759
  56.3 4.6 %collective-permute-start.12 = (bf16[16,16,2560]{2,1,0:T(8,128)(2,1)S(1)}, bf16[16,16,2560]{2,1,0:T(8,128)(2,1)S(1)}, u32[]{:S(2)}, u32[]{:S(2)}) collective-permute-start(bf16[16,16,2560]{2,1,0:T(8,128)(2,1)S(1)} %bitcast.37), channel_id=1, source_target_pairs={{0,1},{1,0},{2,3},{3,2},{4,5},{5,4},{6,7},{7,6},{8,9},{9,8},{10,11... | collective-permute-start | bytes 3932168 | tf_op jit(solution)/shard_map/ppermute | solution.py:759
  77.7 5.9 %collective-permute-start.15 = (bf16[16,16,2048]{2,1,0:T(8,128)(2,1)S(1)}, bf16[16,16,2048]{2,1,0:T(8,128)(2,1)S(1)}, u32[]{:S(2)}, u32[]{:S(2)}) collective-permute-start(bf16[16,16,2048]{2,1,0:T(8,128)(2,1)S(1)} %get-tuple-element.133), channel_id=1, source_target_pairs={{0,1},{1,0},{2,3},{3,2},{4,5},{5,4},{6,7},{7,6},{8,9},{9,8},{10,11... | collective-permute-start | bytes 3145736 | tf_op jit(solution)/shard_map/ppermute | solution.py:759
  77.9 5.7 %collective-permute-start.14 = (bf16[16,16,2048]{2,1,0:T(8,128)(2,1)S(1)}, bf16[16,16,2048]{2,1,0:T(8,128)(2,1)S(1)}, u32[]{:S(2)}, u32[]{:S(2)}) collective-permute-start(bf16[16,16,2048]{2,1,0:T(8,128)(2,1)S(1)} %get-tuple-element.130), channel_id=1, source_target_pairs={{0,1},{1,0},{2,3},{3,2},{4,5},{5,4},{6,7},{7,6},{8,9},{9,8},{10,11... | collective-permute-start | bytes 3145736 | tf_op jit(solution)/shard_map/ppermute | solution.py:759
  84.0 30.5 %collective-permute-start.16 = (bf16[4,16,4096]{2,1,0:T(8,128)(2,1)S(1)}, bf16[4,16,4096]{2,1,0:T(8,128)(2,1)S(1)}, u32[]{:S(2)}, u32[]{:S(2)}) collective-permute-start(bf16[4,16,4096]{2,1,0:T(8,128)(2,1)S(1)} %get-tuple-element.142), channel_id=1, source_target_pairs={{0,2},{1,3},{2,0},{3,1},{4,6},{5,7},{6,4},{7,5},{8,10},{9,11},{10,... | collective-permute-start | bytes 1572872 | tf_op jit(solution)/shard_map/ppermute | solution.py:759
  86.0 28.5 %collective-permute-start.17 = (bf16[4,16,4096]{2,1,0:T(8,128)(2,1)S(1)}, bf16[4,16,4096]{2,1,0:T(8,128)(2,1)S(1)}, u32[]{:S(2)}, u32[]{:S(2)}) collective-permute-start(bf16[4,16,4096]{2,1,0:T(8,128)(2,1)S(1)} %get-tuple-element.143), channel_id=1, source_target_pairs={{0,4},{1,5},{2,6},{3,7},{4,0},{5,1},{6,2},{7,3},{8,12},{9,13},{10,... | collective-permute-start | bytes 1572872 | tf_op jit(solution)/shard_map/ppermute | solution.py:759
  86.1 28.4 %collective-permute-start.18 = (bf16[4,16,4096]{2,1,0:T(8,128)(2,1)S(1)}, bf16[4,16,4096]{2,1,0:T(8,128)(2,1)S(1)}, u32[]{:S(2)}, u32[]{:S(2)}) collective-permute-start(bf16[4,16,4096]{2,1,0:T(8,128)(2,1)S(1)} %get-tuple-element.144), channel_id=1, source_target_pairs={{0,6},{1,7},{2,4},{3,5},{4,2},{5,3},{6,0},{7,1},{8,14},{9,15},{10,... | collective-permute-start | bytes 1572872 | tf_op jit(solution)/shard_map/ppermute | solution.py:759
  114.8 15.3 %collective-permute-start.23 = (bf16[2,16,4096]{2,1,0:T(8,128)(2,1)S(1)}, bf16[2,16,4096]{2,1,0:T(8,128)(2,1)S(1)}, u32[]{:S(2)}, u32[]{:S(2)}) collective-permute-start(bf16[2,16,4096]{2,1,0:T(8,128)(2,1)S(1)} %get-tuple-element.176), channel_id=1, source_target_pairs={{0,16},{1,17},{2,18},{3,19},{4,20},{5,21},{6,22},{7,23},{8,24},{9,... | collective-permute-start | bytes 786440 | tf_op jit(solution)/shard_map/ppermute | solution.py:759
  117.5 12.5 %collective-permute-start.20 = (bf16[4,16,2176]{2,1,0:T(8,128)(2,1)S(1)}, bf16[4,16,2176]{2,1,0:T(8,128)(2,1)S(1)}, u32[]{:S(2)}, u32[]{:S(2)}) collective-permute-start(bf16[4,16,2176]{2,1,0:T(8,128)(2,1)S(1)} %get-tuple-element.173), channel_id=1, source_target_pairs={{0,2},{1,3},{2,0},{3,1},{4,6},{5,7},{6,4},{7,5},{8,10},{9,11},{10,... | collective-permute-start | bytes 835592 | tf_op jit(solution)/shard_map/ppermute | solution.py:759
  119.5 14.4 %collective-permute-start.21 = (bf16[4,16,2176]{2,1,0:T(8,128)(2,1)S(1)}, bf16[4,16,2176]{2,1,0:T(8,128)(2,1)S(1)}, u32[]{:S(2)}, u32[]{:S(2)}) collective-permute-start(bf16[4,16,2176]{2,1,0:T(8,128)(2,1)S(1)} %get-tuple-element.174), channel_id=1, source_target_pairs={{0,4},{1,5},{2,6},{3,7},{4,0},{5,1},{6,2},{7,3},{8,12},{9,13},{10,... | collective-permute-start | bytes 835592 | tf_op jit(solution)/shard_map/ppermute | solution.py:759
  119.6 14.3 %collective-permute-start.22 = (bf16[4,16,2176]{2,1,0:T(8,128)(2,1)S(1)}, bf16[4,16,2176]{2,1,0:T(8,128)(2,1)S(1)}, u32[]{:S(2)}, u32[]{:S(2)}) collective-permute-start(bf16[4,16,2176]{2,1,0:T(8,128)(2,1)S(1)} %get-tuple-element.175), channel_id=1, source_target_pairs={{0,6},{1,7},{2,4},{3,5},{4,2},{5,3},{6,0},{7,1},{8,14},{9,15},{10,... | collective-permute-start | bytes 835592 | tf_op jit(solution)/shard_map/ppermute | solution.py:759
  134.1 10.5 %collective-permute-start.24 = (bf16[1,16,6272]{2,1,0:T(8,128)(2,1)S(1)}, bf16[1,16,6272]{2,1,0:T(8,128)(2,1)S(1)}, u32[]{:S(2)}, u32[]{:S(2)}) collective-permute-start(bf16[1,16,6272]{2,1,0:T(8,128)(2,1)S(1)} %get-tuple-element.184), channel_id=1, source_target_pairs={{0,8},{1,9},{2,10},{3,11},{4,12},{5,13},{6,14},{7,15},{8,0},{9,1},... | collective-permute-start | bytes 602120 | tf_op jit(solution)/shard_map/ppermute | solution.py:759
  136.2 6.0 %collective-permute-start.25 = (bf16[1,16,2176]{2,1,0:T(8,128)(2,1)S(1)}, bf16[1,16,2176]{2,1,0:T(8,128)(2,1)S(1)}, u32[]{:S(2)}, u32[]{:S(2)}) collective-permute-start(bf16[1,16,2176]{2,1,0:T(8,128)(2,1)S(1)} %get-tuple-element.185), channel_id=1, source_target_pairs={{0,16},{1,17},{2,18},{3,19},{4,20},{5,21},{6,22},{7,23},{8,24},{9,... | collective-permute-start | bytes 208904 | tf_op jit(solution)/shard_map/ppermute | solution.py:759
  136.7 7.8 %collective-permute-start.26 = (bf16[1,16,2176]{2,1,0:T(8,128)(2,1)S(1)}, bf16[1,16,2176]{2,1,0:T(8,128)(2,1)S(1)}, u32[]{:S(2)}, u32[]{:S(2)}) collective-permute-start(bf16[1,16,2176]{2,1,0:T(8,128)(2,1)S(1)} %get-tuple-element.186), channel_id=1, source_target_pairs={{0,24},{1,25},{2,26},{3,27},{4,28},{5,29},{6,30},{7,31},{8,16},{9,... | collective-permute-start | bytes 208904 | tf_op jit(solution)/shard_map/ppermute | solution.py:759
  (7 other events, 47.7 us)

commit v2 on v1

--- a/solution.py
+++ b/solution.py
@@ -118,6 +118,14 @@
     return query_side.astype(BF), key_side.T.astype(BF)
 
 
+def longest_pair(q2_t, k2):
+    wide_q = q2_t.astype(F32)
+    wide_k = k2.astype(F32)
+    longest_q = jnp.max(jnp.sum(wide_q * wide_q, axis=0, keepdims=True))
+    longest_k = jnp.max(jnp.sum(wide_k * wide_k, axis=1, keepdims=True))
+    return longest_q * longest_k
+
+
 def pair_forward(normed, weight, bias_q, bias_v, key_aux, qa, ot, outs, pair, block):
     qkv_out, o_out, ot_out, lse_out = outs
     rows = normed.shape[0]
@@ -143,19 +151,36 @@
         q_cols = qa[:, block * index : block * index + block]
         return [dot(keys[h], q_cols) for h in range(2)]
 
-    ahead = score(0)
-    for index in range(count):
-        scores = ahead
-        if index + 1 < count:
-            ahead = score(index + 1)
-        span = slice(block * index, block * index + block)
-        for h in range(2):
-            peak = jnp.max(scores[h], axis=0, keepdims=True)
-            probs = jnp.exp2((scores[h] - peak) * EXP_SCALE).astype(BF)
-            mixed = dot(vts[h], probs)
-            total = mixed[64:65]
-            ot[64 * h : 64 * h + 64, span] = mixed[:64] * (1.0 / total)
-            lse_out[pair, h : h + 1, span] = peak + jnp.log(total) * (1.0 / SCALE)
+    def attend(shifted):
+        ahead = score(0)
+        for index in range(count):
+            scores = ahead
+            if index + 1 < count:
+                ahead = score(index + 1)
+            span = slice(block * index, block * index + block)
+            for h in range(2):
+                if shifted:
+                    peak = jnp.max(scores[h], axis=0, keepdims=True)
+                    probs = jnp.exp2((scores[h] - peak) * EXP_SCALE).astype(BF)
+                else:
+                    peak = 0.0
+                    probs = jnp.exp2(scores[h] * EXP_SCALE).astype(BF)
+                mixed = dot(vts[h], probs)
+                total = mixed[64:65]
+                ot[64 * h : 64 * h + 64, span] = mixed[:64] * (1.0 / total)
+                lse_out[pair, h : h + 1, span] = peak + jnp.log(total) * (1.0 / SCALE)
+
+    bound = longest_pair(qa[0:128, :], k2) * (EXP_SCALE * EXP_SCALE)
+    small = bound < 90.0 * 90.0
+
+    @pl.when(small)
+    def _():
+        attend(False)
+
+    @pl.when(jnp.logical_not(small))
+    def _():
+        attend(True)
+
     ot_out[cols, :] = ot[...].astype(BF)
     o_out[:, cols] = ot[...].T.astype(BF)
 
@@ -533,8 +558,8 @@
     sums[:, span] = jnp.broadcast_to(total, (8, 384))
     scatter_blocks(me, stage, 16, 0, 32, send, keep, span)
     wide = weight[...].astype(F32)
-    vectors[:, 0:1] += jnp.sum(stage[0:512, :] * wide, axis=1, keepdims=True)
-    vectors[:, 1:2] += jnp.sum(wide * total, axis=1, keepdims=True)
+    for index, product in enumerate((stage[0:512, :] * wide, wide * total)):
+        vectors[index] += product[:, 0:128] + product[:, 128:256] + product[:, 256:384]
 
     @pl.when(pair == 3)
     def _():
@@ -550,8 +575,9 @@
         columns[8:9, :] = smalls[0:1, :]
         columns[9:10, :] = smalls[2:3, :]
         tile = columns[...].T
-        plain = vectors[:, 1:2]
-        gain_sum = (vectors[:, 0:1] - tile[:, 9:10] * plain) / tile[:, 8:9]
+        plain = jnp.sum(vectors[1], axis=1, keepdims=True)
+        weighted = jnp.sum(vectors[0], axis=1, keepdims=True)
+        gain_sum = (weighted - tile[:, 9:10] * plain) / tile[:, 8:9]
         lanes = lax.broadcasted_iota(jnp.int32, (512, 128), 1)
         stage[0:512, 0:128] = jnp.where(lanes == 0, gain_sum, jnp.where(lanes == 2, plain, tile))
         lane = lax.broadcasted_iota(jnp.int32, (1, 128), 1)
@@ -602,7 +628,7 @@
             pltpu.VMEM((rows, 384), BF),
             pltpu.VMEM((528, 384), F32),
             pltpu.VMEM((8, 1536), F32),
-            pltpu.VMEM((512, 128), F32),
+            pltpu.VMEM((2, 512, 128), F32),
             pltpu.VMEM((128, 512), F32),
         ],
         compiler_params=pltpu.CompilerParams(vmem_limit_bytes=20 * MIB),

time: 146 us -> 144 us (0.986)
  transfers between devices with their start and end apart: 27 -> 27, of which waited for: 7 -> 7; matrix products, arithmetic and copies ran while one was open for 1% -> 1% of each run, Pallas kernels for 39% -> 38%
where the time goes in v2:
time: 144 us
  Pallas kernels  74.8 us (52%)
  starting transfers between devices  32.5 us (23%)
  waiting for transfers between devices  22.1 us (15%)
  blocking collectives  11.6 us (8%)
    ppermute x27, starting transfers between devices, swap(): return lax.ppermute(value, AXES, [(d, d ^ mask) for d in range(count)])  32.5 us
    pallas_call x1, Pallas kernels, backward(): pl.pallas_call(backward_kernel, grid=(4,), in_specs=[smem()] + parts + [p...  26.7 us
    ppermute x27, waiting for transfers between devices, swap(): return lax.ppermute(value, AXES, [(d, d ^ mask) for d in range(count)])  22.1 us
    pallas_call x1, Pallas kernels, forward(): pl.pallas_call(forward_kernel, in_specs=[smem()] + [vmem()] * 4, out_spec...  16 us
    pallas_call x1, Pallas kernels, feed_first(): pl.pallas_call(feed_first_kernel, in_specs=[smem()] + [vmem()] * 9, out_s...  12.8 us
    all_gather x1, blocking collectives, body(): a_mine = lax.all_gather(after(a_col, c_plane), 'plane').reshape(16, 16, -1)  11.6 us
    pallas_call x1, Pallas kernels, input_terms(): pl.pallas_call(input_kernel, in_specs=[vmem()] * 8, out_specs=[vmem()] *...  6.4 us
    pallas_call x1, Pallas kernels, feed_third(): pl.pallas_call(feed_third_kernel, in_specs=[vmem()] * 7, out_specs=[vmem(...  5.35 us
  transfers between devices with their start and end apart: 27, of which 7 were waited for; matrix products, arithmetic and copies ran while one was open for 1% of the time, Pallas kernels for 38%

profile of v2, /device:TPU:0, one launch (start us, length us, event | category | flops | bytes accessed | tf_op | source)
XLA Modules:
  0.0 144.2 jit_solution(17863152200451322951)
XLA Ops:
  0.6 1.8 %pack.1 = (bf16[16,4224]{1,0:T(8,128)(2,1)}, bf16[16,2048]{1,0:T(8,128)(2,1)}) custom-call(bf16[16,1536]{1,0:T(8,128)(2,1)} %qkv.1, bf16[16,512]{1,0:T(8,128)(2,1)} %mix.1, bf16[16,2048]{1,0:T(8,128)(2,1)} %up.1, bf16[64,512]{1,0:T(8,128)(2,1)} %down.1, bf16[2,16]{1,0:T(2,128)(2,1)} %gain.1, bf16[2,16]{1,0:T(2,128)(2,1)} %shift.1, bf16[2,16]{1,0:T(2,128)(2,1)} %qv.1, ...), custom_call_target="tpu_custom_call" | custom-call | flops 1650000000 | tf_op jit(solution)/shard_map/pack/pallas_call | solution.py:98
  2.4 3.0 %collective-permute-start = (bf16[16,4224]{1,0:T(8,128)(2,1)}, bf16[16,4224]{1,0:T(8,128)(2,1)S(1)}, u32[]{:S(2)}, u32[]{:S(2)}) collective-permute-start(bf16[16,4224]{1,0:T(8,128)(2,1)} %get-tuple-element.114), channel_id=1, source_target_pairs={{0,8},{1,9},{2,10},{3,11},{4,12},{5,13},{6,14},{7,15},{8,0},{9,1},... | collective-permute-start | bytes 405512 | tf_op jit(solution)/shard_map/ppermute | solution.py:785
  5.4 2.6 %collective-permute-start.1 = (bf16[16,4224]{1,0:T(8,128)(2,1)}, bf16[16,4224]{1,0:T(8,128)(2,1)S(1)}, u32[]{:S(2)}, u32[]{:S(2)}) collective-permute-start(bf16[16,4224]{1,0:T(8,128)(2,1)} %get-tuple-element.114), channel_id=1, source_target_pairs={{0,16},{1,17},{2,18},{3,19},{4,20},{5,21},{6,22},{7,23},{8,24},{9,... | collective-permute-start | bytes 405512 | tf_op jit(solution)/shard_map/ppermute | solution.py:785
  13.6 5.3 %collective-permute-done.1 = bf16[16,4224]{1,0:T(8,128)(2,1)S(1)} collective-permute-done((bf16[16,4224]{1,0:T(8,128)(2,1)}, bf16[16,4224]{1,0:T(8,128)(2,1)S(1)}, u32[]{:S(2)}, u32[]{:S(2)}) %collective-permute-start.1) | collective-permute-done | bytes 135200 | tf_op jit(solution)/shard_map/ppermute | solution.py:785
  19.9 3.1 %collective-permute-start.6 = (bf16[4,16,2048]{2,1,0:T(8,128)(2,1)S(1)}, bf16[4,16,2048]{2,1,0:T(8,128)(2,1)S(1)}, u32[]{:S(2)}, u32[]{:S(2)}) collective-permute-start(bf16[4,16,2048]{2,1,0:T(8,128)(2,1)S(1)} %get-tuple-element.200), channel_id=1, source_target_pairs={{0,16},{1,17},{2,18},{3,19},{4,20},{5,21},{6,22},{7,23},{8,24},{9,... | collective-permute-start | bytes 786440 | tf_op jit(solution)/shard_map/ppermute | solution.py:785
  23.0 11.6 %all-gather.mine = bf16[16,16,1664]{2,1,0:T(8,128)(2,1)S(1)} all-gather(bf16[4,16,1664]{2,1,0:T(8,128)(2,1)S(1)} %pad_maximum_fusion.5), channel_id=2, replica_groups=mesh['dp'=4,'plane'=4,'core'=2] {'plane'}, dimensions={0}, use_global_device_ids=true | all-gather | bytes 1064960 | tf_op jit(solution)/shard_map/all_gather | solution.py:852
  34.8 1.7 %collective-permute-start.10 = (bf16[4,16,2560]{2,1,0:T(8,128)(2,1)S(1)}, bf16[4,16,2560]{2,1,0:T(8,128)(2,1)S(1)}, u32[]{:S(2)}, u32[]{:S(2)}) collective-permute-start(bf16[4,16,2560]{2,1,0:T(8,128)(2,1)S(1)} %get-tuple-element.198), channel_id=1, source_target_pairs={{0,6},{1,7},{2,4},{3,5},{4,2},{5,3},{6,0},{7,1},{8,14},{9,15},{10,... | collective-permute-start | bytes 983048 | tf_op jit(solution)/shard_map/ppermute | solution.py:785
  36.6 2.2 %collective-permute-start.8 = (bf16[4,16,2560]{2,1,0:T(8,128)(2,1)S(1)}, bf16[4,16,2560]{2,1,0:T(8,128)(2,1)S(1)}, u32[]{:S(2)}, u32[]{:S(2)}) collective-permute-start(bf16[4,16,2560]{2,1,0:T(8,128)(2,1)S(1)} %get-tuple-element.198), channel_id=1, source_target_pairs={{0,2},{1,3},{2,0},{3,1},{4,6},{5,7},{6,4},{7,5},{8,10},{9,11},{10,... | collective-permute-start | bytes 983048 | tf_op jit(solution)/shard_map/ppermute | solution.py:785
  39.0 16.0 %attend.1 = (bf16[4,3,1024,128]{3,2,1,0:T(8,128)(2,1)S(1)}, bf16[528,1024]{1,0:T(8,128)(2,1)S(1)}, bf16[512,1536]{1,0:T(8,128)(2,1)S(1)}, bf16[1024,512]{1,0:T(8...) custom-call(s32[2]{0:T(128)S(1)} %pad_add_fusion.me_ref, ...), custom_call_target="tpu_custom_call" | custom-call | flops 16499999744 | tf_op jit(solution)/shard_map/attend/pallas_call | solution.py:250
  56.0 3.9 %collective-permute-done.13.other_tall = bf16[16,16,2048]{2,1,0:T(8,128)(2,1)S(1)} collective-permute-done((bf16[16,16,2048]{2,1,0:T(8,128)(2,1)S(1)}, bf16[16,16,2048]{2,1,0:T(8,128)(2,1)S(1)}, u32[]{:S(2)}, u32[]{:S(2)}) %collective-permute-start.13) | collective-permute-done | bytes 1048608 | tf_op jit(solution)/shard_map/ppermute | solution.py:785
  59.9 12.8 %feed_first.1 = (f32[1024,512]{1,0:T(8,128)S(1)}, bf16[528,1024]{1,0:T(8,128)(2,1)S(1)}, bf16[1024,2048]{1,0:T(8,128)(2,1)S(1)}, bf16[16,16,2048]{2,1,0:T(8,128)...) custom-call(s32[2]{0:T(128)S(1)} %pad_add_fusion.me_ref, ...), custom_call_target="tpu_custom_call" | custom-call | flops 19800000512 | tf_op jit(solution)/shard_map/feed_first/pallas_call | solution.py:363
  72.7 4.0 %feed_second.1 = (bf16[16,16,2048]{2,1,0:T(8,128)(2,1)S(1)}, f32[16,16,2048]{2,1,0:T(8,128)S(1)}, f32[1,2048]{1,0:T(1,128)S(1)}) custom-call(s32[2]{0:T(128)S(1)} %pad_add_fusion.me_ref, bf16[528,1024]{1,0:T(8,128)(2,1)S(1)} %get-tuple-element.131.normed_t, bf16[1024,2048]{1,0:T(8,128)(2,1)S(1)} %get-tuple-element.132.grad_pre), custom_call_target="tpu_custom_call" | custom-call | flops 5500000256 | tf_op jit(solution)/shard_map/feed_second/pallas_call | solution.py:403
  77.2 5.3 %feed_third.1 = (f32[1024,512]{1,0:T(8,128)S(1)}, bf16[1024,512]{1,0:T(8,128)(2,1)S(1)}, f32[512,512]{1,0:T(8,128)S(1)}, f32[8,512]{1,0:T(8,128)S(1)}) custom-call(f32[1024,512]{1,0:T(8,128)S(1)} %get-tuple-element.134.middle, bf16[1024,2048]{1,0:T(8,128)(2,1)S(1)} %get-tuple-element.132.grad_pre, bf16[512,512]{1,0:T(8,128)(2,1)S(1)} %get-tuple-element.135.mix, ...), custom_call_target="tpu_custom_call" | custom-call | flops 8800000000 | tf_op jit(solution)/shard_map/feed_third/pallas_call | solution.py:461
  82.9 2.0 %collective-permute-start.16 = (bf16[4,16,4096]{2,1,0:T(8,128)(2,1)S(1)}, bf16[4,16,4096]{2,1,0:T(8,128)(2,1)S(1)}, u32[]{:S(2)}, u32[]{:S(2)}) collective-permute-start(bf16[4,16,4096]{2,1,0:T(8,128)(2,1)S(1)} %get-tuple-element.142), channel_id=1, source_target_pairs={{0,2},{1,3},{2,0},{3,1},{4,6},{5,7},{6,4},{7,5},{8,10},{9,11},{10,... | collective-permute-start | bytes 1572872 | tf_op jit(solution)/shard_map/ppermute | solution.py:785
  86.5 26.7 %attend_back.1 = (bf16[1024,1536]{1,0:T(8,128)(2,1)S(1)}, bf16[16,16,2176]{2,1,0:T(8,128)(2,1)S(1)}, f32[16,16,2176]{2,1,0:T(8,128)S(1)}) custom-call(s32[2]{0:T(128)S(1)} %pad_add_fusion.me_ref, bf16[4,3,1024,128]{3,2,1,0:T(8,128)(2,1)S(1)} %get-tuple-element.145.q.k.v, bf16[4,3,1024,128]{3,2,1,0:T(8,128)(2,1)S(1)} %get-tuple-element.145.q.k.v, ...), custom_call_target="tpu_custom_call" | custom-call | flops 27499999232 | tf_op jit(solution)/shard_map/attend_back/pallas_call | solution.py:604
  113.6 2.0 %collective-permute-start.23 = (bf16[2,16,4096]{2,1,0:T(8,128)(2,1)S(1)}, bf16[2,16,4096]{2,1,0:T(8,128)(2,1)S(1)}, u32[]{:S(2)}, u32[]{:S(2)}) collective-permute-start(bf16[2,16,4096]{2,1,0:T(8,128)(2,1)S(1)} %get-tuple-element.176), channel_id=1, source_target_pairs={{0,16},{1,17},{2,18},{3,19},{4,20},{5,21},{6,22},{7,23},{8,24},{9,... | collective-permute-start | bytes 786440 | tf_op jit(solution)/shard_map/ppermute | solution.py:785
  116.3 2.0 %collective-permute-start.20 = (bf16[4,16,2176]{2,1,0:T(8,128)(2,1)S(1)}, bf16[4,16,2176]{2,1,0:T(8,128)(2,1)S(1)}, u32[]{:S(2)}, u32[]{:S(2)}) collective-permute-start(bf16[4,16,2176]{2,1,0:T(8,128)(2,1)S(1)} %get-tuple-element.173), channel_id=1, source_target_pairs={{0,2},{1,3},{2,0},{3,1},{4,6},{5,7},{6,4},{7,5},{8,10},{9,11},{10,... | collective-permute-start | bytes 835592 | tf_op jit(solution)/shard_map/ppermute | solution.py:785
  119.9 6.4 %input_terms.1 = (f32[1024,512]{1,0:T(8,128)}, bf16[1024,512]{1,0:T(8,128)(2,1)}) custom-call(bf16[1024,512]{1,0:T(8,128)(2,1)S(1)} %copy-done.1, bf16[1024,1536]{1,0:T(8,128)(2,1)S(1)} %get-tuple-element.159.gm, bf16[512,1536]{1,0:T(8,128)(2,1)S(1)} %get-tuple-element.150.weight, f32[8,512]{1,0:T(8,128)S(1)} %get-tuple-element.168.smalls, ...), custom_call_target="tpu_custom_call" | custom-call | flops 8800000000 | tf_op jit(solution)/shard_map/input_terms/pallas_call | solution.py:664
  126.3 2.6 %collective-permute-done.23.du_recv = bf16[2,16,4096]{2,1,0:T(8,128)(2,1)S(1)} collective-permute-done((bf16[2,16,4096]{2,1,0:T(8,128)(2,1)S(1)}, bf16[2,16,4096]{2,1,0:T(8,128)(2,1)S(1)}, u32[]{:S(2)}, u32[]{:S(2)}) %collective-permute-start.23) | collective-permute-done | bytes 262176 | tf_op jit(solution)/shard_map/ppermute | solution.py:785
  128.9 3.9 %collective-permute-done.21.g1 = bf16[4,16,2176]{2,1,0:T(8,128)(2,1)S(1)} collective-permute-done((bf16[4,16,2176]{2,1,0:T(8,128)(2,1)S(1)}, bf16[4,16,2176]{2,1,0:T(8,128)(2,1)S(1)}, u32[]{:S(2)}, u32[]{:S(2)}) %collective-permute-start.21) | collective-permute-done | bytes 278560 | tf_op jit(solution)/shard_map/ppermute | solution.py:785
  132.9 2.1 %collective-permute-start.24 = (bf16[1,16,6272]{2,1,0:T(8,128)(2,1)S(1)}, bf16[1,16,6272]{2,1,0:T(8,128)(2,1)S(1)}, u32[]{:S(2)}, u32[]{:S(2)}) collective-permute-start(bf16[1,16,6272]{2,1,0:T(8,128)(2,1)S(1)} %get-tuple-element.184), channel_id=1, source_target_pairs={{0,8},{1,9},{2,10},{3,11},{4,12},{5,13},{6,14},{7,15},{8,0},{9,1},... | collective-permute-start | bytes 602120 | tf_op jit(solution)/shard_map/ppermute | solution.py:785
  135.5 1.9 %collective-permute-start.26 = (bf16[1,16,2176]{2,1,0:T(8,128)(2,1)S(1)}, bf16[1,16,2176]{2,1,0:T(8,128)(2,1)S(1)}, u32[]{:S(2)}, u32[]{:S(2)}) collective-permute-start(bf16[1,16,2176]{2,1,0:T(8,128)(2,1)S(1)} %get-tuple-element.186), channel_id=1, source_target_pairs={{0,24},{1,25},{2,26},{3,27},{4,28},{5,29},{6,30},{7,31},{8,16},{9,... | collective-permute-start | bytes 208904 | tf_op jit(solution)/shard_map/ppermute | solution.py:785
  137.4 3.5 %collective-permute-done.25.r1 = bf16[1,16,2176]{2,1,0:T(8,128)(2,1)S(1)} collective-permute-done((bf16[1,16,2176]{2,1,0:T(8,128)(2,1)S(1)}, bf16[1,16,2176]{2,1,0:T(8,128)(2,1)S(1)}, u32[]{:S(2)}, u32[]{:S(2)}) %collective-permute-start.25) | collective-permute-done | bytes 69664 | tf_op jit(solution)/shard_map/ppermute | solution.py:785
  140.9 2.4 %collective-permute-done.26.r2 = bf16[1,16,2176]{2,1,0:T(8,128)(2,1)S(1)} collective-permute-done((bf16[1,16,2176]{2,1,0:T(8,128)(2,1)S(1)}, bf16[1,16,2176]{2,1,0:T(8,128)(2,1)S(1)}, u32[]{:S(2)}, u32[]{:S(2)}) %collective-permute-start.26) | collective-permute-done | bytes 69664 | tf_op jit(solution)/shard_map/ppermute | solution.py:785
  (65 shorter events, 14.4 us)
Async XLA Ops:
  2.4 9.7 %collective-permute-start = (bf16[16,4224]{1,0:T(8,128)(2,1)}, bf16[16,4224]{1,0:T(8,128)(2,1)S(1)}, u32[]{:S(2)}, u32[]{:S(2)}) collective-permute-start(bf16[16,4224]{1,0:T(8,128)(2,1)} %get-tuple-element.114), channel_id=1, source_target_pairs={{0,8},{1,9},{2,10},{3,11},{4,12},{5,13},{6,14},{7,15},{8,0},{9,1},... | collective-permute-start | bytes 405512 | tf_op jit(solution)/shard_map/ppermute | solution.py:785
  5.4 13.4 %collective-permute-start.1 = (bf16[16,4224]{1,0:T(8,128)(2,1)}, bf16[16,4224]{1,0:T(8,128)(2,1)S(1)}, u32[]{:S(2)}, u32[]{:S(2)}) collective-permute-start(bf16[16,4224]{1,0:T(8,128)(2,1)} %get-tuple-element.114), channel_id=1, source_target_pairs={{0,16},{1,17},{2,18},{3,19},{4,20},{5,21},{6,22},{7,23},{8,24},{9,... | collective-permute-start | bytes 405512 | tf_op jit(solution)/shard_map/ppermute | solution.py:785
  8.0 10.8 %collective-permute-start.2 = (bf16[16,4224]{1,0:T(8,128)(2,1)}, bf16[16,4224]{1,0:T(8,128)(2,1)S(1)}, u32[]{:S(2)}, u32[]{:S(2)}) collective-permute-start(bf16[16,4224]{1,0:T(8,128)(2,1)} %get-tuple-element.114), channel_id=1, source_target_pairs={{0,24},{1,25},{2,26},{3,27},{4,28},{5,29},{6,30},{7,31},{8,16},{9,... | collective-permute-start | bytes 405512 | tf_op jit(solution)/shard_map/ppermute | solution.py:785
  8.0 10.9 %collective-permute-start.3 = (bf16[16,2048]{1,0:T(8,128)(2,1)}, bf16[16,2048]{1,0:T(8,128)(2,1)S(1)}, u32[]{:S(2)}, u32[]{:S(2)}) collective-permute-start(bf16[16,2048]{1,0:T(8,128)(2,1)} %get-tuple-element.108), channel_id=1, source_target_pairs={{0,2},{1,3},{2,0},{3,1},{4,6},{5,7},{6,4},{7,5},{8,10},{9,11},{10,... | collective-permute-start | bytes 196616 | tf_op jit(solution)/shard_map/ppermute | solution.py:785
  9.7 9.2 %collective-permute-start.4 = (bf16[16,2048]{1,0:T(8,128)(2,1)}, bf16[16,2048]{1,0:T(8,128)(2,1)S(1)}, u32[]{:S(2)}, u32[]{:S(2)}) collective-permute-start(bf16[16,2048]{1,0:T(8,128)(2,1)} %get-tuple-element.108), channel_id=1, source_target_pairs={{0,4},{1,5},{2,6},{3,7},{4,0},{5,1},{6,2},{7,3},{8,12},{9,13},{10,... | collective-permute-start | bytes 196616 | tf_op jit(solution)/shard_map/ppermute | solution.py:785
  12.1 6.9 %collective-permute-start.5 = (bf16[16,2048]{1,0:T(8,128)(2,1)}, bf16[16,2048]{1,0:T(8,128)(2,1)S(1)}, u32[]{:S(2)}, u32[]{:S(2)}) collective-permute-start(bf16[16,2048]{1,0:T(8,128)(2,1)} %get-tuple-element.108), channel_id=1, source_target_pairs={{0,6},{1,7},{2,4},{3,5},{4,2},{5,3},{6,0},{7,1},{8,14},{9,15},{10,... | collective-permute-start | bytes 196616 | tf_op jit(solution)/shard_map/ppermute | solution.py:785
  19.9 14.8 %collective-permute-start.6 = (bf16[4,16,2048]{2,1,0:T(8,128)(2,1)S(1)}, bf16[4,16,2048]{2,1,0:T(8,128)(2,1)S(1)}, u32[]{:S(2)}, u32[]{:S(2)}) collective-permute-start(bf16[4,16,2048]{2,1,0:T(8,128)(2,1)S(1)} %get-tuple-element.200), channel_id=1, source_target_pairs={{0,16},{1,17},{2,18},{3,19},{4,20},{5,21},{6,22},{7,23},{8,24},{9,... | collective-permute-start | bytes 786440 | tf_op jit(solution)/shard_map/ppermute | solution.py:785
  34.8 20.2 %collective-permute-start.10 = (bf16[4,16,2560]{2,1,0:T(8,128)(2,1)S(1)}, bf16[4,16,2560]{2,1,0:T(8,128)(2,1)S(1)}, u32[]{:S(2)}, u32[]{:S(2)}) collective-permute-start(bf16[4,16,2560]{2,1,0:T(8,128)(2,1)S(1)} %get-tuple-element.198), channel_id=1, source_target_pairs={{0,6},{1,7},{2,4},{3,5},{4,2},{5,3},{6,0},{7,1},{8,14},{9,15},{10,... | collective-permute-start | bytes 983048 | tf_op jit(solution)/shard_map/ppermute | solution.py:785
  36.6 18.5 %collective-permute-start.8 = (bf16[4,16,2560]{2,1,0:T(8,128)(2,1)S(1)}, bf16[4,16,2560]{2,1,0:T(8,128)(2,1)S(1)}, u32[]{:S(2)}, u32[]{:S(2)}) collective-permute-start(bf16[4,16,2560]{2,1,0:T(8,128)(2,1)S(1)} %get-tuple-element.198), channel_id=1, source_target_pairs={{0,2},{1,3},{2,0},{3,1},{4,6},{5,7},{6,4},{7,5},{8,10},{9,11},{10,... | collective-permute-start | bytes 983048 | tf_op jit(solution)/shard_map/ppermute | solution.py:785
  38.8 16.3 %collective-permute-start.9 = (bf16[4,16,2560]{2,1,0:T(8,128)(2,1)S(1)}, bf16[4,16,2560]{2,1,0:T(8,128)(2,1)S(1)}, u32[]{:S(2)}, u32[]{:S(2)}) collective-permute-start(bf16[4,16,2560]{2,1,0:T(8,128)(2,1)S(1)} %get-tuple-element.198), channel_id=1, source_target_pairs={{0,4},{1,5},{2,6},{3,7},{4,0},{5,1},{6,2},{7,3},{8,12},{9,13},{10,... | collective-permute-start | bytes 983048 | tf_op jit(solution)/shard_map/ppermute | solution.py:785
  38.8 16.2 %collective-permute-start.11 = (bf16[8,16,2048]{2,1,0:T(8,128)(2,1)S(1)}, bf16[8,16,2048]{2,1,0:T(8,128)(2,1)S(1)}, u32[]{:S(2)}, u32[]{:S(2)}) collective-permute-start(bf16[8,16,2048]{2,1,0:T(8,128)(2,1)S(1)} %bitcast.41), channel_id=1, source_target_pairs={{0,8},{1,9},{2,10},{3,11},{4,12},{5,13},{6,14},{7,15},{8,0},{9,1},... | collective-permute-start | bytes 1572872 | tf_op jit(solution)/shard_map/ppermute | solution.py:785
  55.3 4.6 %collective-permute-start.12 = (bf16[16,16,2560]{2,1,0:T(8,128)(2,1)S(1)}, bf16[16,16,2560]{2,1,0:T(8,128)(2,1)S(1)}, u32[]{:S(2)}, u32[]{:S(2)}) collective-permute-start(bf16[16,16,2560]{2,1,0:T(8,128)(2,1)S(1)} %bitcast.37), channel_id=1, source_target_pairs={{0,1},{1,0},{2,3},{3,2},{4,5},{5,4},{6,7},{7,6},{8,9},{9,8},{10,11... | collective-permute-start | bytes 3932168 | tf_op jit(solution)/shard_map/ppermute | solution.py:785
  76.6 5.9 %collective-permute-start.15 = (bf16[16,16,2048]{2,1,0:T(8,128)(2,1)S(1)}, bf16[16,16,2048]{2,1,0:T(8,128)(2,1)S(1)}, u32[]{:S(2)}, u32[]{:S(2)}) collective-permute-start(bf16[16,16,2048]{2,1,0:T(8,128)(2,1)S(1)} %get-tuple-element.133), channel_id=1, source_target_pairs={{0,1},{1,0},{2,3},{3,2},{4,5},{5,4},{6,7},{7,6},{8,9},{9,8},{10,11... | collective-permute-start | bytes 3145736 | tf_op jit(solution)/shard_map/ppermute | solution.py:785
  76.9 5.7 %collective-permute-start.14 = (bf16[16,16,2048]{2,1,0:T(8,128)(2,1)S(1)}, bf16[16,16,2048]{2,1,0:T(8,128)(2,1)S(1)}, u32[]{:S(2)}, u32[]{:S(2)}) collective-permute-start(bf16[16,16,2048]{2,1,0:T(8,128)(2,1)S(1)} %get-tuple-element.130), channel_id=1, source_target_pairs={{0,1},{1,0},{2,3},{3,2},{4,5},{5,4},{6,7},{7,6},{8,9},{9,8},{10,11... | collective-permute-start | bytes 3145736 | tf_op jit(solution)/shard_map/ppermute | solution.py:785
  82.9 30.3 %collective-permute-start.16 = (bf16[4,16,4096]{2,1,0:T(8,128)(2,1)S(1)}, bf16[4,16,4096]{2,1,0:T(8,128)(2,1)S(1)}, u32[]{:S(2)}, u32[]{:S(2)}) collective-permute-start(bf16[4,16,4096]{2,1,0:T(8,128)(2,1)S(1)} %get-tuple-element.142), channel_id=1, source_target_pairs={{0,2},{1,3},{2,0},{3,1},{4,6},{5,7},{6,4},{7,5},{8,10},{9,11},{10,... | collective-permute-start | bytes 1572872 | tf_op jit(solution)/shard_map/ppermute | solution.py:785
  85.0 28.3 %collective-permute-start.17 = (bf16[4,16,4096]{2,1,0:T(8,128)(2,1)S(1)}, bf16[4,16,4096]{2,1,0:T(8,128)(2,1)S(1)}, u32[]{:S(2)}, u32[]{:S(2)}) collective-permute-start(bf16[4,16,4096]{2,1,0:T(8,128)(2,1)S(1)} %get-tuple-element.143), channel_id=1, source_target_pairs={{0,4},{1,5},{2,6},{3,7},{4,0},{5,1},{6,2},{7,3},{8,12},{9,13},{10,... | collective-permute-start | bytes 1572872 | tf_op jit(solution)/shard_map/ppermute | solution.py:785
  85.0 28.2 %collective-permute-start.18 = (bf16[4,16,4096]{2,1,0:T(8,128)(2,1)S(1)}, bf16[4,16,4096]{2,1,0:T(8,128)(2,1)S(1)}, u32[]{:S(2)}, u32[]{:S(2)}) collective-permute-start(bf16[4,16,4096]{2,1,0:T(8,128)(2,1)S(1)} %get-tuple-element.144), channel_id=1, source_target_pairs={{0,6},{1,7},{2,4},{3,5},{4,2},{5,3},{6,0},{7,1},{8,14},{9,15},{10,... | collective-permute-start | bytes 1572872 | tf_op jit(solution)/shard_map/ppermute | solution.py:785
  113.6 15.3 %collective-permute-start.23 = (bf16[2,16,4096]{2,1,0:T(8,128)(2,1)S(1)}, bf16[2,16,4096]{2,1,0:T(8,128)(2,1)S(1)}, u32[]{:S(2)}, u32[]{:S(2)}) collective-permute-start(bf16[2,16,4096]{2,1,0:T(8,128)(2,1)S(1)} %get-tuple-element.176), channel_id=1, source_target_pairs={{0,16},{1,17},{2,18},{3,19},{4,20},{5,21},{6,22},{7,23},{8,24},{9,... | collective-permute-start | bytes 786440 | tf_op jit(solution)/shard_map/ppermute | solution.py:785
  116.3 12.5 %collective-permute-start.20 = (bf16[4,16,2176]{2,1,0:T(8,128)(2,1)S(1)}, bf16[4,16,2176]{2,1,0:T(8,128)(2,1)S(1)}, u32[]{:S(2)}, u32[]{:S(2)}) collective-permute-start(bf16[4,16,2176]{2,1,0:T(8,128)(2,1)S(1)} %get-tuple-element.173), channel_id=1, source_target_pairs={{0,2},{1,3},{2,0},{3,1},{4,6},{5,7},{6,4},{7,5},{8,10},{9,11},{10,... | collective-permute-start | bytes 835592 | tf_op jit(solution)/shard_map/ppermute | solution.py:785
  118.3 14.4 %collective-permute-start.21 = (bf16[4,16,2176]{2,1,0:T(8,128)(2,1)S(1)}, bf16[4,16,2176]{2,1,0:T(8,128)(2,1)S(1)}, u32[]{:S(2)}, u32[]{:S(2)}) collective-permute-start(bf16[4,16,2176]{2,1,0:T(8,128)(2,1)S(1)} %get-tuple-element.174), channel_id=1, source_target_pairs={{0,4},{1,5},{2,6},{3,7},{4,0},{5,1},{6,2},{7,3},{8,12},{9,13},{10,... | collective-permute-start | bytes 835592 | tf_op jit(solution)/shard_map/ppermute | solution.py:785
  118.4 14.3 %collective-permute-start.22 = (bf16[4,16,2176]{2,1,0:T(8,128)(2,1)S(1)}, bf16[4,16,2176]{2,1,0:T(8,128)(2,1)S(1)}, u32[]{:S(2)}, u32[]{:S(2)}) collective-permute-start(bf16[4,16,2176]{2,1,0:T(8,128)(2,1)S(1)} %get-tuple-element.175), channel_id=1, source_target_pairs={{0,6},{1,7},{2,4},{3,5},{4,2},{5,3},{6,0},{7,1},{8,14},{9,15},{10,... | collective-permute-start | bytes 835592 | tf_op jit(solution)/shard_map/ppermute | solution.py:785
  132.9 10.5 %collective-permute-start.24 = (bf16[1,16,6272]{2,1,0:T(8,128)(2,1)S(1)}, bf16[1,16,6272]{2,1,0:T(8,128)(2,1)S(1)}, u32[]{:S(2)}, u32[]{:S(2)}) collective-permute-start(bf16[1,16,6272]{2,1,0:T(8,128)(2,1)S(1)} %get-tuple-element.184), channel_id=1, source_target_pairs={{0,8},{1,9},{2,10},{3,11},{4,12},{5,13},{6,14},{7,15},{8,0},{9,1},... | collective-permute-start | bytes 602120 | tf_op jit(solution)/shard_map/ppermute | solution.py:785
  135.0 6.0 %collective-permute-start.25 = (bf16[1,16,2176]{2,1,0:T(8,128)(2,1)S(1)}, bf16[1,16,2176]{2,1,0:T(8,128)(2,1)S(1)}, u32[]{:S(2)}, u32[]{:S(2)}) collective-permute-start(bf16[1,16,2176]{2,1,0:T(8,128)(2,1)S(1)} %get-tuple-element.185), channel_id=1, source_target_pairs={{0,16},{1,17},{2,18},{3,19},{4,20},{5,21},{6,22},{7,23},{8,24},{9,... | collective-permute-start | bytes 208904 | tf_op jit(solution)/shard_map/ppermute | solution.py:785
  135.5 7.9 %collective-permute-start.26 = (bf16[1,16,2176]{2,1,0:T(8,128)(2,1)S(1)}, bf16[1,16,2176]{2,1,0:T(8,128)(2,1)S(1)}, u32[]{:S(2)}, u32[]{:S(2)}) collective-permute-start(bf16[1,16,2176]{2,1,0:T(8,128)(2,1)S(1)} %get-tuple-element.186), channel_id=1, source_target_pairs={{0,24},{1,25},{2,26},{3,27},{4,28},{5,29},{6,30},{7,31},{8,16},{9,... | collective-permute-start | bytes 208904 | tf_op jit(solution)/shard_map/ppermute | solution.py:785
  (7 other events, 47.7 us)

commit v3 on v2

--- a/solution.py
+++ b/solution.py
@@ -387,7 +387,7 @@
 
 def feed_second_kernel(me_ref, normed_t, grad_pre, u_send, u_keep, up_bias_grad, stage):
     me = me_ref[0]
-    width = 512
+    width = 1024
 
     def one_chunk(chunk, carry):
         span = block_of(chunk, width)
@@ -409,8 +409,8 @@
             shape((16, 16, 2048), F32),
             shape((1, 2048), F32),
         ],
-        scratch_shapes=[pltpu.VMEM((528, 512), F32)],
-        compiler_params=pltpu.CompilerParams(vmem_limit_bytes=10 * MIB),
+        scratch_shapes=[pltpu.VMEM((528, 1024), F32)],
+        compiler_params=pltpu.CompilerParams(vmem_limit_bytes=12 * MIB),
         cost_estimate=cost(5),
         name="feed_second",
     )(me, normed_t, grad_pre)
@@ -421,7 +421,7 @@
     grad_middle, grad_att, mix_grad, small_grads, low_rows,
 ):
     rows = middle.shape[0]
-    block = 256
+    block = 512
 
     def behind(index, carry):
         gain_sum, shift_sum, branch_sum, cot_sum = carry
@@ -469,7 +469,7 @@
             shape((8, 512), F32),
         ],
         scratch_shapes=[pltpu.VMEM((rows, 512), BF)],
-        compiler_params=pltpu.CompilerParams(vmem_limit_bytes=12 * MIB),
+        compiler_params=pltpu.CompilerParams(vmem_limit_bytes=14 * MIB),
         cost_estimate=cost(8),
         name="feed_third",
     )(middle, grad_pre, mix, up, smalls, cot, ot_in)

time: 144 us -> 144 us (level)
  no operation moved by 1% of the time
where the time goes in v3:
time: 144 us; the launch traced here: 143 us
  Pallas kernels  74 us (51%)
  starting transfers between devices  32.5 us (23%)
  waiting for transfers between devices  22.1 us (15%)
  blocking collectives  11.6 us (8%)
    ppermute x27, starting transfers between devices, swap(): return lax.ppermute(value, AXES, [(d, d ^ mask) for d in range(count)])  32.5 us
    pallas_call x1, Pallas kernels, backward(): pl.pallas_call(backward_kernel, grid=(4,), in_specs=[smem()] + parts + [p...  26.7 us
    ppermute x27, waiting for transfers between devices, swap(): return lax.ppermute(value, AXES, [(d, d ^ mask) for d in range(count)])  22.1 us
    pallas_call x1, Pallas kernels, forward(): pl.pallas_call(forward_kernel, in_specs=[smem()] + [vmem()] * 4, out_spec...  16 us
    pallas_call x1, Pallas kernels, feed_first(): pl.pallas_call(feed_first_kernel, in_specs=[smem()] + [vmem()] * 9, out_s...  12.8 us
    all_gather x1, blocking collectives, body(): a_mine = lax.all_gather(after(a_col, c_plane), 'plane').reshape(16, 16, -1)  11.6 us
    pallas_call x1, Pallas kernels, input_terms(): pl.pallas_call(input_kernel, in_specs=[vmem()] * 8, out_specs=[vmem()] *...  6.4 us
    pallas_call x1, Pallas kernels, feed_third(): pl.pallas_call(feed_third_kernel, in_specs=[vmem()] * 7, out_specs=[vmem(...  4.92 us
  transfers between devices with their start and end apart: 27, of which 7 were waited for; matrix products, arithmetic and copies ran while one was open for 1% of the time, Pallas kernels for 38%

profile of v3, /device:TPU:0, one launch (start us, length us, event | category | flops | bytes accessed | tf_op | source)
XLA Modules:
  0.0 143.4 jit_solution(13286266698552617091)
XLA Ops:
  0.6 1.8 %pack.1 = (bf16[16,4224]{1,0:T(8,128)(2,1)}, bf16[16,2048]{1,0:T(8,128)(2,1)}) custom-call(bf16[16,1536]{1,0:T(8,128)(2,1)} %qkv.1, bf16[16,512]{1,0:T(8,128)(2,1)} %mix.1, bf16[16,2048]{1,0:T(8,128)(2,1)} %up.1, bf16[64,512]{1,0:T(8,128)(2,1)} %down.1, bf16[2,16]{1,0:T(2,128)(2,1)} %gain.1, bf16[2,16]{1,0:T(2,128)(2,1)} %shift.1, bf16[2,16]{1,0:T(2,128)(2,1)} %qv.1, ...), custom_call_target="tpu_custom_call" | custom-call | flops 1650000000 | tf_op jit(solution)/shard_map/pack/pallas_call | solution.py:98
  2.4 3.0 %collective-permute-start = (bf16[16,4224]{1,0:T(8,128)(2,1)}, bf16[16,4224]{1,0:T(8,128)(2,1)S(1)}, u32[]{:S(2)}, u32[]{:S(2)}) collective-permute-start(bf16[16,4224]{1,0:T(8,128)(2,1)} %get-tuple-element.114), channel_id=1, source_target_pairs={{0,8},{1,9},{2,10},{3,11},{4,12},{5,13},{6,14},{7,15},{8,0},{9,1},... | collective-permute-start | bytes 405512 | tf_op jit(solution)/shard_map/ppermute | solution.py:785
  5.4 2.6 %collective-permute-start.1 = (bf16[16,4224]{1,0:T(8,128)(2,1)}, bf16[16,4224]{1,0:T(8,128)(2,1)S(1)}, u32[]{:S(2)}, u32[]{:S(2)}) collective-permute-start(bf16[16,4224]{1,0:T(8,128)(2,1)} %get-tuple-element.114), channel_id=1, source_target_pairs={{0,16},{1,17},{2,18},{3,19},{4,20},{5,21},{6,22},{7,23},{8,24},{9,... | collective-permute-start | bytes 405512 | tf_op jit(solution)/shard_map/ppermute | solution.py:785
  13.6 5.3 %collective-permute-done.1 = bf16[16,4224]{1,0:T(8,128)(2,1)S(1)} collective-permute-done((bf16[16,4224]{1,0:T(8,128)(2,1)}, bf16[16,4224]{1,0:T(8,128)(2,1)S(1)}, u32[]{:S(2)}, u32[]{:S(2)}) %collective-permute-start.1) | collective-permute-done | bytes 135200 | tf_op jit(solution)/shard_map/ppermute | solution.py:785
  19.9 3.1 %collective-permute-start.6 = (bf16[4,16,2048]{2,1,0:T(8,128)(2,1)S(1)}, bf16[4,16,2048]{2,1,0:T(8,128)(2,1)S(1)}, u32[]{:S(2)}, u32[]{:S(2)}) collective-permute-start(bf16[4,16,2048]{2,1,0:T(8,128)(2,1)S(1)} %get-tuple-element.200), channel_id=1, source_target_pairs={{0,16},{1,17},{2,18},{3,19},{4,20},{5,21},{6,22},{7,23},{8,24},{9,... | collective-permute-start | bytes 786440 | tf_op jit(solution)/shard_map/ppermute | solution.py:785
  23.0 11.6 %all-gather.mine = bf16[16,16,1664]{2,1,0:T(8,128)(2,1)S(1)} all-gather(bf16[4,16,1664]{2,1,0:T(8,128)(2,1)S(1)} %pad_maximum_fusion.5), channel_id=2, replica_groups=mesh['dp'=4,'plane'=4,'core'=2] {'plane'}, dimensions={0}, use_global_device_ids=true | all-gather | bytes 1064960 | tf_op jit(solution)/shard_map/all_gather | solution.py:852
  34.8 1.7 %collective-permute-start.10 = (bf16[4,16,2560]{2,1,0:T(8,128)(2,1)S(1)}, bf16[4,16,2560]{2,1,0:T(8,128)(2,1)S(1)}, u32[]{:S(2)}, u32[]{:S(2)}) collective-permute-start(bf16[4,16,2560]{2,1,0:T(8,128)(2,1)S(1)} %get-tuple-element.198), channel_id=1, source_target_pairs={{0,6},{1,7},{2,4},{3,5},{4,2},{5,3},{6,0},{7,1},{8,14},{9,15},{10,... | collective-permute-start | bytes 983048 | tf_op jit(solution)/shard_map/ppermute | solution.py:785
  36.6 2.2 %collective-permute-start.8 = (bf16[4,16,2560]{2,1,0:T(8,128)(2,1)S(1)}, bf16[4,16,2560]{2,1,0:T(8,128)(2,1)S(1)}, u32[]{:S(2)}, u32[]{:S(2)}) collective-permute-start(bf16[4,16,2560]{2,1,0:T(8,128)(2,1)S(1)} %get-tuple-element.198), channel_id=1, source_target_pairs={{0,2},{1,3},{2,0},{3,1},{4,6},{5,7},{6,4},{7,5},{8,10},{9,11},{10,... | collective-permute-start | bytes 983048 | tf_op jit(solution)/shard_map/ppermute | solution.py:785
  39.0 16.0 %attend.1 = (bf16[4,3,1024,128]{3,2,1,0:T(8,128)(2,1)S(1)}, bf16[528,1024]{1,0:T(8,128)(2,1)S(1)}, bf16[512,1536]{1,0:T(8,128)(2,1)S(1)}, bf16[1024,512]{1,0:T(8...) custom-call(s32[2]{0:T(128)S(1)} %pad_add_fusion.me_ref, ...), custom_call_target="tpu_custom_call" | custom-call | flops 16499999744 | tf_op jit(solution)/shard_map/attend/pallas_call | solution.py:250
  56.0 3.9 %collective-permute-done.13.other_tall = bf16[16,16,2048]{2,1,0:T(8,128)(2,1)S(1)} collective-permute-done((bf16[16,16,2048]{2,1,0:T(8,128)(2,1)S(1)}, bf16[16,16,2048]{2,1,0:T(8,128)(2,1)S(1)}, u32[]{:S(2)}, u32[]{:S(2)}) %collective-permute-start.13) | collective-permute-done | bytes 1048608 | tf_op jit(solution)/shard_map/ppermute | solution.py:785
  59.9 12.8 %feed_first.1 = (f32[1024,512]{1,0:T(8,128)S(1)}, bf16[528,1024]{1,0:T(8,128)(2,1)S(1)}, bf16[1024,2048]{1,0:T(8,128)(2,1)S(1)}, bf16[16,16,2048]{2,1,0:T(8,128)...) custom-call(s32[2]{0:T(128)S(1)} %pad_add_fusion.me_ref, ...), custom_call_target="tpu_custom_call" | custom-call | flops 19800000512 | tf_op jit(solution)/shard_map/feed_first/pallas_call | solution.py:363
  72.7 3.6 %feed_second.1 = (bf16[16,16,2048]{2,1,0:T(8,128)(2,1)S(1)}, f32[16,16,2048]{2,1,0:T(8,128)S(1)}, f32[1,2048]{1,0:T(1,128)S(1)}) custom-call(s32[2]{0:T(128)S(1)} %pad_add_fusion.me_ref, bf16[528,1024]{1,0:T(8,128)(2,1)S(1)} %get-tuple-element.131.normed_t, bf16[1024,2048]{1,0:T(8,128)(2,1)S(1)} %get-tuple-element.132.grad_pre), custom_call_target="tpu_custom_call" | custom-call | flops 5500000256 | tf_op jit(solution)/shard_map/feed_second/pallas_call | solution.py:403
  76.8 4.9 %feed_third.1 = (f32[1024,512]{1,0:T(8,128)S(1)}, bf16[1024,512]{1,0:T(8,128)(2,1)S(1)}, f32[512,512]{1,0:T(8,128)S(1)}, f32[8,512]{1,0:T(8,128)S(1)}) custom-call(f32[1024,512]{1,0:T(8,128)S(1)} %get-tuple-element.134.middle, bf16[1024,2048]{1,0:T(8,128)(2,1)S(1)} %get-tuple-element.132.grad_pre, bf16[512,512]{1,0:T(8,128)(2,1)S(1)} %get-tuple-element.135.mix, ...), custom_call_target="tpu_custom_call" | custom-call | flops 8800000000 | tf_op jit(solution)/shard_map/feed_third/pallas_call | solution.py:461
  82.2 2.0 %collective-permute-start.16 = (bf16[4,16,4096]{2,1,0:T(8,128)(2,1)S(1)}, bf16[4,16,4096]{2,1,0:T(8,128)(2,1)S(1)}, u32[]{:S(2)}, u32[]{:S(2)}) collective-permute-start(bf16[4,16,4096]{2,1,0:T(8,128)(2,1)S(1)} %get-tuple-element.142), channel_id=1, source_target_pairs={{0,2},{1,3},{2,0},{3,1},{4,6},{5,7},{6,4},{7,5},{8,10},{9,11},{10,... | collective-permute-start | bytes 1572872 | tf_op jit(solution)/shard_map/ppermute | solution.py:785
  85.7 26.7 %attend_back.1 = (bf16[1024,1536]{1,0:T(8,128)(2,1)S(1)}, bf16[16,16,2176]{2,1,0:T(8,128)(2,1)S(1)}, f32[16,16,2176]{2,1,0:T(8,128)S(1)}) custom-call(s32[2]{0:T(128)S(1)} %pad_add_fusion.me_ref, bf16[4,3,1024,128]{3,2,1,0:T(8,128)(2,1)S(1)} %get-tuple-element.145.q.k.v, bf16[4,3,1024,128]{3,2,1,0:T(8,128)(2,1)S(1)} %get-tuple-element.145.q.k.v, ...), custom_call_target="tpu_custom_call" | custom-call | flops 27499999232 | tf_op jit(solution)/shard_map/attend_back/pallas_call | solution.py:604
  112.8 2.0 %collective-permute-start.23 = (bf16[2,16,4096]{2,1,0:T(8,128)(2,1)S(1)}, bf16[2,16,4096]{2,1,0:T(8,128)(2,1)S(1)}, u32[]{:S(2)}, u32[]{:S(2)}) collective-permute-start(bf16[2,16,4096]{2,1,0:T(8,128)(2,1)S(1)} %get-tuple-element.176), channel_id=1, source_target_pairs={{0,16},{1,17},{2,18},{3,19},{4,20},{5,21},{6,22},{7,23},{8,24},{9,... | collective-permute-start | bytes 786440 | tf_op jit(solution)/shard_map/ppermute | solution.py:785
  115.5 2.0 %collective-permute-start.20 = (bf16[4,16,2176]{2,1,0:T(8,128)(2,1)S(1)}, bf16[4,16,2176]{2,1,0:T(8,128)(2,1)S(1)}, u32[]{:S(2)}, u32[]{:S(2)}) collective-permute-start(bf16[4,16,2176]{2,1,0:T(8,128)(2,1)S(1)} %get-tuple-element.173), channel_id=1, source_target_pairs={{0,2},{1,3},{2,0},{3,1},{4,6},{5,7},{6,4},{7,5},{8,10},{9,11},{10,... | collective-permute-start | bytes 835592 | tf_op jit(solution)/shard_map/ppermute | solution.py:785
  119.1 6.4 %input_terms.1 = (f32[1024,512]{1,0:T(8,128)}, bf16[1024,512]{1,0:T(8,128)(2,1)}) custom-call(bf16[1024,512]{1,0:T(8,128)(2,1)S(1)} %copy-done.1, bf16[1024,1536]{1,0:T(8,128)(2,1)S(1)} %get-tuple-element.159.gm, bf16[512,1536]{1,0:T(8,128)(2,1)S(1)} %get-tuple-element.150.weight, f32[8,512]{1,0:T(8,128)S(1)} %get-tuple-element.168.smalls, ...), custom_call_target="tpu_custom_call" | custom-call | flops 8800000000 | tf_op jit(solution)/shard_map/input_terms/pallas_call | solution.py:664
  125.5 2.5 %collective-permute-done.23.du_recv = bf16[2,16,4096]{2,1,0:T(8,128)(2,1)S(1)} collective-permute-done((bf16[2,16,4096]{2,1,0:T(8,128)(2,1)S(1)}, bf16[2,16,4096]{2,1,0:T(8,128)(2,1)S(1)}, u32[]{:S(2)}, u32[]{:S(2)}) %collective-permute-start.23) | collective-permute-done | bytes 262176 | tf_op jit(solution)/shard_map/ppermute | solution.py:785
  128.1 3.9 %collective-permute-done.21.g1 = bf16[4,16,2176]{2,1,0:T(8,128)(2,1)S(1)} collective-permute-done((bf16[4,16,2176]{2,1,0:T(8,128)(2,1)S(1)}, bf16[4,16,2176]{2,1,0:T(8,128)(2,1)S(1)}, u32[]{:S(2)}, u32[]{:S(2)}) %collective-permute-start.21) | collective-permute-done | bytes 278560 | tf_op jit(solution)/shard_map/ppermute | solution.py:785
  132.1 2.1 %collective-permute-start.24 = (bf16[1,16,6272]{2,1,0:T(8,128)(2,1)S(1)}, bf16[1,16,6272]{2,1,0:T(8,128)(2,1)S(1)}, u32[]{:S(2)}, u32[]{:S(2)}) collective-permute-start(bf16[1,16,6272]{2,1,0:T(8,128)(2,1)S(1)} %get-tuple-element.184), channel_id=1, source_target_pairs={{0,8},{1,9},{2,10},{3,11},{4,12},{5,13},{6,14},{7,15},{8,0},{9,1},... | collective-permute-start | bytes 602120 | tf_op jit(solution)/shard_map/ppermute | solution.py:785
  134.8 1.9 %collective-permute-start.26 = (bf16[1,16,2176]{2,1,0:T(8,128)(2,1)S(1)}, bf16[1,16,2176]{2,1,0:T(8,128)(2,1)S(1)}, u32[]{:S(2)}, u32[]{:S(2)}) collective-permute-start(bf16[1,16,2176]{2,1,0:T(8,128)(2,1)S(1)} %get-tuple-element.186), channel_id=1, source_target_pairs={{0,24},{1,25},{2,26},{3,27},{4,28},{5,29},{6,30},{7,31},{8,16},{9,... | collective-permute-start | bytes 208904 | tf_op jit(solution)/shard_map/ppermute | solution.py:785
  136.7 3.5 %collective-permute-done.25.r1 = bf16[1,16,2176]{2,1,0:T(8,128)(2,1)S(1)} collective-permute-done((bf16[1,16,2176]{2,1,0:T(8,128)(2,1)S(1)}, bf16[1,16,2176]{2,1,0:T(8,128)(2,1)S(1)}, u32[]{:S(2)}, u32[]{:S(2)}) %collective-permute-start.25) | collective-permute-done | bytes 69664 | tf_op jit(solution)/shard_map/ppermute | solution.py:785
  140.2 2.4 %collective-permute-done.26.r2 = bf16[1,16,2176]{2,1,0:T(8,128)(2,1)S(1)} collective-permute-done((bf16[1,16,2176]{2,1,0:T(8,128)(2,1)S(1)}, bf16[1,16,2176]{2,1,0:T(8,128)(2,1)S(1)}, u32[]{:S(2)}, u32[]{:S(2)}) %collective-permute-start.26) | collective-permute-done | bytes 69664 | tf_op jit(solution)/shard_map/ppermute | solution.py:785
  (65 shorter events, 14.5 us)
Async XLA Ops:
  2.4 9.7 %collective-permute-start = (bf16[16,4224]{1,0:T(8,128)(2,1)}, bf16[16,4224]{1,0:T(8,128)(2,1)S(1)}, u32[]{:S(2)}, u32[]{:S(2)}) collective-permute-start(bf16[16,4224]{1,0:T(8,128)(2,1)} %get-tuple-element.114), channel_id=1, source_target_pairs={{0,8},{1,9},{2,10},{3,11},{4,12},{5,13},{6,14},{7,15},{8,0},{9,1},... | collective-permute-start | bytes 405512 | tf_op jit(solution)/shard_map/ppermute | solution.py:785
  5.4 13.4 %collective-permute-start.1 = (bf16[16,4224]{1,0:T(8,128)(2,1)}, bf16[16,4224]{1,0:T(8,128)(2,1)S(1)}, u32[]{:S(2)}, u32[]{:S(2)}) collective-permute-start(bf16[16,4224]{1,0:T(8,128)(2,1)} %get-tuple-element.114), channel_id=1, source_target_pairs={{0,16},{1,17},{2,18},{3,19},{4,20},{5,21},{6,22},{7,23},{8,24},{9,... | collective-permute-start | bytes 405512 | tf_op jit(solution)/shard_map/ppermute | solution.py:785
  8.0 10.8 %collective-permute-start.2 = (bf16[16,4224]{1,0:T(8,128)(2,1)}, bf16[16,4224]{1,0:T(8,128)(2,1)S(1)}, u32[]{:S(2)}, u32[]{:S(2)}) collective-permute-start(bf16[16,4224]{1,0:T(8,128)(2,1)} %get-tuple-element.114), channel_id=1, source_target_pairs={{0,24},{1,25},{2,26},{3,27},{4,28},{5,29},{6,30},{7,31},{8,16},{9,... | collective-permute-start | bytes 405512 | tf_op jit(solution)/shard_map/ppermute | solution.py:785
  8.0 10.9 %collective-permute-start.3 = (bf16[16,2048]{1,0:T(8,128)(2,1)}, bf16[16,2048]{1,0:T(8,128)(2,1)S(1)}, u32[]{:S(2)}, u32[]{:S(2)}) collective-permute-start(bf16[16,2048]{1,0:T(8,128)(2,1)} %get-tuple-element.108), channel_id=1, source_target_pairs={{0,2},{1,3},{2,0},{3,1},{4,6},{5,7},{6,4},{7,5},{8,10},{9,11},{10,... | collective-permute-start | bytes 196616 | tf_op jit(solution)/shard_map/ppermute | solution.py:785
  9.7 9.2 %collective-permute-start.4 = (bf16[16,2048]{1,0:T(8,128)(2,1)}, bf16[16,2048]{1,0:T(8,128)(2,1)S(1)}, u32[]{:S(2)}, u32[]{:S(2)}) collective-permute-start(bf16[16,2048]{1,0:T(8,128)(2,1)} %get-tuple-element.108), channel_id=1, source_target_pairs={{0,4},{1,5},{2,6},{3,7},{4,0},{5,1},{6,2},{7,3},{8,12},{9,13},{10,... | collective-permute-start | bytes 196616 | tf_op jit(solution)/shard_map/ppermute | solution.py:785
  12.1 6.9 %collective-permute-start.5 = (bf16[16,2048]{1,0:T(8,128)(2,1)}, bf16[16,2048]{1,0:T(8,128)(2,1)S(1)}, u32[]{:S(2)}, u32[]{:S(2)}) collective-permute-start(bf16[16,2048]{1,0:T(8,128)(2,1)} %get-tuple-element.108), channel_id=1, source_target_pairs={{0,6},{1,7},{2,4},{3,5},{4,2},{5,3},{6,0},{7,1},{8,14},{9,15},{10,... | collective-permute-start | bytes 196616 | tf_op jit(solution)/shard_map/ppermute | solution.py:785
  19.9 14.8 %collective-permute-start.6 = (bf16[4,16,2048]{2,1,0:T(8,128)(2,1)S(1)}, bf16[4,16,2048]{2,1,0:T(8,128)(2,1)S(1)}, u32[]{:S(2)}, u32[]{:S(2)}) collective-permute-start(bf16[4,16,2048]{2,1,0:T(8,128)(2,1)S(1)} %get-tuple-element.200), channel_id=1, source_target_pairs={{0,16},{1,17},{2,18},{3,19},{4,20},{5,21},{6,22},{7,23},{8,24},{9,... | collective-permute-start | bytes 786440 | tf_op jit(solution)/shard_map/ppermute | solution.py:785
  34.8 20.2 %collective-permute-start.10 = (bf16[4,16,2560]{2,1,0:T(8,128)(2,1)S(1)}, bf16[4,16,2560]{2,1,0:T(8,128)(2,1)S(1)}, u32[]{:S(2)}, u32[]{:S(2)}) collective-permute-start(bf16[4,16,2560]{2,1,0:T(8,128)(2,1)S(1)} %get-tuple-element.198), channel_id=1, source_target_pairs={{0,6},{1,7},{2,4},{3,5},{4,2},{5,3},{6,0},{7,1},{8,14},{9,15},{10,... | collective-permute-start | bytes 983048 | tf_op jit(solution)/shard_map/ppermute | solution.py:785
  36.6 18.5 %collective-permute-start.8 = (bf16[4,16,2560]{2,1,0:T(8,128)(2,1)S(1)}, bf16[4,16,2560]{2,1,0:T(8,128)(2,1)S(1)}, u32[]{:S(2)}, u32[]{:S(2)}) collective-permute-start(bf16[4,16,2560]{2,1,0:T(8,128)(2,1)S(1)} %get-tuple-element.198), channel_id=1, source_target_pairs={{0,2},{1,3},{2,0},{3,1},{4,6},{5,7},{6,4},{7,5},{8,10},{9,11},{10,... | collective-permute-start | bytes 983048 | tf_op jit(solution)/shard_map/ppermute | solution.py:785
  38.8 16.3 %collective-permute-start.9 = (bf16[4,16,2560]{2,1,0:T(8,128)(2,1)S(1)}, bf16[4,16,2560]{2,1,0:T(8,128)(2,1)S(1)}, u32[]{:S(2)}, u32[]{:S(2)}) collective-permute-start(bf16[4,16,2560]{2,1,0:T(8,128)(2,1)S(1)} %get-tuple-element.198), channel_id=1, source_target_pairs={{0,4},{1,5},{2,6},{3,7},{4,0},{5,1},{6,2},{7,3},{8,12},{9,13},{10,... | collective-permute-start | bytes 983048 | tf_op jit(solution)/shard_map/ppermute | solution.py:785
  38.8 16.2 %collective-permute-start.11 = (bf16[8,16,2048]{2,1,0:T(8,128)(2,1)S(1)}, bf16[8,16,2048]{2,1,0:T(8,128)(2,1)S(1)}, u32[]{:S(2)}, u32[]{:S(2)}) collective-permute-start(bf16[8,16,2048]{2,1,0:T(8,128)(2,1)S(1)} %bitcast.41), channel_id=1, source_target_pairs={{0,8},{1,9},{2,10},{3,11},{4,12},{5,13},{6,14},{7,15},{8,0},{9,1},... | collective-permute-start | bytes 1572872 | tf_op jit(solution)/shard_map/ppermute | solution.py:785
  55.3 4.6 %collective-permute-start.12 = (bf16[16,16,2560]{2,1,0:T(8,128)(2,1)S(1)}, bf16[16,16,2560]{2,1,0:T(8,128)(2,1)S(1)}, u32[]{:S(2)}, u32[]{:S(2)}) collective-permute-start(bf16[16,16,2560]{2,1,0:T(8,128)(2,1)S(1)} %bitcast.37), channel_id=1, source_target_pairs={{0,1},{1,0},{2,3},{3,2},{4,5},{5,4},{6,7},{7,6},{8,9},{9,8},{10,11... | collective-permute-start | bytes 3932168 | tf_op jit(solution)/shard_map/ppermute | solution.py:785
  76.2 5.5 %collective-permute-start.15 = (bf16[16,16,2048]{2,1,0:T(8,128)(2,1)S(1)}, bf16[16,16,2048]{2,1,0:T(8,128)(2,1)S(1)}, u32[]{:S(2)}, u32[]{:S(2)}) collective-permute-start(bf16[16,16,2048]{2,1,0:T(8,128)(2,1)S(1)} %get-tuple-element.133), channel_id=1, source_target_pairs={{0,1},{1,0},{2,3},{3,2},{4,5},{5,4},{6,7},{7,6},{8,9},{9,8},{10,11... | collective-permute-start | bytes 3145736 | tf_op jit(solution)/shard_map/ppermute | solution.py:785
  76.5 5.3 %collective-permute-start.14 = (bf16[16,16,2048]{2,1,0:T(8,128)(2,1)S(1)}, bf16[16,16,2048]{2,1,0:T(8,128)(2,1)S(1)}, u32[]{:S(2)}, u32[]{:S(2)}) collective-permute-start(bf16[16,16,2048]{2,1,0:T(8,128)(2,1)S(1)} %get-tuple-element.130), channel_id=1, source_target_pairs={{0,1},{1,0},{2,3},{3,2},{4,5},{5,4},{6,7},{7,6},{8,9},{9,8},{10,11... | collective-permute-start | bytes 3145736 | tf_op jit(solution)/shard_map/ppermute | solution.py:785
  82.2 30.3 %collective-permute-start.16 = (bf16[4,16,4096]{2,1,0:T(8,128)(2,1)S(1)}, bf16[4,16,4096]{2,1,0:T(8,128)(2,1)S(1)}, u32[]{:S(2)}, u32[]{:S(2)}) collective-permute-start(bf16[4,16,4096]{2,1,0:T(8,128)(2,1)S(1)} %get-tuple-element.142), channel_id=1, source_target_pairs={{0,2},{1,3},{2,0},{3,1},{4,6},{5,7},{6,4},{7,5},{8,10},{9,11},{10,... | collective-permute-start | bytes 1572872 | tf_op jit(solution)/shard_map/ppermute | solution.py:785
  84.2 28.3 %collective-permute-start.17 = (bf16[4,16,4096]{2,1,0:T(8,128)(2,1)S(1)}, bf16[4,16,4096]{2,1,0:T(8,128)(2,1)S(1)}, u32[]{:S(2)}, u32[]{:S(2)}) collective-permute-start(bf16[4,16,4096]{2,1,0:T(8,128)(2,1)S(1)} %get-tuple-element.143), channel_id=1, source_target_pairs={{0,4},{1,5},{2,6},{3,7},{4,0},{5,1},{6,2},{7,3},{8,12},{9,13},{10,... | collective-permute-start | bytes 1572872 | tf_op jit(solution)/shard_map/ppermute | solution.py:785
  84.3 28.2 %collective-permute-start.18 = (bf16[4,16,4096]{2,1,0:T(8,128)(2,1)S(1)}, bf16[4,16,4096]{2,1,0:T(8,128)(2,1)S(1)}, u32[]{:S(2)}, u32[]{:S(2)}) collective-permute-start(bf16[4,16,4096]{2,1,0:T(8,128)(2,1)S(1)} %get-tuple-element.144), channel_id=1, source_target_pairs={{0,6},{1,7},{2,4},{3,5},{4,2},{5,3},{6,0},{7,1},{8,14},{9,15},{10,... | collective-permute-start | bytes 1572872 | tf_op jit(solution)/shard_map/ppermute | solution.py:785
  112.8 15.3 %collective-permute-start.23 = (bf16[2,16,4096]{2,1,0:T(8,128)(2,1)S(1)}, bf16[2,16,4096]{2,1,0:T(8,128)(2,1)S(1)}, u32[]{:S(2)}, u32[]{:S(2)}) collective-permute-start(bf16[2,16,4096]{2,1,0:T(8,128)(2,1)S(1)} %get-tuple-element.176), channel_id=1, source_target_pairs={{0,16},{1,17},{2,18},{3,19},{4,20},{5,21},{6,22},{7,23},{8,24},{9,... | collective-permute-start | bytes 786440 | tf_op jit(solution)/shard_map/ppermute | solution.py:785
  115.5 12.5 %collective-permute-start.20 = (bf16[4,16,2176]{2,1,0:T(8,128)(2,1)S(1)}, bf16[4,16,2176]{2,1,0:T(8,128)(2,1)S(1)}, u32[]{:S(2)}, u32[]{:S(2)}) collective-permute-start(bf16[4,16,2176]{2,1,0:T(8,128)(2,1)S(1)} %get-tuple-element.173), channel_id=1, source_target_pairs={{0,2},{1,3},{2,0},{3,1},{4,6},{5,7},{6,4},{7,5},{8,10},{9,11},{10,... | collective-permute-start | bytes 835592 | tf_op jit(solution)/shard_map/ppermute | solution.py:785
  117.6 14.4 %collective-permute-start.21 = (bf16[4,16,2176]{2,1,0:T(8,128)(2,1)S(1)}, bf16[4,16,2176]{2,1,0:T(8,128)(2,1)S(1)}, u32[]{:S(2)}, u32[]{:S(2)}) collective-permute-start(bf16[4,16,2176]{2,1,0:T(8,128)(2,1)S(1)} %get-tuple-element.174), channel_id=1, source_target_pairs={{0,4},{1,5},{2,6},{3,7},{4,0},{5,1},{6,2},{7,3},{8,12},{9,13},{10,... | collective-permute-start | bytes 835592 | tf_op jit(solution)/shard_map/ppermute | solution.py:785
  117.7 14.3 %collective-permute-start.22 = (bf16[4,16,2176]{2,1,0:T(8,128)(2,1)S(1)}, bf16[4,16,2176]{2,1,0:T(8,128)(2,1)S(1)}, u32[]{:S(2)}, u32[]{:S(2)}) collective-permute-start(bf16[4,16,2176]{2,1,0:T(8,128)(2,1)S(1)} %get-tuple-element.175), channel_id=1, source_target_pairs={{0,6},{1,7},{2,4},{3,5},{4,2},{5,3},{6,0},{7,1},{8,14},{9,15},{10,... | collective-permute-start | bytes 835592 | tf_op jit(solution)/shard_map/ppermute | solution.py:785
  132.1 10.5 %collective-permute-start.24 = (bf16[1,16,6272]{2,1,0:T(8,128)(2,1)S(1)}, bf16[1,16,6272]{2,1,0:T(8,128)(2,1)S(1)}, u32[]{:S(2)}, u32[]{:S(2)}) collective-permute-start(bf16[1,16,6272]{2,1,0:T(8,128)(2,1)S(1)} %get-tuple-element.184), channel_id=1, source_target_pairs={{0,8},{1,9},{2,10},{3,11},{4,12},{5,13},{6,14},{7,15},{8,0},{9,1},... | collective-permute-start | bytes 602120 | tf_op jit(solution)/shard_map/ppermute | solution.py:785
  134.2 6.0 %collective-permute-start.25 = (bf16[1,16,2176]{2,1,0:T(8,128)(2,1)S(1)}, bf16[1,16,2176]{2,1,0:T(8,128)(2,1)S(1)}, u32[]{:S(2)}, u32[]{:S(2)}) collective-permute-start(bf16[1,16,2176]{2,1,0:T(8,128)(2,1)S(1)} %get-tuple-element.185), channel_id=1, source_target_pairs={{0,16},{1,17},{2,18},{3,19},{4,20},{5,21},{6,22},{7,23},{8,24},{9,... | collective-permute-start | bytes 208904 | tf_op jit(solution)/shard_map/ppermute | solution.py:785
  134.8 7.8 %collective-permute-start.26 = (bf16[1,16,2176]{2,1,0:T(8,128)(2,1)S(1)}, bf16[1,16,2176]{2,1,0:T(8,128)(2,1)S(1)}, u32[]{:S(2)}, u32[]{:S(2)}) collective-permute-start(bf16[1,16,2176]{2,1,0:T(8,128)(2,1)S(1)} %get-tuple-element.186), channel_id=1, source_target_pairs={{0,24},{1,25},{2,26},{3,27},{4,28},{5,29},{6,30},{7,31},{8,16},{9,... | collective-permute-start | bytes 208904 | tf_op jit(solution)/shard_map/ppermute | solution.py:785
  (7 other events, 47.7 us)

commit v4 on v3

--- a/solution.py
+++ b/solution.py
@@ -207,12 +207,12 @@
     key_aux_out[...] = key_side
 
     def norm_block(index, carry):
-        span = pl.ds(pl.multiple_of(index * 256, 256), 256)
+        span = block_of(index, 512)
         centred, scale = row_stats(tokens[span, :].astype(F32))
         normed_out[span, :] = (centred * scale * smalls[0:1, :] + smalls[2:3, :]).astype(BF)
         return carry
 
-    lax.fori_loop(0, tokens.shape[0] // 256, norm_block, 0)
+    lax.fori_loop(0, tokens.shape[0] // 512, norm_block, 0)
     normed = normed_out[...]
     normed_t[0:512, :] = normed.T
     ones_row = lax.broadcasted_iota(jnp.int32, (16, normed.shape[0]), 0) == 0
@@ -328,7 +328,7 @@
             span = slice(512 * part, 512 * part + 512)
             down[pl.ds(row, 16), :] = source[4 * TALL_ORDER[i] + j, :, span]
     rows = tokens.shape[0]
-    block = 256
+    block = 512
 
     def ahead(index, carry):
         span = pl.ds(pl.multiple_of(index * block, block), block)

time: 144 us -> 143 us (level)
  no operation moved by 1% of the time
where the time goes in v4:
time: 143 us
  Pallas kernels  73.2 us (51%)
  starting transfers between devices  32.5 us (23%)
  waiting for transfers between devices  22.1 us (15%)
  blocking collectives  11.6 us (8%)
    ppermute x27, starting transfers between devices, swap(): return lax.ppermute(value, AXES, [(d, d ^ mask) for d in range(count)])  32.5 us
    pallas_call x1, Pallas kernels, backward(): pl.pallas_call(backward_kernel, grid=(4,), in_specs=[smem()] + parts + [p...  26.7 us
    ppermute x27, waiting for transfers between devices, swap(): return lax.ppermute(value, AXES, [(d, d ^ mask) for d in range(count)])  22.1 us
    pallas_call x1, Pallas kernels, forward(): pl.pallas_call(forward_kernel, in_specs=[smem()] + [vmem()] * 4, out_spec...  15.7 us
    pallas_call x1, Pallas kernels, feed_first(): pl.pallas_call(feed_first_kernel, in_specs=[smem()] + [vmem()] * 9, out_s...  12.3 us
    all_gather x1, blocking collectives, body(): a_mine = lax.all_gather(after(a_col, c_plane), 'plane').reshape(16, 16, -1)  11.6 us
    pallas_call x1, Pallas kernels, input_terms(): pl.pallas_call(input_kernel, in_specs=[vmem()] * 8, out_specs=[vmem()] *...  6.4 us
    pallas_call x1, Pallas kernels, feed_third(): pl.pallas_call(feed_third_kernel, in_specs=[vmem()] * 7, out_specs=[vmem(...  4.92 us
  transfers between devices with their start and end apart: 27, of which 7 were waited for; matrix products, arithmetic and copies ran while one was open for 1% of the time, Pallas kernels for 38%

profile of v4, /device:TPU:0, one launch (start us, length us, event | category | flops | bytes accessed | tf_op | source)
XLA Modules:
  0.0 142.6 jit_solution(3912012838857143569)
XLA Ops:
  0.6 1.8 %pack.1 = (bf16[16,4224]{1,0:T(8,128)(2,1)}, bf16[16,2048]{1,0:T(8,128)(2,1)}) custom-call(bf16[16,1536]{1,0:T(8,128)(2,1)} %qkv.1, bf16[16,512]{1,0:T(8,128)(2,1)} %mix.1, bf16[16,2048]{1,0:T(8,128)(2,1)} %up.1, bf16[64,512]{1,0:T(8,128)(2,1)} %down.1, bf16[2,16]{1,0:T(2,128)(2,1)} %gain.1, bf16[2,16]{1,0:T(2,128)(2,1)} %shift.1, bf16[2,16]{1,0:T(2,128)(2,1)} %qv.1, ...), custom_call_target="tpu_custom_call" | custom-call | flops 1650000000 | tf_op jit(solution)/shard_map/pack/pallas_call | solution.py:98
  2.4 3.0 %collective-permute-start = (bf16[16,4224]{1,0:T(8,128)(2,1)}, bf16[16,4224]{1,0:T(8,128)(2,1)S(1)}, u32[]{:S(2)}, u32[]{:S(2)}) collective-permute-start(bf16[16,4224]{1,0:T(8,128)(2,1)} %get-tuple-element.114), channel_id=1, source_target_pairs={{0,8},{1,9},{2,10},{3,11},{4,12},{5,13},{6,14},{7,15},{8,0},{9,1},... | collective-permute-start | bytes 405512 | tf_op jit(solution)/shard_map/ppermute | solution.py:785
  5.4 2.6 %collective-permute-start.1 = (bf16[16,4224]{1,0:T(8,128)(2,1)}, bf16[16,4224]{1,0:T(8,128)(2,1)S(1)}, u32[]{:S(2)}, u32[]{:S(2)}) collective-permute-start(bf16[16,4224]{1,0:T(8,128)(2,1)} %get-tuple-element.114), channel_id=1, source_target_pairs={{0,16},{1,17},{2,18},{3,19},{4,20},{5,21},{6,22},{7,23},{8,24},{9,... | collective-permute-start | bytes 405512 | tf_op jit(solution)/shard_map/ppermute | solution.py:785
  13.6 5.3 %collective-permute-done.1 = bf16[16,4224]{1,0:T(8,128)(2,1)S(1)} collective-permute-done((bf16[16,4224]{1,0:T(8,128)(2,1)}, bf16[16,4224]{1,0:T(8,128)(2,1)S(1)}, u32[]{:S(2)}, u32[]{:S(2)}) %collective-permute-start.1) | collective-permute-done | bytes 135200 | tf_op jit(solution)/shard_map/ppermute | solution.py:785
  19.9 3.1 %collective-permute-start.6 = (bf16[4,16,2048]{2,1,0:T(8,128)(2,1)S(1)}, bf16[4,16,2048]{2,1,0:T(8,128)(2,1)S(1)}, u32[]{:S(2)}, u32[]{:S(2)}) collective-permute-start(bf16[4,16,2048]{2,1,0:T(8,128)(2,1)S(1)} %get-tuple-element.200), channel_id=1, source_target_pairs={{0,16},{1,17},{2,18},{3,19},{4,20},{5,21},{6,22},{7,23},{8,24},{9,... | collective-permute-start | bytes 786440 | tf_op jit(solution)/shard_map/ppermute | solution.py:785
  23.0 11.6 %all-gather.mine = bf16[16,16,1664]{2,1,0:T(8,128)(2,1)S(1)} all-gather(bf16[4,16,1664]{2,1,0:T(8,128)(2,1)S(1)} %pad_maximum_fusion.5), channel_id=2, replica_groups=mesh['dp'=4,'plane'=4,'core'=2] {'plane'}, dimensions={0}, use_global_device_ids=true | all-gather | bytes 1064960 | tf_op jit(solution)/shard_map/all_gather | solution.py:852
  34.8 1.7 %collective-permute-start.10 = (bf16[4,16,2560]{2,1,0:T(8,128)(2,1)S(1)}, bf16[4,16,2560]{2,1,0:T(8,128)(2,1)S(1)}, u32[]{:S(2)}, u32[]{:S(2)}) collective-permute-start(bf16[4,16,2560]{2,1,0:T(8,128)(2,1)S(1)} %get-tuple-element.198), channel_id=1, source_target_pairs={{0,6},{1,7},{2,4},{3,5},{4,2},{5,3},{6,0},{7,1},{8,14},{9,15},{10,... | collective-permute-start | bytes 983048 | tf_op jit(solution)/shard_map/ppermute | solution.py:785
  36.6 2.2 %collective-permute-start.8 = (bf16[4,16,2560]{2,1,0:T(8,128)(2,1)S(1)}, bf16[4,16,2560]{2,1,0:T(8,128)(2,1)S(1)}, u32[]{:S(2)}, u32[]{:S(2)}) collective-permute-start(bf16[4,16,2560]{2,1,0:T(8,128)(2,1)S(1)} %get-tuple-element.198), channel_id=1, source_target_pairs={{0,2},{1,3},{2,0},{3,1},{4,6},{5,7},{6,4},{7,5},{8,10},{9,11},{10,... | collective-permute-start | bytes 983048 | tf_op jit(solution)/shard_map/ppermute | solution.py:785
  39.0 15.7 %attend.1 = (bf16[4,3,1024,128]{3,2,1,0:T(8,128)(2,1)S(1)}, bf16[528,1024]{1,0:T(8,128)(2,1)S(1)}, bf16[512,1536]{1,0:T(8,128)(2,1)S(1)}, bf16[1024,512]{1,0:T(8...) custom-call(s32[2]{0:T(128)S(1)} %pad_add_fusion.me_ref, ...), custom_call_target="tpu_custom_call" | custom-call | flops 16499999744 | tf_op jit(solution)/shard_map/attend/pallas_call | solution.py:250
  55.7 3.9 %collective-permute-done.13.other_tall = bf16[16,16,2048]{2,1,0:T(8,128)(2,1)S(1)} collective-permute-done((bf16[16,16,2048]{2,1,0:T(8,128)(2,1)S(1)}, bf16[16,16,2048]{2,1,0:T(8,128)(2,1)S(1)}, u32[]{:S(2)}, u32[]{:S(2)}) %collective-permute-start.13) | collective-permute-done | bytes 1048608 | tf_op jit(solution)/shard_map/ppermute | solution.py:785
  59.6 12.3 %feed_first.1 = (f32[1024,512]{1,0:T(8,128)S(1)}, bf16[528,1024]{1,0:T(8,128)(2,1)S(1)}, bf16[1024,2048]{1,0:T(8,128)(2,1)S(1)}, bf16[16,16,2048]{2,1,0:T(8,128)...) custom-call(s32[2]{0:T(128)S(1)} %pad_add_fusion.me_ref, ...), custom_call_target="tpu_custom_call" | custom-call | flops 19800000512 | tf_op jit(solution)/shard_map/feed_first/pallas_call | solution.py:363
  71.9 3.6 %feed_second.1 = (bf16[16,16,2048]{2,1,0:T(8,128)(2,1)S(1)}, f32[16,16,2048]{2,1,0:T(8,128)S(1)}, f32[1,2048]{1,0:T(1,128)S(1)}) custom-call(s32[2]{0:T(128)S(1)} %pad_add_fusion.me_ref, bf16[528,1024]{1,0:T(8,128)(2,1)S(1)} %get-tuple-element.131.normed_t, bf16[1024,2048]{1,0:T(8,128)(2,1)S(1)} %get-tuple-element.132.grad_pre), custom_call_target="tpu_custom_call" | custom-call | flops 5500000256 | tf_op jit(solution)/shard_map/feed_second/pallas_call | solution.py:403
  76.0 4.9 %feed_third.1 = (f32[1024,512]{1,0:T(8,128)S(1)}, bf16[1024,512]{1,0:T(8,128)(2,1)S(1)}, f32[512,512]{1,0:T(8,128)S(1)}, f32[8,512]{1,0:T(8,128)S(1)}) custom-call(f32[1024,512]{1,0:T(8,128)S(1)} %get-tuple-element.134.middle, bf16[1024,2048]{1,0:T(8,128)(2,1)S(1)} %get-tuple-element.132.grad_pre, bf16[512,512]{1,0:T(8,128)(2,1)S(1)} %get-tuple-element.135.mix, ...), custom_call_target="tpu_custom_call" | custom-call | flops 8800000000 | tf_op jit(solution)/shard_map/feed_third/pallas_call | solution.py:461
  81.4 2.0 %collective-permute-start.16 = (bf16[4,16,4096]{2,1,0:T(8,128)(2,1)S(1)}, bf16[4,16,4096]{2,1,0:T(8,128)(2,1)S(1)}, u32[]{:S(2)}, u32[]{:S(2)}) collective-permute-start(bf16[4,16,4096]{2,1,0:T(8,128)(2,1)S(1)} %get-tuple-element.142), channel_id=1, source_target_pairs={{0,2},{1,3},{2,0},{3,1},{4,6},{5,7},{6,4},{7,5},{8,10},{9,11},{10,... | collective-permute-start | bytes 1572872 | tf_op jit(solution)/shard_map/ppermute | solution.py:785
  84.9 26.7 %attend_back.1 = (bf16[1024,1536]{1,0:T(8,128)(2,1)S(1)}, bf16[16,16,2176]{2,1,0:T(8,128)(2,1)S(1)}, f32[16,16,2176]{2,1,0:T(8,128)S(1)}) custom-call(s32[2]{0:T(128)S(1)} %pad_add_fusion.me_ref, bf16[4,3,1024,128]{3,2,1,0:T(8,128)(2,1)S(1)} %get-tuple-element.145.q.k.v, bf16[4,3,1024,128]{3,2,1,0:T(8,128)(2,1)S(1)} %get-tuple-element.145.q.k.v, ...), custom_call_target="tpu_custom_call" | custom-call | flops 27499999232 | tf_op jit(solution)/shard_map/attend_back/pallas_call | solution.py:604
  112.0 2.0 %collective-permute-start.23 = (bf16[2,16,4096]{2,1,0:T(8,128)(2,1)S(1)}, bf16[2,16,4096]{2,1,0:T(8,128)(2,1)S(1)}, u32[]{:S(2)}, u32[]{:S(2)}) collective-permute-start(bf16[2,16,4096]{2,1,0:T(8,128)(2,1)S(1)} %get-tuple-element.176), channel_id=1, source_target_pairs={{0,16},{1,17},{2,18},{3,19},{4,20},{5,21},{6,22},{7,23},{8,24},{9,... | collective-permute-start | bytes 786440 | tf_op jit(solution)/shard_map/ppermute | solution.py:785
  114.7 2.0 %collective-permute-start.20 = (bf16[4,16,2176]{2,1,0:T(8,128)(2,1)S(1)}, bf16[4,16,2176]{2,1,0:T(8,128)(2,1)S(1)}, u32[]{:S(2)}, u32[]{:S(2)}) collective-permute-start(bf16[4,16,2176]{2,1,0:T(8,128)(2,1)S(1)} %get-tuple-element.173), channel_id=1, source_target_pairs={{0,2},{1,3},{2,0},{3,1},{4,6},{5,7},{6,4},{7,5},{8,10},{9,11},{10,... | collective-permute-start | bytes 835592 | tf_op jit(solution)/shard_map/ppermute | solution.py:785
  118.3 6.4 %input_terms.1 = (f32[1024,512]{1,0:T(8,128)}, bf16[1024,512]{1,0:T(8,128)(2,1)}) custom-call(bf16[1024,512]{1,0:T(8,128)(2,1)S(1)} %copy-done.1, bf16[1024,1536]{1,0:T(8,128)(2,1)S(1)} %get-tuple-element.159.gm, bf16[512,1536]{1,0:T(8,128)(2,1)S(1)} %get-tuple-element.150.weight, f32[8,512]{1,0:T(8,128)S(1)} %get-tuple-element.168.smalls, ...), custom_call_target="tpu_custom_call" | custom-call | flops 8800000000 | tf_op jit(solution)/shard_map/input_terms/pallas_call | solution.py:664
  124.7 2.5 %collective-permute-done.23.du_recv = bf16[2,16,4096]{2,1,0:T(8,128)(2,1)S(1)} collective-permute-done((bf16[2,16,4096]{2,1,0:T(8,128)(2,1)S(1)}, bf16[2,16,4096]{2,1,0:T(8,128)(2,1)S(1)}, u32[]{:S(2)}, u32[]{:S(2)}) %collective-permute-start.23) | collective-permute-done | bytes 262176 | tf_op jit(solution)/shard_map/ppermute | solution.py:785
  127.3 3.9 %collective-permute-done.21.g1 = bf16[4,16,2176]{2,1,0:T(8,128)(2,1)S(1)} collective-permute-done((bf16[4,16,2176]{2,1,0:T(8,128)(2,1)S(1)}, bf16[4,16,2176]{2,1,0:T(8,128)(2,1)S(1)}, u32[]{:S(2)}, u32[]{:S(2)}) %collective-permute-start.21) | collective-permute-done | bytes 278560 | tf_op jit(solution)/shard_map/ppermute | solution.py:785
  131.4 2.1 %collective-permute-start.24 = (bf16[1,16,6272]{2,1,0:T(8,128)(2,1)S(1)}, bf16[1,16,6272]{2,1,0:T(8,128)(2,1)S(1)}, u32[]{:S(2)}, u32[]{:S(2)}) collective-permute-start(bf16[1,16,6272]{2,1,0:T(8,128)(2,1)S(1)} %get-tuple-element.184), channel_id=1, source_target_pairs={{0,8},{1,9},{2,10},{3,11},{4,12},{5,13},{6,14},{7,15},{8,0},{9,1},... | collective-permute-start | bytes 602120 | tf_op jit(solution)/shard_map/ppermute | solution.py:785
  134.0 1.9 %collective-permute-start.26 = (bf16[1,16,2176]{2,1,0:T(8,128)(2,1)S(1)}, bf16[1,16,2176]{2,1,0:T(8,128)(2,1)S(1)}, u32[]{:S(2)}, u32[]{:S(2)}) collective-permute-start(bf16[1,16,2176]{2,1,0:T(8,128)(2,1)S(1)} %get-tuple-element.186), channel_id=1, source_target_pairs={{0,24},{1,25},{2,26},{3,27},{4,28},{5,29},{6,30},{7,31},{8,16},{9,... | collective-permute-start | bytes 208904 | tf_op jit(solution)/shard_map/ppermute | solution.py:785
  135.9 3.5 %collective-permute-done.25.r1 = bf16[1,16,2176]{2,1,0:T(8,128)(2,1)S(1)} collective-permute-done((bf16[1,16,2176]{2,1,0:T(8,128)(2,1)S(1)}, bf16[1,16,2176]{2,1,0:T(8,128)(2,1)S(1)}, u32[]{:S(2)}, u32[]{:S(2)}) %collective-permute-start.25) | collective-permute-done | bytes 69664 | tf_op jit(solution)/shard_map/ppermute | solution.py:785
  139.4 2.4 %collective-permute-done.26.r2 = bf16[1,16,2176]{2,1,0:T(8,128)(2,1)S(1)} collective-permute-done((bf16[1,16,2176]{2,1,0:T(8,128)(2,1)S(1)}, bf16[1,16,2176]{2,1,0:T(8,128)(2,1)S(1)}, u32[]{:S(2)}, u32[]{:S(2)}) %collective-permute-start.26) | collective-permute-done | bytes 69664 | tf_op jit(solution)/shard_map/ppermute | solution.py:785
  (65 shorter events, 14.5 us)
Async XLA Ops:
  2.4 9.7 %collective-permute-start = (bf16[16,4224]{1,0:T(8,128)(2,1)}, bf16[16,4224]{1,0:T(8,128)(2,1)S(1)}, u32[]{:S(2)}, u32[]{:S(2)}) collective-permute-start(bf16[16,4224]{1,0:T(8,128)(2,1)} %get-tuple-element.114), channel_id=1, source_target_pairs={{0,8},{1,9},{2,10},{3,11},{4,12},{5,13},{6,14},{7,15},{8,0},{9,1},... | collective-permute-start | bytes 405512 | tf_op jit(solution)/shard_map/ppermute | solution.py:785
  5.4 13.4 %collective-permute-start.1 = (bf16[16,4224]{1,0:T(8,128)(2,1)}, bf16[16,4224]{1,0:T(8,128)(2,1)S(1)}, u32[]{:S(2)}, u32[]{:S(2)}) collective-permute-start(bf16[16,4224]{1,0:T(8,128)(2,1)} %get-tuple-element.114), channel_id=1, source_target_pairs={{0,16},{1,17},{2,18},{3,19},{4,20},{5,21},{6,22},{7,23},{8,24},{9,... | collective-permute-start | bytes 405512 | tf_op jit(solution)/shard_map/ppermute | solution.py:785
  8.0 10.8 %collective-permute-start.2 = (bf16[16,4224]{1,0:T(8,128)(2,1)}, bf16[16,4224]{1,0:T(8,128)(2,1)S(1)}, u32[]{:S(2)}, u32[]{:S(2)}) collective-permute-start(bf16[16,4224]{1,0:T(8,128)(2,1)} %get-tuple-element.114), channel_id=1, source_target_pairs={{0,24},{1,25},{2,26},{3,27},{4,28},{5,29},{6,30},{7,31},{8,16},{9,... | collective-permute-start | bytes 405512 | tf_op jit(solution)/shard_map/ppermute | solution.py:785
  8.0 10.9 %collective-permute-start.3 = (bf16[16,2048]{1,0:T(8,128)(2,1)}, bf16[16,2048]{1,0:T(8,128)(2,1)S(1)}, u32[]{:S(2)}, u32[]{:S(2)}) collective-permute-start(bf16[16,2048]{1,0:T(8,128)(2,1)} %get-tuple-element.108), channel_id=1, source_target_pairs={{0,2},{1,3},{2,0},{3,1},{4,6},{5,7},{6,4},{7,5},{8,10},{9,11},{10,... | collective-permute-start | bytes 196616 | tf_op jit(solution)/shard_map/ppermute | solution.py:785
  9.7 9.2 %collective-permute-start.4 = (bf16[16,2048]{1,0:T(8,128)(2,1)}, bf16[16,2048]{1,0:T(8,128)(2,1)S(1)}, u32[]{:S(2)}, u32[]{:S(2)}) collective-permute-start(bf16[16,2048]{1,0:T(8,128)(2,1)} %get-tuple-element.108), channel_id=1, source_target_pairs={{0,4},{1,5},{2,6},{3,7},{4,0},{5,1},{6,2},{7,3},{8,12},{9,13},{10,... | collective-permute-start | bytes 196616 | tf_op jit(solution)/shard_map/ppermute | solution.py:785
  12.1 6.9 %collective-permute-start.5 = (bf16[16,2048]{1,0:T(8,128)(2,1)}, bf16[16,2048]{1,0:T(8,128)(2,1)S(1)}, u32[]{:S(2)}, u32[]{:S(2)}) collective-permute-start(bf16[16,2048]{1,0:T(8,128)(2,1)} %get-tuple-element.108), channel_id=1, source_target_pairs={{0,6},{1,7},{2,4},{3,5},{4,2},{5,3},{6,0},{7,1},{8,14},{9,15},{10,... | collective-permute-start | bytes 196616 | tf_op jit(solution)/shard_map/ppermute | solution.py:785
  19.9 14.8 %collective-permute-start.6 = (bf16[4,16,2048]{2,1,0:T(8,128)(2,1)S(1)}, bf16[4,16,2048]{2,1,0:T(8,128)(2,1)S(1)}, u32[]{:S(2)}, u32[]{:S(2)}) collective-permute-start(bf16[4,16,2048]{2,1,0:T(8,128)(2,1)S(1)} %get-tuple-element.200), channel_id=1, source_target_pairs={{0,16},{1,17},{2,18},{3,19},{4,20},{5,21},{6,22},{7,23},{8,24},{9,... | collective-permute-start | bytes 786440 | tf_op jit(solution)/shard_map/ppermute | solution.py:785
  34.8 19.9 %collective-permute-start.10 = (bf16[4,16,2560]{2,1,0:T(8,128)(2,1)S(1)}, bf16[4,16,2560]{2,1,0:T(8,128)(2,1)S(1)}, u32[]{:S(2)}, u32[]{:S(2)}) collective-permute-start(bf16[4,16,2560]{2,1,0:T(8,128)(2,1)S(1)} %get-tuple-element.198), channel_id=1, source_target_pairs={{0,6},{1,7},{2,4},{3,5},{4,2},{5,3},{6,0},{7,1},{8,14},{9,15},{10,... | collective-permute-start | bytes 983048 | tf_op jit(solution)/shard_map/ppermute | solution.py:785
  36.6 18.2 %collective-permute-start.8 = (bf16[4,16,2560]{2,1,0:T(8,128)(2,1)S(1)}, bf16[4,16,2560]{2,1,0:T(8,128)(2,1)S(1)}, u32[]{:S(2)}, u32[]{:S(2)}) collective-permute-start(bf16[4,16,2560]{2,1,0:T(8,128)(2,1)S(1)} %get-tuple-element.198), channel_id=1, source_target_pairs={{0,2},{1,3},{2,0},{3,1},{4,6},{5,7},{6,4},{7,5},{8,10},{9,11},{10,... | collective-permute-start | bytes 983048 | tf_op jit(solution)/shard_map/ppermute | solution.py:785
  38.8 16.0 %collective-permute-start.9 = (bf16[4,16,2560]{2,1,0:T(8,128)(2,1)S(1)}, bf16[4,16,2560]{2,1,0:T(8,128)(2,1)S(1)}, u32[]{:S(2)}, u32[]{:S(2)}) collective-permute-start(bf16[4,16,2560]{2,1,0:T(8,128)(2,1)S(1)} %get-tuple-element.198), channel_id=1, source_target_pairs={{0,4},{1,5},{2,6},{3,7},{4,0},{5,1},{6,2},{7,3},{8,12},{9,13},{10,... | collective-permute-start | bytes 983048 | tf_op jit(solution)/shard_map/ppermute | solution.py:785
  38.8 15.9 %collective-permute-start.11 = (bf16[8,16,2048]{2,1,0:T(8,128)(2,1)S(1)}, bf16[8,16,2048]{2,1,0:T(8,128)(2,1)S(1)}, u32[]{:S(2)}, u32[]{:S(2)}) collective-permute-start(bf16[8,16,2048]{2,1,0:T(8,128)(2,1)S(1)} %bitcast.41), channel_id=1, source_target_pairs={{0,8},{1,9},{2,10},{3,11},{4,12},{5,13},{6,14},{7,15},{8,0},{9,1},... | collective-permute-start | bytes 1572872 | tf_op jit(solution)/shard_map/ppermute | solution.py:785
  55.0 4.6 %collective-permute-start.12 = (bf16[16,16,2560]{2,1,0:T(8,128)(2,1)S(1)}, bf16[16,16,2560]{2,1,0:T(8,128)(2,1)S(1)}, u32[]{:S(2)}, u32[]{:S(2)}) collective-permute-start(bf16[16,16,2560]{2,1,0:T(8,128)(2,1)S(1)} %bitcast.37), channel_id=1, source_target_pairs={{0,1},{1,0},{2,3},{3,2},{4,5},{5,4},{6,7},{7,6},{8,9},{9,8},{10,11... | collective-permute-start | bytes 3932168 | tf_op jit(solution)/shard_map/ppermute | solution.py:785
  75.4 5.5 %collective-permute-start.15 = (bf16[16,16,2048]{2,1,0:T(8,128)(2,1)S(1)}, bf16[16,16,2048]{2,1,0:T(8,128)(2,1)S(1)}, u32[]{:S(2)}, u32[]{:S(2)}) collective-permute-start(bf16[16,16,2048]{2,1,0:T(8,128)(2,1)S(1)} %get-tuple-element.133), channel_id=1, source_target_pairs={{0,1},{1,0},{2,3},{3,2},{4,5},{5,4},{6,7},{7,6},{8,9},{9,8},{10,11... | collective-permute-start | bytes 3145736 | tf_op jit(solution)/shard_map/ppermute | solution.py:785
  75.7 5.3 %collective-permute-start.14 = (bf16[16,16,2048]{2,1,0:T(8,128)(2,1)S(1)}, bf16[16,16,2048]{2,1,0:T(8,128)(2,1)S(1)}, u32[]{:S(2)}, u32[]{:S(2)}) collective-permute-start(bf16[16,16,2048]{2,1,0:T(8,128)(2,1)S(1)} %get-tuple-element.130), channel_id=1, source_target_pairs={{0,1},{1,0},{2,3},{3,2},{4,5},{5,4},{6,7},{7,6},{8,9},{9,8},{10,11... | collective-permute-start | bytes 3145736 | tf_op jit(solution)/shard_map/ppermute | solution.py:785
  81.4 30.3 %collective-permute-start.16 = (bf16[4,16,4096]{2,1,0:T(8,128)(2,1)S(1)}, bf16[4,16,4096]{2,1,0:T(8,128)(2,1)S(1)}, u32[]{:S(2)}, u32[]{:S(2)}) collective-permute-start(bf16[4,16,4096]{2,1,0:T(8,128)(2,1)S(1)} %get-tuple-element.142), channel_id=1, source_target_pairs={{0,2},{1,3},{2,0},{3,1},{4,6},{5,7},{6,4},{7,5},{8,10},{9,11},{10,... | collective-permute-start | bytes 1572872 | tf_op jit(solution)/shard_map/ppermute | solution.py:785
  83.4 28.3 %collective-permute-start.17 = (bf16[4,16,4096]{2,1,0:T(8,128)(2,1)S(1)}, bf16[4,16,4096]{2,1,0:T(8,128)(2,1)S(1)}, u32[]{:S(2)}, u32[]{:S(2)}) collective-permute-start(bf16[4,16,4096]{2,1,0:T(8,128)(2,1)S(1)} %get-tuple-element.143), channel_id=1, source_target_pairs={{0,4},{1,5},{2,6},{3,7},{4,0},{5,1},{6,2},{7,3},{8,12},{9,13},{10,... | collective-permute-start | bytes 1572872 | tf_op jit(solution)/shard_map/ppermute | solution.py:785
  83.5 28.2 %collective-permute-start.18 = (bf16[4,16,4096]{2,1,0:T(8,128)(2,1)S(1)}, bf16[4,16,4096]{2,1,0:T(8,128)(2,1)S(1)}, u32[]{:S(2)}, u32[]{:S(2)}) collective-permute-start(bf16[4,16,4096]{2,1,0:T(8,128)(2,1)S(1)} %get-tuple-element.144), channel_id=1, source_target_pairs={{0,6},{1,7},{2,4},{3,5},{4,2},{5,3},{6,0},{7,1},{8,14},{9,15},{10,... | collective-permute-start | bytes 1572872 | tf_op jit(solution)/shard_map/ppermute | solution.py:785
  112.0 15.3 %collective-permute-start.23 = (bf16[2,16,4096]{2,1,0:T(8,128)(2,1)S(1)}, bf16[2,16,4096]{2,1,0:T(8,128)(2,1)S(1)}, u32[]{:S(2)}, u32[]{:S(2)}) collective-permute-start(bf16[2,16,4096]{2,1,0:T(8,128)(2,1)S(1)} %get-tuple-element.176), channel_id=1, source_target_pairs={{0,16},{1,17},{2,18},{3,19},{4,20},{5,21},{6,22},{7,23},{8,24},{9,... | collective-permute-start | bytes 786440 | tf_op jit(solution)/shard_map/ppermute | solution.py:785
  114.7 12.5 %collective-permute-start.20 = (bf16[4,16,2176]{2,1,0:T(8,128)(2,1)S(1)}, bf16[4,16,2176]{2,1,0:T(8,128)(2,1)S(1)}, u32[]{:S(2)}, u32[]{:S(2)}) collective-permute-start(bf16[4,16,2176]{2,1,0:T(8,128)(2,1)S(1)} %get-tuple-element.173), channel_id=1, source_target_pairs={{0,2},{1,3},{2,0},{3,1},{4,6},{5,7},{6,4},{7,5},{8,10},{9,11},{10,... | collective-permute-start | bytes 835592 | tf_op jit(solution)/shard_map/ppermute | solution.py:785
  116.8 14.4 %collective-permute-start.21 = (bf16[4,16,2176]{2,1,0:T(8,128)(2,1)S(1)}, bf16[4,16,2176]{2,1,0:T(8,128)(2,1)S(1)}, u32[]{:S(2)}, u32[]{:S(2)}) collective-permute-start(bf16[4,16,2176]{2,1,0:T(8,128)(2,1)S(1)} %get-tuple-element.174), channel_id=1, source_target_pairs={{0,4},{1,5},{2,6},{3,7},{4,0},{5,1},{6,2},{7,3},{8,12},{9,13},{10,... | collective-permute-start | bytes 835592 | tf_op jit(solution)/shard_map/ppermute | solution.py:785
  116.9 14.3 %collective-permute-start.22 = (bf16[4,16,2176]{2,1,0:T(8,128)(2,1)S(1)}, bf16[4,16,2176]{2,1,0:T(8,128)(2,1)S(1)}, u32[]{:S(2)}, u32[]{:S(2)}) collective-permute-start(bf16[4,16,2176]{2,1,0:T(8,128)(2,1)S(1)} %get-tuple-element.175), channel_id=1, source_target_pairs={{0,6},{1,7},{2,4},{3,5},{4,2},{5,3},{6,0},{7,1},{8,14},{9,15},{10,... | collective-permute-start | bytes 835592 | tf_op jit(solution)/shard_map/ppermute | solution.py:785
  131.4 10.5 %collective-permute-start.24 = (bf16[1,16,6272]{2,1,0:T(8,128)(2,1)S(1)}, bf16[1,16,6272]{2,1,0:T(8,128)(2,1)S(1)}, u32[]{:S(2)}, u32[]{:S(2)}) collective-permute-start(bf16[1,16,6272]{2,1,0:T(8,128)(2,1)S(1)} %get-tuple-element.184), channel_id=1, source_target_pairs={{0,8},{1,9},{2,10},{3,11},{4,12},{5,13},{6,14},{7,15},{8,0},{9,1},... | collective-permute-start | bytes 602120 | tf_op jit(solution)/shard_map/ppermute | solution.py:785
  133.4 6.0 %collective-permute-start.25 = (bf16[1,16,2176]{2,1,0:T(8,128)(2,1)S(1)}, bf16[1,16,2176]{2,1,0:T(8,128)(2,1)S(1)}, u32[]{:S(2)}, u32[]{:S(2)}) collective-permute-start(bf16[1,16,2176]{2,1,0:T(8,128)(2,1)S(1)} %get-tuple-element.185), channel_id=1, source_target_pairs={{0,16},{1,17},{2,18},{3,19},{4,20},{5,21},{6,22},{7,23},{8,24},{9,... | collective-permute-start | bytes 208904 | tf_op jit(solution)/shard_map/ppermute | solution.py:785
  134.0 7.8 %collective-permute-start.26 = (bf16[1,16,2176]{2,1,0:T(8,128)(2,1)S(1)}, bf16[1,16,2176]{2,1,0:T(8,128)(2,1)S(1)}, u32[]{:S(2)}, u32[]{:S(2)}) collective-permute-start(bf16[1,16,2176]{2,1,0:T(8,128)(2,1)S(1)} %get-tuple-element.186), channel_id=1, source_target_pairs={{0,24},{1,25},{2,26},{3,27},{4,28},{5,29},{6,30},{7,31},{8,16},{9,... | collective-permute-start | bytes 208904 | tf_op jit(solution)/shard_map/ppermute | solution.py:785
  (7 other events, 47.7 us)
